TPU v7x, 32 devices: a whole 2x2x4 slice. The times are simulated.
32 devices in a mesh: ox: 4 (over z), oy: 8 (over y, x, core).
Axes of the slice: x: 2, y: 2, z: 4, core: 2. Of those that a mesh axis runs over, the one named last changes fastest.
Arguments:
- zonal_flow: float32 [4, 512, 1024], P(None, 'ox', 'oy'), may hold values from -3 to 3
- merid_flow: float32 [4, 512, 1024], P(None, 'ox', 'oy'), may hold values from -3 to 3
- thickness: float32 [4, 512, 1024], P(None, 'ox', 'oy'), may hold values from 0.8 to 2
- land_sea: int32 [512, 1024], P('ox', 'oy'), may hold values 0 or 1
- viscosity: float32 [512, 1024], P('ox', 'oy'), may hold values from 0.2 to 3
- wind_stress: float32 [2, 512, 1024], P(None, 'ox', 'oy'), may hold values from -5 to 5
- reduced_gravity: float32 [4], replicated, may hold values from 0.1 to 1
- conv_first: bfloat16 [3, 3, 64, 4], replicated, may hold values from -1 to 1
- bias_first: float32 [64], replicated, may hold values from -3 to 3
- conv_second: bfloat16 [3, 3, 64, 64], replicated, may hold values from -0.25 to 0.25
- bias_second: float32 [64], replicated, may hold values from -3 to 3
- conv_last: bfloat16 [3, 3, 1, 64], replicated, may hold values from -0.25 to 0.25
Outputs:
- zonal_next: float32 [4, 512, 1024], P(None, 'ox', 'oy')
- merid_next: float32 [4, 512, 1024], P(None, 'ox', 'oy')
- thickness_next: float32 [4, 512, 1024], P(None, 'ox', 'oy')
- viscosity_next: float32 [512, 1024], P('ox', 'oy')
Inputs may be any that keep to these rules, and one draw needn't show every extreme that they name: `land_sea`: 1 marks a sea cell.
All inputs are finite; a program needn't handle non-finite values. No bound on the sum of `land_sea` on one device may be relied on, other than what follows from the above.
Results may differ from a plain program's by a relative error of at most 0.0019.
Values may be sent and summed in bfloat16 or wider, within the bound.
No kernel may reach another device: no remote copies, remote signals or barrier semaphores. Data moves between devices by JAX's collectives and lax.ppermute only.
A program may use at most 192 MiB of HBM per device.

v0:
```python
import jax
import jax.numpy as jnp
from jax import lax
from jax.sharding import PartitionSpec as P

TIME_STEP = 0.05
REST_DEPTH = 1.4
DRAG_RATE = 0.5


def with_halo(block, sides, width, periodic):
    for axis, dim in sides:
        count = lax.axis_size(axis)
        forward = [(i, i + 1) for i in range(count - 1)]
        if periodic:
            forward.append((count - 1, 0))
        backward = [(target, source) for source, target in forward]
        low = lax.ppermute(
            lax.slice_in_dim(block, block.shape[dim] - width, None, axis=dim), axis, forward
        )
        high = lax.ppermute(lax.slice_in_dim(block, 0, width, axis=dim), axis, backward)
        block = jnp.concatenate([low, block, high], axis=dim)
    return block


def viscous(field, near, visc, visc_near):
    total = 0.5 * (visc + visc_near[0]) * (near[0] - field)
    for side in range(1, 4):
        total = total + 0.5 * (visc + visc_near[side]) * (near[side] - field)
    return total


def conv_valid(extended, weight):
    width = extended.shape[1] - 2
    height = extended.shape[2] - 2
    total = jnp.zeros((weight.shape[2], width, height), jnp.float32)
    for row_off in range(3):
        for col_off in range(3):
            total = total + jnp.einsum(
                "oc,cxy->oxy",
                weight[row_off, col_off],
                extended[:, row_off : row_off + width, col_off : col_off + height],
                preferred_element_type=jnp.float32,
            )
    return total


def run_network(features, widen, conv_first, bias_first, conv_second, bias_second, conv_last):
    hidden = features
    for weight, bias_term in ((conv_first, bias_first), (conv_second, bias_second)):
        summed = conv_valid(widen(hidden), weight) + bias_term[:, None, None]
        hidden = jax.nn.silu(summed).astype(jnp.bfloat16)
    return conv_valid(widen(hidden), conv_last)


def local(
    zonal_flow,
    merid_flow,
    thickness,
    land_sea,
    viscosity,
    wind_stress,
    reduced_gravity,
    conv_first,
    bias_first,
    conv_second,
    bias_second,
    conv_last,
):
    layers, columns, rows = zonal_flow.shape
    sea = land_sea.astype(jnp.float32)
    zonal_m = zonal_flow * sea
    merid_m = merid_flow * sea
    flux_x = zonal_m * thickness
    flux_y = merid_m * thickness
    visc_row = viscosity[None]
    lon_side = with_halo(
        jnp.concatenate([flux_x, zonal_m, merid_m, visc_row], axis=0), (("ox", 1),), 1, True
    )
    lat_side = with_halo(
        jnp.concatenate([flux_y, zonal_m, merid_m, visc_row], axis=0), (("oy", 2),), 1, False
    )
    east_all = lon_side[:, 2:, :]
    west_all = lon_side[:, :-2, :]
    north_all = lat_side[:, :, 2:]
    south_all = lat_side[:, :, :-2]
    diverge = (east_all[:layers] - west_all[:layers]) * 0.5 + (
        north_all[:layers] - south_all[:layers]
    ) * 0.5
    thickness_next = thickness - TIME_STEP * sea * diverge
    anomaly = thickness_next - REST_DEPTH
    interface = jnp.cumsum(anomaly[::-1], axis=0)[::-1]
    pressure = jnp.cumsum(reduced_gravity[:, None, None] * interface, axis=0)
    press_lon = with_halo(pressure, (("ox", 1),), 1, True)
    press_lat = with_halo(pressure, (("oy", 2),), 1, False)
    grad_x = (press_lon[:, 2:, :] - press_lon[:, :-2, :]) * 0.5
    grad_y = (press_lat[:, :, 2:] - press_lat[:, :, :-2]) * 0.5
    last = 3 * layers
    visc_near = (east_all[last], west_all[last], north_all[last], south_all[last])
    zonal_near = tuple(
        (side[layers : 2 * layers] for side in (east_all, west_all, north_all, south_all))
    )
    merid_near = tuple(
        (side[2 * layers : last] for side in (east_all, west_all, north_all, south_all))
    )
    zonal_visc = viscous(zonal_m, zonal_near, viscosity, visc_near)
    merid_visc = viscous(merid_m, merid_near, viscosity, visc_near)
    lat_rows = lax.axis_index("oy") * rows + jnp.arange(rows)
    total_rows = rows * lax.axis_size("oy")
    coriolis = 0.3 + 1.4 * (lat_rows.astype(jnp.float32) + 0.5) / total_rows
    layer_ids = jnp.arange(layers)
    top = (layer_ids == 0).astype(jnp.float32)[:, None, None]
    bottom = (layer_ids == layers - 1).astype(jnp.float32)[:, None, None]
    force_x = wind_stress[0] / thickness_next[0]
    force_y = wind_stress[1] / thickness_next[0]
    zonal_next = sea * (
        zonal_m
        + TIME_STEP
        * (coriolis * merid_m - grad_x + zonal_visc + top * force_x - DRAG_RATE * bottom * zonal_m)
    )
    merid_next = sea * (
        merid_m
        + TIME_STEP
        * (-coriolis * zonal_m - grad_y + merid_visc + top * force_y - DRAG_RATE * bottom * merid_m)
    )
    energy = 0.5 * jnp.sum(
        thickness_next * (zonal_next * zonal_next + merid_next * merid_next), axis=0
    )
    energy = energy / jnp.sum(thickness_next, axis=0)
    features = jnp.stack(
        [zonal_next[0], merid_next[0], sea * (thickness_next[0] - REST_DEPTH), sea * energy]
    ).astype(jnp.bfloat16)
    banded = lax.all_to_all(features, "oy", split_axis=1, concat_axis=2, tiled=True)

    def widen_band(field):
        extended = with_halo(field, ((("ox", "oy"), 1),), 1, True)
        return jnp.pad(extended, ((0, 0), (0, 0), (1, 1)))

    output = run_network(
        banded, widen_band, conv_first, bias_first, conv_second, bias_second, conv_last
    )
    output = lax.all_to_all(output, "oy", split_axis=2, concat_axis=1, tiled=True)
    viscosity_next = jnp.exp(output[0])
    return (zonal_next, merid_next, thickness_next, viscosity_next)


def solution(mesh):
    in_specs = (
        P(None, "ox", "oy"),
        P(None, "ox", "oy"),
        P(None, "ox", "oy"),
        P("ox", "oy"),
        P("ox", "oy"),
        P(None, "ox", "oy"),
        P(),
        P(),
        P(),
        P(),
        P(),
        P(),
    )
    out_specs = (P(None, "ox", "oy"), P(None, "ox", "oy"), P(None, "ox", "oy"), P("ox", "oy"))
    return jax.shard_map(local, mesh=mesh, in_specs=in_specs, out_specs=out_specs, check_vma=False)
```

profile of v0, /device:TPU:4, one launch (start us, length us, event | category | flops | bytes accessed | tf_op | source)
XLA Modules:
  0.0 142.2 jit_solution(1628908533077970725)
XLA Ops:
  0.6 0.8 convert_element_type.36
  1.5 1.2 fusion.197
  2.7 1.1 pad_maximum_fusion.5
  3.8 3.7 %collective-permute-start = (f32[13,1,128]{2,1,0:T(1,128)S(1)}, f32[13,1,128]{2,1,0:T(1,128)S(1)}, u32[]{:S(2)}, u32[]{:S(2)}) collective-permute-start(f32[13,1,128]{2,1,0:T(1,128)S(1)} %get-tuple-element.30), channel_id=1, source_target_pairs={{8,0},{16,8},{24,16},{0,24},{9,1},{17,9},{25,17},{1,25},{10,2},{18... | collective-permute-start | bytes 19976 | tf_op jit(solution)/shard_map/ppermute | solution.py:21
  8.0 2.5 %collective-permute-start.2 = (f32[13,128,1]{1,2,0:T(1,128)S(1)}, f32[13,128,1]{1,2,0:T(1,128)S(1)}, u32[]{:S(2)}, u32[]{:S(2)}) collective-permute-start(f32[13,128,1]{1,2,0:T(1,128)S(1)} %copy.70), channel_id=1, source_target_pairs={{1,0},{2,1},{3,2},{4,3},{5,4},{6,5},{7,6},{9,8},{10,9},{11,10},{12... | collective-permute-start | bytes 19976 | tf_op jit(solution)/shard_map/ppermute | solution.py:21
  10.8 1.9 %collective-permute-start.3 = (f32[13,128,1]{1,2,0:T(1,128)S(1)}, f32[13,128,1]{1,2,0:T(1,128)S(1)}, u32[]{:S(2)}, u32[]{:S(2)}) collective-permute-start(f32[13,128,1]{1,2,0:T(1,128)S(1)} %copy.72), channel_id=1, source_target_pairs={{0,1},{1,2},{2,3},{3,4},{4,5},{5,6},{6,7},{8,9},{9,10},{10,11},{11... | collective-permute-start | bytes 19976 | tf_op jit(solution)/shard_map/ppermute | solution.py:18
  12.8 0.5 compare_convert_fusion
  13.3 0.6 multiply_add_fusion
  13.9 0.5 compare_select_fusion
  14.4 0.3 copy.71
  14.8 1.9 %collective-permute-done.3 = f32[13,128,1]{1,2,0:T(1,128)S(1)} collective-permute-done((f32[13,128,1]{1,2,0:T(1,128)S(1)}, f32[13,128,1]{1,2,0:T(1,128)S(1)}, u32[]{:S(2)}, u32[]{:S(2)}) %collective-permute-start.3) | collective-permute-done | bytes 6688 | tf_op jit(solution)/shard_map/ppermute | solution.py:18
  16.7 0.3 copy.73
  17.6 0.7 fusion.92
  18.3 1.0 rev.7
  19.3 0.8 fusion.90
  20.4 2.6 %collective-permute-start.6 = (f32[4,128,1]{2,1,0:T(8,128)S(1)}, f32[4,128,1]{2,1,0:T(8,128)S(1)}, u32[]{:S(2)}, u32[]{:S(2)}) collective-permute-start(f32[4,128,1]{2,1,0:T(8,128)S(1)} %get-tuple-element.42), channel_id=1, source_target_pairs={{1,0},{2,1},{3,2},{4,3},{5,4},{6,5},{7,6},{9,8},{10,9},{11,10},{12... | collective-permute-start | bytes 6152 | tf_op jit(solution)/shard_map/ppermute | solution.py:21
  23.0 1.9 %collective-permute-start.7 = (f32[4,128,1]{2,1,0:T(8,128)S(1)}, f32[4,128,1]{2,1,0:T(8,128)S(1)}, u32[]{:S(2)}, u32[]{:S(2)}) collective-permute-start(f32[4,128,1]{2,1,0:T(8,128)S(1)} %get-tuple-element.43), channel_id=1, source_target_pairs={{0,1},{1,2},{2,3},{3,4},{4,5},{5,6},{6,7},{8,9},{9,10},{10,11},{11... | collective-permute-start | bytes 6152 | tf_op jit(solution)/shard_map/ppermute | solution.py:18
  24.9 3.6 %collective-permute-start.4 = (f32[4,1,128]{2,1,0:T(1,128)S(1)}, f32[4,1,128]{2,1,0:T(1,128)S(1)}, u32[]{:S(2)}, u32[]{:S(2)}) collective-permute-start(f32[4,1,128]{2,1,0:T(1,128)S(1)} %get-tuple-element.40), channel_id=1, source_target_pairs={{8,0},{16,8},{24,16},{0,24},{9,1},{17,9},{25,17},{1,25},{10,2},{18... | collective-permute-start | bytes 6152 | tf_op jit(solution)/shard_map/ppermute | solution.py:21
  28.6 3.0 %collective-permute-done.7 = f32[4,128,1]{2,1,0:T(8,128)S(1)} collective-permute-done((f32[4,128,1]{2,1,0:T(8,128)S(1)}, f32[4,128,1]{2,1,0:T(8,128)S(1)}, u32[]{:S(2)}, u32[]{:S(2)}) %collective-permute-start.7) | collective-permute-done | bytes 2080 | tf_op jit(solution)/shard_map/ppermute | solution.py:18
  31.6 2.3 %collective-permute-done.5 = f32[4,1,128]{2,1,0:T(1,128)S(1)} collective-permute-done((f32[4,1,128]{2,1,0:T(1,128)S(1)}, f32[4,1,128]{2,1,0:T(1,128)S(1)}, u32[]{:S(2)}, u32[]{:S(2)}) %collective-permute-start.5) | collective-permute-done | bytes 2080 | tf_op jit(solution)/shard_map/ppermute | solution.py:18
  34.0 0.9 multiply_reduce_fusion
  35.1 7.2 %all_to_all.27 = bf16[4,128,128]{2,0,1:T(4,128)(2,1)S(1)} all-to-all(bf16[4,128,128]{2,0,1:T(4,128)(2,1)S(1)} %copy.74), channel_id=1, replica_groups=mesh['ox'=4,'oy'=8] {'oy'}, dimensions={1} | all-to-all | bytes 262144 | tf_op jit(solution)/shard_map/all_to_all | solution.py:133
  42.5 2.6 %collective-permute-start.9 = (bf16[4,1,1024]{2,0,1:T(4,128)(2,1)S(1)}, bf16[4,1,1024]{2,0,1:T(4,128)(2,1)S(1)}, u32[]{:S(2)}, u32[]{:S(2)}) collective-permute-start(bf16[4,1,1024]{2,0,1:T(4,128)(2,1)S(1)} %get-tuple-element.45), channel_id=1, source_target_pairs={{1,0},{2,1},{3,2},{4,3},{5,4},{6,5},{7,6},{8,7},{9,8},{10,9},{11,1... | collective-permute-start | bytes 24584 | tf_op jit(solution)/shard_map/ppermute | solution.py:21
  45.1 0.8 fusion.153
  45.9 0.6 collective-permute-done.8
  46.6 0.7 fusion.106
  47.4 0.8 fusion.108
  48.2 2.8 %fusion.110 = f32[16,1024,64]{1,2,0:T(8,128)} fusion(bf16[4,18,1026]{2,0,1:T(4,128)(2,1)S(1)} %select_maximum_fusion.2, bf16[3,3,64,4]{2,3,1,0:T(4,128)(2,1)S(1)} %copy-done.8), kind=kOutput, calls=%fused_computation.149 | convolution fusion | flops 8388608 | bytes 4326400 | tf_op jit(solution)/shard_map/oc,cxy->oxy/dot_general | solution.py:39
  51.0 2.8 %fusion.112 = f32[16,1024,64]{1,2,0:T(8,128)} fusion(bf16[4,18,1026]{2,0,1:T(4,128)(2,1)S(1)} %select_maximum_fusion.2, bf16[3,3,64,4]{2,3,1,0:T(4,128)(2,1)S(1)} %copy-done.8), kind=kOutput, calls=%fused_computation.151 | convolution fusion | flops 8388608 | bytes 4326400 | tf_op jit(solution)/shard_map/oc,cxy->oxy/dot_general | solution.py:39
  53.7 2.7 %fusion.114 = f32[16,1024,64]{1,2,0:T(8,128)} fusion(bf16[4,18,1026]{2,0,1:T(4,128)(2,1)S(1)} %select_maximum_fusion.2, bf16[3,3,64,4]{2,3,1,0:T(4,128)(2,1)S(1)} %copy-done.8), kind=kOutput, calls=%fused_computation.153 | convolution fusion | flops 8388608 | bytes 4326400 | tf_op jit(solution)/shard_map/oc,cxy->oxy/dot_general | solution.py:39
  56.4 2.7 %fusion.94 = f32[16,1024,64]{1,2,0:T(8,128)} fusion(bf16[4,16,1024]{2,0,1:T(4,128)(2,1)S(1)} %all_to_all.23, bf16[4,1,1024]{2,0,1:T(4,128)(2,1)S(1)} %collective-permute-done.8, bf16[3,3,64,4]{2,3,1,0:T(4,128)(2,1)S(1)} %copy-done.8), kind=kOutput, calls=%fused_computation.135 | convolution fusion | flops 8667136 | bytes 4334592 | tf_op jit(solution)/shard_map/oc,cxy->oxy/dot_general | solution.py:39
  59.2 2.7 %fusion.98 = f32[16,1024,64]{1,2,0:T(8,128)} fusion(bf16[4,1,1024]{2,0,1:T(4,128)(2,1)S(1)} %collective-permute-done.9, bf16[4,16,1024]{2,0,1:T(4,128)(2,1)S(1)} %all_to_all.23, bf16[3,3,64,4]{2,3,1,0:T(4,128)(2,1)S(1)} %copy-done.8), kind=kOutput, calls=%fused_computation.139 | convolution fusion | flops 8667136 | bytes 4334592 | tf_op jit(solution)/shard_map/oc,cxy->oxy/dot_general | solution.py:39
  61.9 9.6 %fusion.7 = bf16[64,16,1024]{2,0,1:T(8,128)(2,1)S(1)} fusion(f32[16,1024,64]{1,2,0:T(8,128)} %fusion.98, f32[16,1024,64]{1,2,0:T(8,128)S(1)} %fusion.106, f32[16,1024,64]{1,2,0:T(8,128)S(1)} %fusion.108, f32[16,1024,64]{1,2,0:T(8,128)S(1)} %fusion.153, f32[16,1024,64]{1,2,0:T(8,128)} %fusion.110, f32[16,1024,64]{1,2,0:T(8,128)} %fusion.112, ...), kind=kOutput, calls=%fused_computation.13 | convolution fusion | flops 23068672 | bytes 35784192 | tf_op jit(solution)/shard_map/oc,cxy->oxy/dot_general | solution.py:39
  71.6 2.8 %collective-permute-start.11 = (bf16[64,1,1024]{2,0,1:T(8,128)(2,1)S(1)}, bf16[64,1,1024]{2,0,1:T(8,128)(2,1)S(1)}, u32[]{:S(2)}, u32[]{:S(2)}) collective-permute-start(bf16[64,1,1024]{2,0,1:T(8,128)(2,1)S(1)} %get-tuple-element.23), channel_id=1, source_target_pairs={{1,0},{2,1},{3,2},{4,3},{5,4},{6,5},{7,6},{8,7},{9,8},{10,9},{11,1... | collective-permute-start | bytes 393224 | tf_op jit(solution)/shard_map/ppermute | solution.py:21
  74.4 0.7 fusion.134
  75.1 2.5 %collective-permute-done.10 = bf16[64,1,1024]{2,0,1:T(8,128)(2,1)S(1)} collective-permute-done((bf16[64,1,1024]{2,0,1:T(8,128)(2,1)S(1)}, bf16[64,1,1024]{2,0,1:T(8,128)(2,1)S(1)}, u32[]{:S(2)}, u32[]{:S(2)}) %collective-permute-start.10) | collective-permute-done | bytes 131104 | tf_op jit(solution)/shard_map/ppermute | solution.py:18
  77.6 1.8 %fusion.13 = bf16[64,18,1026]{2,0,1:T(8,128)(2,1)S(1)} fusion(bf16[64,1,1024]{2,0,1:T(8,128)(2,1)S(1)} %collective-permute-done.11, bf16[64,16,1024]{2,0,1:T(8,128)(2,1)S(1)} %fusion.7, bf16[64,1,1024]{2,0,1:T(8,128)(2,1)S(1)} %collective-permute-done.10), kind=kLoop, calls=%fused_computation.21 | loop fusion | flops 14183424 | bytes 4723200 | tf_op jit(solution)/shard_map/concatenate | solution.py:22
  79.5 2.7 %fusion.38 = f32[16,1024,64]{1,2,0:T(8,128)} fusion(bf16[64,18,1026]{2,0,1:T(8,128)(2,1)S(1)} %fusion.13, bf16[3,3,64,64]{3,2,1,0:T(8,128)(2,1)S(1)} %copy-done.6), kind=kOutput, calls=%fused_computation.47 | convolution fusion | flops 134217728 | bytes 6307840 | tf_op jit(solution)/shard_map/oc,cxy->oxy/dot_general | solution.py:39
  82.2 2.8 %fusion.40 = f32[16,1024,64]{1,2,0:T(8,128)} fusion(bf16[64,18,1026]{2,0,1:T(8,128)(2,1)S(1)} %fusion.13, bf16[3,3,64,64]{3,2,1,0:T(8,128)(2,1)S(1)} %copy-done.6), kind=kOutput, calls=%fused_computation.49 | convolution fusion | flops 134217728 | bytes 6307840 | tf_op jit(solution)/shard_map/oc,cxy->oxy/dot_general | solution.py:39
  85.0 2.6 %fusion.42 = f32[16,1024,64]{1,2,0:T(8,128)} fusion(bf16[64,18,1026]{2,0,1:T(8,128)(2,1)S(1)} %fusion.13, bf16[3,3,64,64]{3,2,1,0:T(8,128)(2,1)S(1)} %copy-done.6), kind=kOutput, calls=%fused_computation.51 | convolution fusion | flops 134217728 | bytes 6307840 | tf_op jit(solution)/shard_map/oc,cxy->oxy/dot_general | solution.py:39
  87.6 2.8 %fusion.44 = f32[16,1024,64]{1,2,0:T(8,128)} fusion(bf16[64,18,1026]{2,0,1:T(8,128)(2,1)S(1)} %fusion.13, bf16[3,3,64,64]{3,2,1,0:T(8,128)(2,1)S(1)} %copy-done.6), kind=kOutput, calls=%fused_computation.53 | convolution fusion | flops 134217728 | bytes 6307840 | tf_op jit(solution)/shard_map/oc,cxy->oxy/dot_general | solution.py:39
  90.4 2.7 %fusion.48 = f32[16,1024,64]{1,2,0:T(8,128)} fusion(bf16[64,18,1026]{2,0,1:T(8,128)(2,1)S(1)} %fusion.13, bf16[3,3,64,64]{3,2,1,0:T(8,128)(2,1)S(1)} %copy-done.6), kind=kOutput, calls=%fused_computation.58 | convolution fusion | flops 134217728 | bytes 6307840 | tf_op jit(solution)/shard_map/oc,cxy->oxy/dot_general | solution.py:39
  93.1 2.7 %fusion.46 = f32[16,1024,64]{1,2,0:T(8,128)} fusion(bf16[64,16,1024]{2,0,1:T(8,128)(2,1)S(1)} %fusion.7, bf16[64,1,1024]{2,0,1:T(8,128)(2,1)S(1)} %collective-permute-done.10, bf16[3,3,64,64]{3,2,1,0:T(8,128)(2,1)S(1)} %copy-done.6), kind=kOutput, calls=%fused_computation.56 | convolution fusion | flops 138412032 | bytes 6438912 | tf_op jit(solution)/shard_map/oc,cxy->oxy/dot_general | solution.py:39
  95.8 2.6 %fusion.36 = f32[16,1024,64]{1,2,0:T(8,128)} fusion(bf16[64,1,1024]{2,0,1:T(8,128)(2,1)S(1)} %collective-permute-done.11, bf16[64,16,1024]{2,0,1:T(8,128)(2,1)S(1)} %fusion.7, bf16[3,3,64,64]{3,2,1,0:T(8,128)(2,1)S(1)} %copy-done.6), kind=kOutput, calls=%fused_computation.45 | convolution fusion | flops 138412032 | bytes 6438912 | tf_op jit(solution)/shard_map/oc,cxy->oxy/dot_general | solution.py:39
  98.4 10.9 %fusion.8 = bf16[64,16,1024]{2,0,1:T(8,128)(2,1)S(1)} fusion(f32[16,1024,64]{1,2,0:T(8,128)} %fusion.36, f32[16,1024,64]{1,2,0:T(8,128)} %fusion.38, f32[16,1024,64]{1,2,0:T(8,128)} %fusion.40, f32[16,1024,64]{1,2,0:T(8,128)S(1)} %fusion.134, f32[16,1024,64]{1,2,0:T(8,128)} %fusion.42, f32[16,1024,64]{1,2,0:T(8,128)} %fusion.44, ...), kind=kOutput, calls=%fused_computation.14 | convolution fusion | flops 148897792 | bytes 37765632 | tf_op jit(solution)/shard_map/oc,cxy->oxy/dot_general | solution.py:39
  109.4 2.6 %collective-permute-start.13 = (bf16[64,1,1024]{2,0,1:T(8,128)(2,1)S(1)}, bf16[64,1,1024]{2,0,1:T(8,128)(2,1)S(1)}, u32[]{:S(2)}, u32[]{:S(2)}) collective-permute-start(bf16[64,1,1024]{2,0,1:T(8,128)(2,1)S(1)} %get-tuple-element.21), channel_id=1, source_target_pairs={{1,0},{2,1},{3,2},{4,3},{5,4},{6,5},{7,6},{8,7},{9,8},{10,9},{11,1... | collective-permute-start | bytes 393224 | tf_op jit(solution)/shard_map/ppermute | solution.py:21
  112.1 0.5 fusion.172
  112.6 3.4 %collective-permute-done.12 = bf16[64,1,1024]{2,0,1:T(8,128)(2,1)S(1)} collective-permute-done((bf16[64,1,1024]{2,0,1:T(8,128)(2,1)S(1)}, bf16[64,1,1024]{2,0,1:T(8,128)(2,1)S(1)}, u32[]{:S(2)}, u32[]{:S(2)}) %collective-permute-start.12) | collective-permute-done | bytes 131104 | tf_op jit(solution)/shard_map/ppermute | solution.py:18
  116.0 1.8 %select_maximum_fusion = bf16[64,18,1026]{2,0,1:T(8,128)(2,1)S(1)} fusion(bf16[64,1,1024]{2,0,1:T(8,128)(2,1)S(1)} %collective-permute-done.13, bf16[64,16,1024]{2,0,1:T(8,128)(2,1)S(1)} %fusion.8, bf16[64,1,1024]{2,0,1:T(8,128)(2,1)S(1)} %collective-permute-done.12), kind=kLoop, calls=%fused_computation.15 | loop fusion | flops 14183424 | bytes 4723200 | tf_op jit(solution)/shard_map/concatenate | solution.py:22
  117.8 0.9 fusion.22
  118.7 0.4 fusion.24
  119.1 0.9 fusion.26
  119.9 0.4 fusion.28
  120.3 0.9 fusion.30
  121.2 0.4 fusion.32
  121.6 0.5 fusion.14
  122.1 0.5 fusion.18
  122.7 0.3 copy.76
  123.0 0.5 broadcast.201
  123.5 1.9 %reduce = f32[1024,16]{1,0:T(8,128)S(1)} reduce(f32[1024,1,16]{2,1,0:T(1,128)S(1)} %bitcast.265, f32[]{:T(128)} %broadcast.201), dimensions={1}, to_apply=%bitcast.252.reduce_sub_computation | reduce | bytes 131076
  125.7 13.7 %all_to_all.28 = f32[8,1,2048]{2,1,0:T(1,128)S(1)} all-to-all(f32[8,1,2048]{2,1,0:T(1,128)S(1)} %reshape.142), channel_id=1, replica_groups=mesh['ox'=4,'oy'=8] {'oy'}, dimensions={0} | all-to-all | bytes 131072 | tf_op jit(solution)/shard_map/all_to_all | solution.py:142
  139.5 0.8 reduce.1
  140.3 0.9 reshape.143
  141.5 0.6 copy.78
  (74 shorter events, 3.1 us)
Async XLA Ops:
  2.7 10.1 %copy-start.3 = (s32[128,128]{1,0:T(8,128)S(1)}, s32[128,128]{1,0:T(8,128)}, u32[]{:S(2)}) copy-start(s32[128,128]{1,0:T(8,128)} %param.15) | copy-start | bytes 196612
  3.8 13.3 %copy-start = (f32[128,128]{1,0:T(8,128)S(1)}, f32[128,128]{1,0:T(8,128)}, u32[]{:S(2)}) copy-start(f32[128,128]{1,0:T(8,128)} %param.16) | copy-start | bytes 196612
  3.8 13.2 %collective-permute-start = (f32[13,1,128]{2,1,0:T(1,128)S(1)}, f32[13,1,128]{2,1,0:T(1,128)S(1)}, u32[]{:S(2)}, u32[]{:S(2)}) collective-permute-start(f32[13,1,128]{2,1,0:T(1,128)S(1)} %get-tuple-element.30), channel_id=1, source_target_pairs={{8,0},{16,8},{24,16},{0,24},{9,1},{17,9},{25,17},{1,25},{10,2},{18... | collective-permute-start | bytes 19976 | tf_op jit(solution)/shard_map/ppermute | solution.py:21
  7.5 9.6 %collective-permute-start.1 = (f32[13,1,128]{2,1,0:T(1,128)S(1)}, f32[13,1,128]{2,1,0:T(1,128)S(1)}, u32[]{:S(2)}, u32[]{:S(2)}) collective-permute-start(f32[13,1,128]{2,1,0:T(1,128)S(1)} %get-tuple-element.31), channel_id=1, source_target_pairs={{0,8},{8,16},{16,24},{24,0},{1,9},{9,17},{17,25},{25,1},{2,10},{10... | collective-permute-start | bytes 19976 | tf_op jit(solution)/shard_map/ppermute | solution.py:18
  7.5 9.7 %copy-start.2 = (f32[4,128,128]{2,1,0:T(8,128)S(1)}, f32[4,128,128]{2,1,0:T(8,128)}, u32[]{:S(2)}) copy-start(f32[4,128,128]{2,1,0:T(8,128)} %param.14) | copy-start | bytes 786436
  8.0 6.4 %collective-permute-start.2 = (f32[13,128,1]{1,2,0:T(1,128)S(1)}, f32[13,128,1]{1,2,0:T(1,128)S(1)}, u32[]{:S(2)}, u32[]{:S(2)}) collective-permute-start(f32[13,128,1]{1,2,0:T(1,128)S(1)} %copy.70), channel_id=1, source_target_pairs={{1,0},{2,1},{3,2},{4,3},{5,4},{6,5},{7,6},{9,8},{10,9},{11,10},{12... | collective-permute-start | bytes 19976 | tf_op jit(solution)/shard_map/ppermute | solution.py:21
  10.8 5.9 %collective-permute-start.3 = (f32[13,128,1]{1,2,0:T(1,128)S(1)}, f32[13,128,1]{1,2,0:T(1,128)S(1)}, u32[]{:S(2)}, u32[]{:S(2)}) collective-permute-start(f32[13,128,1]{1,2,0:T(1,128)S(1)} %copy.72), channel_id=1, source_target_pairs={{0,1},{1,2},{2,3},{3,4},{4,5},{5,6},{6,7},{8,9},{9,10},{10,11},{11... | collective-permute-start | bytes 19976 | tf_op jit(solution)/shard_map/ppermute | solution.py:18
  17.5 17.4 %copy-start.1 = (f32[4,128,128]{2,1,0:T(8,128)}, f32[4,128,128]{2,1,0:T(8,128)S(1)}, u32[]{:S(2)}) copy-start(f32[4,128,128]{2,1,0:T(8,128)S(1)} %fusion.89) | copy-start | bytes 786436
  17.5 16.4 %copy-start.11 = (f32[4]{0:T(128)S(1)}, f32[4]{0:T(128)}, u32[]{:S(2)}) copy-start(f32[4]{0:T(128)} %compare_convert_fusion) | copy-start | bytes 52
  17.5 16.4 %copy-start.12 = (f32[128]{0:T(128)S(1)}, f32[128]{0:T(128)}, u32[]{:S(2)}) copy-start(f32[128]{0:T(128)} %get-tuple-element.48) | copy-start | bytes 1540
  17.5 16.4 %copy-start.13 = (f32[128]{0:T(128)S(1)}, f32[128]{0:T(128)}, u32[]{:S(2)}) copy-start(f32[128]{0:T(128)} %get-tuple-element.49) | copy-start | bytes 1540
  17.6 16.4 %copy-start.14 = (f32[4]{0:T(128)S(1)}, f32[4]{0:T(128)}, u32[]{:S(2)}) copy-start(f32[4]{0:T(128)} %compare_select_fusion) | copy-start | bytes 52
  19.3 9.3 %copy-start.7 = (f32[2,128,128]{2,1,0:T(8,128)S(1)}, f32[2,128,128]{2,1,0:T(8,128)}, u32[]{:S(2)}) copy-start(f32[2,128,128]{2,1,0:T(8,128)} %param.17) | copy-start | bytes 393220
  20.4 24.7 %copy-start.8 = (bf16[3,3,64,4]{2,3,1,0:T(4,128)(2,1)S(1)}, bf16[3,3,64,4]{2,3,1,0:T(4,128)(2,1)}, u32[]{:S(2)}) copy-start(bf16[3,3,64,4]{2,3,1,0:T(4,128)(2,1)} %param.19) | copy-start | bytes 13828
  20.4 8.2 %collective-permute-start.6 = (f32[4,128,1]{2,1,0:T(8,128)S(1)}, f32[4,128,1]{2,1,0:T(8,128)S(1)}, u32[]{:S(2)}, u32[]{:S(2)}) collective-permute-start(f32[4,128,1]{2,1,0:T(8,128)S(1)} %get-tuple-element.42), channel_id=1, source_target_pairs={{1,0},{2,1},{3,2},{4,3},{5,4},{6,5},{7,6},{9,8},{10,9},{11,10},{12... | collective-permute-start | bytes 6152 | tf_op jit(solution)/shard_map/ppermute | solution.py:21
  23.0 8.6 %collective-permute-start.7 = (f32[4,128,1]{2,1,0:T(8,128)S(1)}, f32[4,128,1]{2,1,0:T(8,128)S(1)}, u32[]{:S(2)}, u32[]{:S(2)}) collective-permute-start(f32[4,128,1]{2,1,0:T(8,128)S(1)} %get-tuple-element.43), channel_id=1, source_target_pairs={{0,1},{1,2},{2,3},{3,4},{4,5},{5,6},{6,7},{8,9},{9,10},{10,11},{11... | collective-permute-start | bytes 6152 | tf_op jit(solution)/shard_map/ppermute | solution.py:18
  24.9 6.7 %collective-permute-start.4 = (f32[4,1,128]{2,1,0:T(1,128)S(1)}, f32[4,1,128]{2,1,0:T(1,128)S(1)}, u32[]{:S(2)}, u32[]{:S(2)}) collective-permute-start(f32[4,1,128]{2,1,0:T(1,128)S(1)} %get-tuple-element.40), channel_id=1, source_target_pairs={{8,0},{16,8},{24,16},{0,24},{9,1},{17,9},{25,17},{1,25},{10,2},{18... | collective-permute-start | bytes 6152 | tf_op jit(solution)/shard_map/ppermute | solution.py:21
  28.5 5.4 %collective-permute-start.5 = (f32[4,1,128]{2,1,0:T(1,128)S(1)}, f32[4,1,128]{2,1,0:T(1,128)S(1)}, u32[]{:S(2)}, u32[]{:S(2)}) collective-permute-start(f32[4,1,128]{2,1,0:T(1,128)S(1)} %get-tuple-element.41), channel_id=1, source_target_pairs={{0,8},{8,16},{16,24},{24,0},{1,9},{9,17},{17,25},{25,1},{2,10},{10... | collective-permute-start | bytes 6152 | tf_op jit(solution)/shard_map/ppermute | solution.py:18
  34.8 7.5 %copy-start.5 = (f32[4,128,128]{2,1,0:T(8,128)}, f32[4,128,128]{2,1,0:T(8,128)S(1)}, u32[]{:S(2)}) copy-start(f32[4,128,128]{2,1,0:T(8,128)S(1)} %get-tuple-element.15) | copy-start | bytes 786436
  34.8 12.5 %copy-start.4 = (f32[4,128,128]{2,1,0:T(8,128)}, f32[4,128,128]{2,1,0:T(8,128)S(1)}, u32[]{:S(2)}) copy-start(f32[4,128,128]{2,1,0:T(8,128)S(1)} %get-tuple-element.14) | copy-start | bytes 786436
  42.4 4.0 %collective-permute-start.8 = (bf16[4,1,1024]{2,0,1:T(4,128)(2,1)S(1)}, bf16[4,1,1024]{2,0,1:T(4,128)(2,1)S(1)}, u32[]{:S(2)}, u32[]{:S(2)}) collective-permute-start(bf16[4,1,1024]{2,0,1:T(4,128)(2,1)S(1)} %get-tuple-element.44), channel_id=1, source_target_pairs={{0,1},{1,2},{2,3},{3,4},{4,5},{5,6},{6,7},{7,8},{8,9},{9,10},{10,1... | collective-permute-start | bytes 24584 | tf_op jit(solution)/shard_map/ppermute | solution.py:18
  42.5 4.0 %collective-permute-start.9 = (bf16[4,1,1024]{2,0,1:T(4,128)(2,1)S(1)}, bf16[4,1,1024]{2,0,1:T(4,128)(2,1)S(1)}, u32[]{:S(2)}, u32[]{:S(2)}) collective-permute-start(bf16[4,1,1024]{2,0,1:T(4,128)(2,1)S(1)} %get-tuple-element.45), channel_id=1, source_target_pairs={{1,0},{2,1},{3,2},{4,3},{5,4},{6,5},{7,6},{8,7},{9,8},{10,9},{11,1... | collective-permute-start | bytes 24584 | tf_op jit(solution)/shard_map/ppermute | solution.py:21
  56.4 5.4 %copy-start.9 = (f32[64]{0:T(128)S(1)}, f32[64]{0:T(128)}, u32[]{:S(2)}) copy-start(f32[64]{0:T(128)} %param.20) | copy-start | bytes 772
  61.9 12.5 %copy-start.6 = (bf16[3,3,64,64]{3,2,1,0:T(8,128)(2,1)S(1)}, bf16[3,3,64,64]{3,2,1,0:T(8,128)(2,1)}, u32[]{:S(2)}) copy-start(bf16[3,3,64,64]{3,2,1,0:T(8,128)(2,1)} %param.21) | copy-start | bytes 221188
  71.5 6.1 %collective-permute-start.10 = (bf16[64,1,1024]{2,0,1:T(8,128)(2,1)S(1)}, bf16[64,1,1024]{2,0,1:T(8,128)(2,1)S(1)}, u32[]{:S(2)}, u32[]{:S(2)}) collective-permute-start(bf16[64,1,1024]{2,0,1:T(8,128)(2,1)S(1)} %get-tuple-element.22), channel_id=1, source_target_pairs={{0,1},{1,2},{2,3},{3,4},{4,5},{5,6},{6,7},{7,8},{8,9},{9,10},{10,1... | collective-permute-start | bytes 393224 | tf_op jit(solution)/shard_map/ppermute | solution.py:18
  71.6 6.1 %collective-permute-start.11 = (bf16[64,1,1024]{2,0,1:T(8,128)(2,1)S(1)}, bf16[64,1,1024]{2,0,1:T(8,128)(2,1)S(1)}, u32[]{:S(2)}, u32[]{:S(2)}) collective-permute-start(bf16[64,1,1024]{2,0,1:T(8,128)(2,1)S(1)} %get-tuple-element.23), channel_id=1, source_target_pairs={{1,0},{2,1},{3,2},{4,3},{5,4},{6,5},{7,6},{8,7},{9,8},{10,9},{11,1... | collective-permute-start | bytes 393224 | tf_op jit(solution)/shard_map/ppermute | solution.py:21
  95.8 2.6 %copy-start.10 = (f32[64]{0:T(128)S(1)}, f32[64]{0:T(128)}, u32[]{:S(2)}) copy-start(f32[64]{0:T(128)} %param.22) | copy-start | bytes 772
  98.4 13.6 %copy-start.15 = (bf16[3,3,1,64]{3,1,2,0:T(4,128)(2,1)S(1)}, bf16[3,3,1,64]{3,1,2,0:T(4,128)(2,1)}, u32[]{:S(2)}) copy-start(bf16[3,3,1,64]{3,1,2,0:T(4,128)(2,1)} %param.23) | copy-start | bytes 3460
  109.4 6.6 %collective-permute-start.12 = (bf16[64,1,1024]{2,0,1:T(8,128)(2,1)S(1)}, bf16[64,1,1024]{2,0,1:T(8,128)(2,1)S(1)}, u32[]{:S(2)}, u32[]{:S(2)}) collective-permute-start(bf16[64,1,1024]{2,0,1:T(8,128)(2,1)S(1)} %get-tuple-element.20), channel_id=1, source_target_pairs={{0,1},{1,2},{2,3},{3,4},{4,5},{5,6},{6,7},{7,8},{8,9},{9,10},{10,1... | collective-permute-start | bytes 393224 | tf_op jit(solution)/shard_map/ppermute | solution.py:18
  109.4 6.6 %collective-permute-start.13 = (bf16[64,1,1024]{2,0,1:T(8,128)(2,1)S(1)}, bf16[64,1,1024]{2,0,1:T(8,128)(2,1)S(1)}, u32[]{:S(2)}, u32[]{:S(2)}) collective-permute-start(bf16[64,1,1024]{2,0,1:T(8,128)(2,1)S(1)} %get-tuple-element.21), channel_id=1, source_target_pairs={{1,0},{2,1},{3,2},{4,3},{5,4},{6,5},{7,6},{8,7},{9,8},{10,9},{11,1... | collective-permute-start | bytes 393224 | tf_op jit(solution)/shard_map/ppermute | solution.py:21
where the time goes:
time: 145 us; the launch traced here: 142 us
  matrix products  61.4 us (42%)
  starting transfers between devices  24.6 us (17%)
  blocking collectives  20.9 us (14%)
  other arithmetic  14.4 us (10%)
  waiting for transfers between devices  13.8 us (10%)
  local copies, waits for them, and re-layouts  5.9 us (4%)
    dot_general x27, matrix products, conv_valid(): jnp.einsum('oc,cxy->oxy', weight[row_off, col_off], extended[:, row_off:r...  61.4 us
    ppermute x7, starting transfers between devices, with_halo(): lax.ppermute(lax.slice_in_dim(block, 0, width, axis=dim), axis, backward)  20.5 us
    ppermute x7, waiting for transfers between devices, with_halo(): lax.ppermute(lax.slice_in_dim(block, block.shape[dim] - width, None, axis...  13.8 us
    all_to_all x1, blocking collectives, local(): lax.all_to_all(output, 'oy', split_axis=2, concat_axis=1, tiled=True)  13.7 us
    all_to_all x1, blocking collectives, local(): lax.all_to_all(features, 'oy', split_axis=1, concat_axis=2, tiled=True)  7.17 us
    ppermute x7, starting transfers between devices, with_halo(): lax.ppermute(lax.slice_in_dim(block, block.shape[dim] - width, None, axis...  4.06 us
    concatenate x4, other arithmetic, with_halo(): block = jnp.concatenate([low, block, high], axis=dim)  3.94 us
  transfers between devices with their start and end apart: 14, of which 6 were waited for; matrix products, arithmetic and copies ran while one was open for 4% of the time, Pallas kernels for 0%

commit v1 on v0

v1 whole, which is shorter than its diff:
```python
import functools

import jax
import jax.numpy as jnp
from jax import lax
from jax.experimental import pallas as pl
from jax.experimental.pallas import tpu as pltpu
from jax.sharding import PartitionSpec as P

TIME_STEP = 0.05
REST_DEPTH = 1.4
DRAG_RATE = 0.5

F32 = jnp.float32
BF16 = jnp.bfloat16
EDGE = 8
FIELDS = 16
PITCH = 80
VMEM = pl.BlockSpec(memory_space=pltpu.VMEM)


def own_fields(zonal, merid, thick, land, visc, wind, rows):
    sea = land[rows, :].astype(F32)
    layers = zonal.shape[0]
    maps = [zonal[l, rows, :] * sea for l in range(layers)]
    maps += [merid[l, rows, :] * sea for l in range(layers)]
    maps += [thick[l, rows, :] - REST_DEPTH for l in range(layers)]
    return maps + [sea, visc[rows, :], wind[0, rows, :], wind[1, rows, :]]


def pack_kernel(zonal, merid, thick, land, visc, wind, lat_a, lat_b, lon_a, lon_b):
    columns, lat = land.shape
    even_y = lax.rem(lax.axis_index("oy"), 2) == 0
    even_x = lax.rem(lax.axis_index("ox"), 2) == 0
    lane = lax.broadcasted_iota(jnp.int32, (16, lat), 1) // EDGE
    maps_low = own_fields(zonal, merid, thick, land, visc, wind, slice(0, EDGE))
    maps_high = own_fields(zonal, merid, thick, land, visc, wind, slice(columns - EDGE, columns))
    for f in range(0, FIELDS, 2):
        low = jnp.concatenate(maps_low[f : f + 2], axis=0)
        high = jnp.concatenate(maps_high[f : f + 2], axis=0)
        lon_a[EDGE * f : EDGE * f + 16, :] = jnp.where(even_x, high, low).astype(BF16)
        lon_b[EDGE * f : EDGE * f + 16, :] = jnp.where(even_x, low, high).astype(BF16)
    for c in range(0, columns, 16):
        low = jnp.zeros((16, lat), F32)
        high = jnp.zeros((16, lat), F32)
        for f, field in enumerate(own_fields(zonal, merid, thick, land, visc, wind, slice(c, c + 16))):
            here = lane == f
            low = jnp.where(here, pltpu.roll(field, EDGE * f % lat, 1), low)
            high = jnp.where(here, pltpu.roll(field, (EDGE * f + EDGE) % lat, 1), high)
        lat_a[c : c + 16, :] = jnp.where(even_y, high, low).astype(BF16)
        lat_b[c : c + 16, :] = jnp.where(even_y, low, high).astype(BF16)


def corner_kernel(lon_a, lon_b, got_a, got_b, out_a, out_b):
    columns = got_a.shape[0]
    even_x = lax.rem(lax.axis_index("ox"), 2) == 0
    size = lon_a.shape[0]
    out_a[0:size, :] = lon_a[...]
    out_b[0:size, :] = lon_b[...]
    for n, got in enumerate((got_a, got_b)):
        low = got[0:16, :]
        high = got[columns - 16 : columns, :]
        out_a[size + 16 * n : size + 16 * n + 16, :] = jnp.where(even_x, high, low)
        out_b[size + 16 * n : size + 16 * n + 16, :] = jnp.where(even_x, low, high)


def weight_kernel(first, second, last, bias_first, bias_second, w1, w2, w3, b1, b2):
    hidden = second.shape[2]
    zero = jnp.zeros((hidden, hidden), F32)
    turned = [[second[a, b].astype(F32).T * 0.5 for b in range(3)] for a in range(3)]
    tap = lambda a, b: turned[a][b] if 0 <= a < 3 and 0 <= b < 3 else zero
    for px in range(4):
        for py in range(4):
            ex, ey, a, b = px % 2, py % 2, px // 2, py // 2
            row = ((2 * a + b) * 4 + 2 * ex + ey) * hidden
            for dx in range(2):
                w2[row : row + hidden, 128 * dx : 128 * dx + 128] = jnp.concatenate(
                    [tap(px - dx, py), tap(px - dx, py - 1)], axis=1
                ).astype(BF16)
    feats = first.shape[3]
    spot = lax.broadcasted_iota(jnp.int32, (256, feats), 0)
    chan = lax.broadcasted_iota(jnp.int32, (256, feats), 1)
    total = jnp.zeros((256, hidden), F32)
    ddx, ddy = spot // 128, (spot // 64) % 2
    for a in range(3):
        for b in range(3):
            want = ((ddx + a) * 4 + ddy + b) * feats + chan
            place = jnp.where(spot % 64 == want, 0.5, 0.0).astype(BF16)
            total = total + lax.dot_general(
                place, first[a, b], (((1,), (1,)), ((), ())), preferred_element_type=F32
            )
    base = jnp.concatenate(
        [
            jnp.concatenate([total[0:64], total[64:128]], axis=1),
            jnp.concatenate([total[128:192], total[192:256]], axis=1),
        ],
        axis=1,
    )
    for s in range(4):
        off = 80 + 32 * s
        w1[s] = jnp.concatenate(
            [jnp.zeros((off, 256), F32), base, jnp.zeros((192 - off, 256), F32)], axis=0
        ).astype(BF16)
    row = lax.broadcasted_iota(jnp.int32, (16, 128), 0)
    blank = jnp.zeros((1, hidden), F32)
    piece = lambda a, b: last[a, b].astype(F32) if 0 <= a < 3 and 0 <= b < 3 else blank
    for ex in range(2):
        tile = jnp.zeros((16, 128), F32)
        for k in range(16):
            a, dx, b, dy = k // 8, (k // 4) % 2, (k // 2) % 2, k % 2
            p, q = 2 * a + ex - dx, 2 * b - dy
            line = jnp.concatenate([piece(p, q), piece(p, q + 1)], axis=1)
            tile = jnp.where(row == k, jnp.broadcast_to(line, (16, 128)), tile)
        w3[:, 128 * ex : 128 * ex + 128] = tile.astype(BF16)
    for bias, out in ((bias_first, b1), (bias_second, b2)):
        half = bias[...] * 0.5
        out[...] = jnp.broadcast_to(jnp.concatenate([half] * 4, axis=1), (8, 256))


def main_kernel(
    lat_count,
    zonal,
    merid,
    thick,
    land,
    visc,
    wind,
    gravity,
    lat_a,
    lat_b,
    lon_a,
    lon_b,
    w1,
    w2,
    w3,
    b1,
    b2,
    zonal_out,
    merid_out,
    thick_out,
    visc_out,
    ext,
    nxt,
    prs,
    spread,
    feat,
    act,
    act_up,
    parts,
    sums,
):
    layers, columns, lat = zonal.shape
    oy = lax.axis_index("oy")
    even_y = lax.rem(oy, 2) == 0
    even_x = lax.rem(lax.axis_index("ox"), 2) == 0
    base = 2 * EDGE
    wide = 2 * lat
    sea_id, visc_id, wind_id = 3 * layers, 3 * layers + 1, 3 * layers + 2

    west = jnp.where(even_x, lon_b[...], lon_a[...])
    east = jnp.where(even_x, lon_a[...], lon_b[...])
    size = EDGE * FIELDS
    north, south = [], []
    for side, slot in ((west, slice(8, 16)), (east, slice(0, 8))):
        from_a = side[size : size + 16].astype(F32)[slot]
        from_b = side[size + 16 : size + 32].astype(F32)[slot]
        north.append(jnp.where(even_y, from_a, from_b))
        south.append(jnp.where(even_y, from_b, from_a))
    west = west[:size].astype(F32)
    east = east[:size].astype(F32)
    lane = lax.broadcasted_iota(jnp.int32, (EDGE, lat), 1)

    def second_tile(n_rows, s_rows, f):
        up = pltpu.roll(n_rows, (lat - EDGE * f) % lat, 1)
        down = pltpu.roll(s_rows, (2 * lat - EDGE - EDGE * f) % lat, 1)
        return jnp.where(lane < EDGE, up, jnp.where(lane >= lat - EDGE, down, 0.0))

    def put(f, row, first_tile, n_rows, s_rows):
        far = second_tile(n_rows, s_rows, f)
        if 2 * layers <= f < 3 * layers:
            far = far + REST_DEPTH
        ext[f, row : row + EDGE, 0:lat] = first_tile
        ext[f, row : row + EDGE, lat:wide] = far

    for f in range(FIELDS):
        lift = REST_DEPTH if 2 * layers <= f < 3 * layers else 0.0
        put(f, base - EDGE, west[EDGE * f : EDGE * f + EDGE] + lift, north[0], south[0])
        put(f, base + columns, east[EDGE * f : EDGE * f + EDGE] + lift, north[1], south[1])
    for c in range(0, columns, 16):
        got_a = lat_a[c : c + 16, :].astype(F32)
        got_b = lat_b[c : c + 16, :].astype(F32)
        n_both = jnp.where(even_y, got_a, got_b)
        s_both = jnp.where(even_y, got_b, got_a)
        for h in range(0, 16, EDGE):
            rows = slice(c + h, c + h + EDGE)
            sea = land[rows, :].astype(F32)
            maps = [zonal[l, rows, :] * sea for l in range(layers)]
            maps += [merid[l, rows, :] * sea for l in range(layers)]
            maps += [thick[l, rows, :] for l in range(layers)]
            maps += [sea, visc[rows, :], wind[0, rows, :], wind[1, rows, :]]
            for f in range(FIELDS):
                put(f, base + c + h, maps[f], n_both[h : h + EDGE], s_both[h : h + EDGE])

    def up(x):
        return pltpu.roll(x, wide - 1, 1)

    def down(x):
        return pltpu.roll(x, 1, 1)

    chunks = (columns + 2 * EDGE) // EDGE
    for ch in range(chunks):
        r = EDGE + EDGE * ch
        here, plus, minus = slice(r, r + 8), slice(r + 1, r + 9), slice(r - 1, r + 7)
        sea = ext[sea_id, here, :]
        odd = []
        for l in range(layers):
            h = ext[2 * layers + l, here, :]
            flux_e = ext[l, plus, :] * ext[2 * layers + l, plus, :]
            flux_w = ext[l, minus, :] * ext[2 * layers + l, minus, :]
            flux_y = ext[layers + l, here, :] * h
            diverge = (flux_e - flux_w) * 0.5 + (up(flux_y) - down(flux_y)) * 0.5
            h = h - TIME_STEP * sea * diverge
            nxt[l, r : r + 8, :] = h
            if 1 <= ch < chunks - 1:
                thick_out[l, r - base : r - base + 8, :] = h[:, 0:lat]
            odd.append(h - REST_DEPTH)
        for l in reversed(range(layers - 1)):
            odd[l] = odd[l] + odd[l + 1]
        total = jnp.zeros_like(sea)
        for l in range(layers):
            total = total + gravity[l] * odd[l]
            prs[l, r : r + 8, :] = total

    place = lax.broadcasted_iota(jnp.int32, (EDGE, wide), 1)
    place = jnp.where(place < lat + lat // 2, place, place - wide)
    total_rows = lat_count * lat
    coriolis = 0.3 + 1.4 * ((oy * lat + place).astype(F32) + 0.5) / total_rows
    in_lat = (place >= -3) & (place < lat + 3)
    for ch in range(chunks):
        r = EDGE + EDGE * ch
        here, plus, minus = slice(r, r + 8), slice(r + 1, r + 9), slice(r - 1, r + 7)
        sea = ext[sea_id, here, :]
        v = ext[visc_id, here, :]
        mix = [
            0.5 * (v + ext[visc_id, plus, :]),
            0.5 * (v + ext[visc_id, minus, :]),
            0.5 * (v + up(v)),
            0.5 * (v + down(v)),
        ]

        def lap(f, q):
            near = (ext[f, plus, :], ext[f, minus, :], up(q), down(q))
            total = mix[0] * (near[0] - q)
            for side in range(1, 4):
                total = total + mix[side] * (near[side] - q)
            return total

        heavy = jnp.zeros_like(sea)
        moving = jnp.zeros_like(sea)
        for l in range(layers):
            zm = ext[l, here, :]
            vm = ext[layers + l, here, :]
            p = prs[l, here, :]
            h = nxt[l, here, :]
            grad_x = (prs[l, plus, :] - prs[l, minus, :]) * 0.5
            grad_y = (up(p) - down(p)) * 0.5
            push_x = coriolis * vm - grad_x + lap(l, zm)
            push_y = -coriolis * zm - grad_y + lap(layers + l, vm)
            if l == 0:
                push_x = push_x + ext[wind_id, here, :] / h
                push_y = push_y + ext[wind_id + 1, here, :] / h
            if l == layers - 1:
                push_x = push_x - DRAG_RATE * zm
                push_y = push_y - DRAG_RATE * vm
            zn = sea * (zm + TIME_STEP * push_x)
            vn = sea * (vm + TIME_STEP * push_y)
            if 1 <= ch < chunks - 1:
                zonal_out[l, r - base : r - base + 8, :] = zn[:, 0:lat]
                merid_out[l, r - base : r - base + 8, :] = vn[:, 0:lat]
            heavy = heavy + h
            moving = moving + h * (zn * zn + vn * vn)
            if l == 0:
                maps = [zn, vn, sea * (h - REST_DEPTH)]
        maps.append(sea * (0.5 * moving / heavy))
        keep = in_lat
        if ch == 0 or ch == chunks - 1:
            column = lax.broadcasted_iota(jnp.int32, (EDGE, wide), 0) + (r - base)
            keep = keep & (column >= -3) & (column < columns + 3)
        for f, m in enumerate(maps):
            m = jnp.where(keep, m, 0.0)
            for dy in range(4):
                spread[EDGE * ch : EDGE * ch + 8, 4 * dy + f, :] = pltpu.roll(m, (wide - dy) % wide, 1) if dy else m

    block = lax.broadcasted_iota(jnp.int32, (PITCH, wide), 0)
    source = lax.broadcasted_iota(jnp.int32, (PITCH, wide), 1)
    blocks = lat // 2 + 2
    chooser = jnp.where(
        (block < blocks) & (source == lax.rem(wide - 3 + 2 * block, wide)), 1.0, 0.0
    ).astype(BF16)
    tiles = (columns + 2 * EDGE) // 8
    for t in range(0, tiles, 2):
        got = spread[8 * t : 8 * t + 16].reshape(256, wide).astype(BF16)
        g = lax.dot_general(
            chooser, got, (((1,), (1,)), ((), ())), preferred_element_type=F32
        ).astype(BF16)
        feat[t, :, 0:128] = g[:, 0:128]
        feat[t, :, 128:256] = g[:, 128:256]
        feat[t + 1, :, 0:128] = g[:, 128:256]
        if t > 0:
            feat[t - 1, :, 128:256] = g[:, 0:128]

    south_end = jnp.where(oy == 0, 0.0, 1.0)
    north_end = jnp.where(oy == lat_count - 1, 0.0, 1.0)
    brow = lax.broadcasted_iota(jnp.int32, (8, 256), 0)
    quad = lax.broadcasted_iota(jnp.int32, (8, 256), 1) // 64 % 2
    low_1 = jnp.where(brow == 0, south_end, 1.0)
    high_1 = jnp.where(brow == blocks - 1 - 64, north_end, 1.0)
    low_2 = jnp.where((brow == 0) & (quad == 0), south_end, 1.0)
    high_2 = jnp.where((brow == blocks - 2 - 64) & (quad == 1), north_end, 1.0)

    def activate(total, bias, count, low, high):
        total = total + bias
        total = total * jnp.tanh(total) + total
        total = total.reshape(count, PITCH, 256)
        return jnp.concatenate(
            [total[:, 0:8] * low, total[:, 8:64], total[:, 64:72] * high, total[:, 72:]], axis=1
        )

    bias1 = b1[0:1, :]
    bias2 = b2[0:1, :]
    group = 4

    def first_conv(t, count, s):
        left = feat[pl.ds(t, count)].reshape(count * PITCH, 256)
        h = jnp.dot(left, w1[s], preferred_element_type=F32)
        h = activate(h, bias1, count, low_1, high_1)
        flat = h.reshape(count * PITCH, 256)
        moved = pltpu.roll(flat, count * PITCH - 1, 0).reshape(count, PITCH, 256)
        act[pl.ds(t, count), s] = h.astype(BF16)
        act_up[pl.ds(t, count), s] = moved.astype(BF16)

    whole_groups = (columns // 8) // group

    def first_step(g, carry):
        for s in range(4):
            first_conv(g * group, group, s)
        return carry

    lax.fori_loop(0, whole_groups, first_step, 0)
    for s in range(2):
        first_conv(columns // 8, 1, s)

    zero_part = jnp.zeros((16, 128), F32)

    def second_step(t, carry):
        for half in range(2):
            first_s = 2 * half
            nxt_t, nxt_s = (t, first_s + 2) if half == 0 else (t + 1, 0)
            rows = 2 * PITCH
            top = act[t, first_s : first_s + 2].reshape(rows, 256)
            top_up = act_up[t, first_s : first_s + 2].reshape(rows, 256)
            one = act[t, first_s + 1]
            two = act[nxt_t, nxt_s]
            one_up = act_up[t, first_s + 1]
            two_up = act_up[nxt_t, nxt_s]
            low = jnp.concatenate([one, two], axis=0)
            low_up = jnp.concatenate([one_up, two_up], axis=0)
            left = jnp.concatenate([top, top_up, low, low_up], axis=1)
            h = jnp.dot(left, w2[...], preferred_element_type=F32)
            h = activate(h, bias2, 2, low_2, high_2).astype(BF16)
            for k in range(2):
                parts[t * 4 + first_s + k] = zero_part
                parts[t * 4 + first_s + k, :, 0:PITCH] = lax.dot_general(
                    w3[...], h[k], (((1,), (1,)), ((), ())), preferred_element_type=F32
                )
        return carry

    lax.fori_loop(0, columns // 8, second_step, 0)
    t = columns // 8
    left = jnp.concatenate([act[t, 0], act_up[t, 0], act[t, 1], act_up[t, 1]], axis=1)
    h = jnp.dot(left, w2[...], preferred_element_type=F32)
    h = activate(h, bias2, 1, low_2, high_2).astype(BF16)
    parts[4 * t] = zero_part
    parts[4 * t, :, 0:PITCH] = lax.dot_general(
        w3[...], h[0], (((1,), (1,)), ((), ())), preferred_element_type=F32
    )

    for i in range(columns // 2):
        sums[8 * i : 8 * i + 8, :] = parts[i, 0:8, :] + parts[i + 1, 8:16, :]
    jj = lax.broadcasted_iota(jnp.int32, (128, lat), 0)
    ll = lax.broadcasted_iota(jnp.int32, (128, lat), 1)
    out = jnp.zeros((columns, lat), F32)
    for k in range(4):
        x = sums[pl.ds(k, columns, stride=4), :]
        high = x.astype(BF16)
        rest = (x - high.astype(F32)).astype(BF16)
        put_at = jnp.where(ll == 2 * (jj - k // 2) + k % 2, 1.0, 0.0).astype(BF16)
        out = out + jnp.dot(high, put_at, preferred_element_type=F32)
        out = out + jnp.dot(rest, put_at, preferred_element_type=F32)
    visc_out[...] = jnp.exp(out)


def swap(x, axis, parity, count, periodic):
    pairs = []
    for i in range(count):
        j = i + 1 if i % 2 == parity else i - 1
        if periodic or 0 <= j < count:
            pairs.append((i, j % count))
    return lax.ppermute(x, axis, pairs)


def local(
    nx,
    ny,
    zonal,
    merid,
    thick,
    land,
    visc,
    wind,
    gravity,
    conv_first,
    bias_first,
    conv_second,
    bias_second,
    conv_last,
):
    layers, columns, lat = zonal.shape
    big = pltpu.CompilerParams(vmem_limit_bytes=48 * 1024 * 1024)
    lon_rows = EDGE * FIELDS
    lat_a, lat_b, lon_a, lon_b = pl.pallas_call(
        pack_kernel,
        out_shape=[jax.ShapeDtypeStruct((columns, lat), BF16)] * 2
        + [jax.ShapeDtypeStruct((lon_rows, lat), BF16)] * 2,
        in_specs=[VMEM] * 6,
        out_specs=[VMEM] * 4,
        compiler_params=big,
        name="pack",
    )(zonal, merid, thick, land, visc, wind)
    lat_a = swap(lat_a, "oy", 0, ny, False)
    lat_b = swap(lat_b, "oy", 1, ny, False)
    w1, w2, w3, b1, b2 = pl.pallas_call(
        weight_kernel,
        out_shape=[
            jax.ShapeDtypeStruct((4, 256, 256), BF16),
            jax.ShapeDtypeStruct((1024, 256), BF16),
            jax.ShapeDtypeStruct((16, 256), BF16),
            jax.ShapeDtypeStruct((8, 256), F32),
            jax.ShapeDtypeStruct((8, 256), F32),
        ],
        in_specs=[VMEM] * 5,
        out_specs=[VMEM] * 5,
        compiler_params=big,
        name="weights",
    )(conv_first, conv_second, conv_last, bias_first[None], bias_second[None])
    lon_a, lon_b = pl.pallas_call(
        corner_kernel,
        out_shape=[jax.ShapeDtypeStruct((lon_rows + 32, lat), BF16)] * 2,
        in_specs=[VMEM] * 4,
        out_specs=[VMEM] * 2,
        compiler_params=big,
        name="corners",
    )(lon_a, lon_b, lat_a, lat_b)
    lon_a = swap(lon_a, "ox", 0, nx, True)
    lon_b = swap(lon_b, "ox", 1, nx, True)
    wide = 2 * lat
    outer = columns + 4 * EDGE
    tiles = columns // 8 + 2
    return pl.pallas_call(
        functools.partial(main_kernel, ny),
        out_shape=[jax.ShapeDtypeStruct((layers, columns, lat), F32)] * 3
        + [jax.ShapeDtypeStruct((columns, lat), F32)],
        in_specs=[VMEM] * 6 + [pl.BlockSpec(memory_space=pltpu.SMEM)] + [VMEM] * 9,
        out_specs=[VMEM] * 4,
        scratch_shapes=[
            pltpu.VMEM((FIELDS, outer, wide), F32),
            pltpu.VMEM((layers, outer, wide), F32),
            pltpu.VMEM((layers, outer, wide), F32),
            pltpu.VMEM((columns + 2 * EDGE, 16, wide), F32),
            pltpu.VMEM((tiles, PITCH, 256), BF16),
            pltpu.VMEM((tiles - 1, 4, PITCH, 256), BF16),
            pltpu.VMEM((tiles - 1, 4, PITCH, 256), BF16),
            pltpu.VMEM((columns // 2 + 1, 16, 128), F32),
            pltpu.VMEM((4 * columns, 128), F32),
        ],
        compiler_params=big,
        name="step",
    )(zonal, merid, thick, land, visc, wind, gravity, lat_a, lat_b, lon_a, lon_b, w1, w2, w3, b1, b2)


def solution(mesh):
    in_specs = (
        P(None, "ox", "oy"),
        P(None, "ox", "oy"),
        P(None, "ox", "oy"),
        P("ox", "oy"),
        P("ox", "oy"),
        P(None, "ox", "oy"),
        P(),
        P(),
        P(),
        P(),
        P(),
        P(),
    )
    out_specs = (P(None, "ox", "oy"), P(None, "ox", "oy"), P(None, "ox", "oy"), P("ox", "oy"))
    body = functools.partial(local, mesh.shape["ox"], mesh.shape["oy"])
    return jax.shard_map(body, mesh=mesh, in_specs=in_specs, out_specs=out_specs, check_vma=False)
```

time: 145 us -> 41.7 us (0.29); the launches traced: 142 us -> 41.4 us
  matrix products: 61.4 us -> 0 us
  Pallas kernels: 0 us -> 21.4 us
  blocking collectives: 20.9 us -> 0 us
  starting transfers between devices: 24.6 us -> 7.68 us
  other arithmetic: 14.4 us -> 0 us
  waiting for transfers between devices: 13.8 us -> 5.24 us
    dot_general x27 -> x0, matrix products: 61.4 us -> none  [conv_valid(): jnp.einsum('oc,cxy->oxy', weight[row_off, col_off], extended[:, row_off:r...]
    pallas_call x0 -> x4, Pallas kernels: none -> 21.4 us  [the longest x1 20.5 us: local(): pl.pallas_call(functools.partial(main_kernel, ny), out_shape=[jax.ShapeDt...]
    all_to_all x2 -> x0, blocking collectives: 20.9 us -> none  [the longest x1 13.7 us: local(): lax.all_to_all(output, 'oy', split_axis=2, concat_axis=1, tiled=True)]
    ppermute x14 -> x4, starting transfers between devices: 24.6 us -> 7.68 us  [swap(): return lax.ppermute(x, axis, pairs)]
    ppermute x14 -> x4, waiting for transfers between devices: 13.8 us -> 5.24 us  [swap(): return lax.ppermute(x, axis, pairs)]
    concatenate x5 -> x0, other arithmetic: 5 us -> none  [the longest x4 3.94 us: with_halo(): block = jnp.concatenate([low, block, high], axis=dim)]
    unnamed x37 -> x38, local copies, waits for them, and re-layouts: 1.79 us -> 6.26 us
    unnamed x1 -> x0, other arithmetic: 1.94 us -> none
  transfers between devices with their start and end apart: 14 -> 4, of which waited for: 6 -> 2; matrix products, arithmetic and copies ran while one was open for 4% -> 0% of each run, Pallas kernels for 0% -> 1%
where the time goes in v1:
time: 41.7 us; the launch traced here: 41.4 us
  Pallas kernels  21.4 us (51%)
  starting transfers between devices  7.68 us (18%)
  local copies, waits for them, and re-layouts  6.26 us (15%)
  waiting for transfers between devices  5.24 us (13%)
  between operations  0.8 us (2%)
    pallas_call x1, Pallas kernels, local(): pl.pallas_call(functools.partial(main_kernel, ny), out_shape=[jax.ShapeDt...  20.5 us
    ppermute x4, starting transfers between devices, swap(): return lax.ppermute(x, axis, pairs)  7.68 us
    unnamed x38, local copies, waits for them, and re-layouts  6.26 us
    ppermute x4, waiting for transfers between devices, swap(): return lax.ppermute(x, axis, pairs)  5.24 us
  transfers between devices with their start and end apart: 4, of which 2 were waited for; matrix products, arithmetic and copies ran while one was open for 0% of the time, Pallas kernels for 1%

profile of v1, /device:TPU:4, one launch (start us, length us, event | category | flops | bytes accessed | tf_op | source)
XLA Modules:
  0.0 41.4 jit_solution(5536694600201534300)
XLA Ops:
  0.6 0.0 copy-start
  0.6 0.9 %copy-done = f32[4,128,128]{2,1,0:T(8,128)S(1)} copy-done((f32[4,128,128]{2,1,0:T(8,128)S(1)}, f32[4,128,128]{2,1,0:T(8,128)}, u32[]{:S(2)}) %copy-start) | copy-done | bytes 262168
  1.6 0.0 copy-start.2
  1.6 0.9 %copy-done.2 = f32[4,128,128]{2,1,0:T(8,128)S(1)} copy-done((f32[4,128,128]{2,1,0:T(8,128)S(1)}, f32[4,128,128]{2,1,0:T(8,128)}, u32[]{:S(2)}) %copy-start.2) | copy-done | bytes 262168
  2.5 0.0 copy-start.4
  2.5 0.9 %copy-done.4 = f32[4,128,128]{2,1,0:T(8,128)S(1)} copy-done((f32[4,128,128]{2,1,0:T(8,128)S(1)}, f32[4,128,128]{2,1,0:T(8,128)}, u32[]{:S(2)}) %copy-start.4) | copy-done | bytes 262168
  3.5 0.0 copy-start.6
  3.5 0.9 %copy-done.6 = f32[2,128,128]{2,1,0:T(8,128)S(1)} copy-done((f32[2,128,128]{2,1,0:T(8,128)S(1)}, f32[2,128,128]{2,1,0:T(8,128)}, u32[]{:S(2)}) %copy-start.6) | copy-done | bytes 131096
  4.4 0.0 copy-start.8
  4.4 0.8 %copy-done.8 = s32[128,128]{1,0:T(8,128)S(1)} copy-done((s32[128,128]{1,0:T(8,128)S(1)}, s32[128,128]{1,0:T(8,128)}, u32[]{:S(2)}) %copy-start.8) | copy-done | bytes 65560
  5.2 0.0 copy-start.10
  5.2 0.8 %copy-done.10 = f32[128,128]{1,0:T(8,128)S(1)} copy-done((f32[128,128]{1,0:T(8,128)S(1)}, f32[128,128]{1,0:T(8,128)}, u32[]{:S(2)}) %copy-start.10) | copy-done | bytes 65560
  6.1 0.0 copy-start.12
  6.1 0.0 copy-start.5
  6.1 0.0 copy-start.7
  6.1 0.0 copy-start.11
  6.1 0.3 pack.1
  6.4 0.1 collective-permute-start
  6.5 3.4 %collective-permute-start.1 = (bf16[128,128]{1,0:T(8,128)(2,1)S(1)}, bf16[128,128]{1,0:T(8,128)(2,1)S(1)}, u32[]{:S(2)}, u32[]{:S(2)}) collective-permute-start(bf16[128,128]{1,0:T(8,128)(2,1)S(1)} %get-tuple-element.16), channel_id=1, source_target_pairs={{1,2},{2,1},{3,4},{4,3},{5,6},{6,5},{9,10},{10,9},{11,12},{12,11},... | collective-permute-start | bytes 98312 | tf_op jit(solution)/shard_map/ppermute | solution.py:409
  9.9 0.0 collective-permute-done.got_a.lat_a
  9.9 2.7 %collective-permute-done.1.got_b.lat_b = bf16[128,128]{1,0:T(8,128)(2,1)S(1)} collective-permute-done((bf16[128,128]{1,0:T(8,128)(2,1)S(1)}, bf16[128,128]{1,0:T(8,128)(2,1)S(1)}, u32[]{:S(2)}, u32[]{:S(2)}) %collective-permute-start.1) | collective-permute-done | bytes 32800 | tf_op jit(solution)/shard_map/ppermute | solution.py:409
  12.6 0.0 copy-start.17
  12.6 0.0 copy-start.16
  12.6 0.0 copy-start.13
  12.6 0.0 copy-start.14
  12.6 0.0 copy-start.3
  12.7 0.0 copy-start.1
  12.7 1.7 %collective-permute-start.2 = (bf16[160,128]{1,0:T(8,128)(2,1)S(1)}, bf16[160,128]{1,0:T(8,128)(2,1)S(1)}, u32[]{:S(2)}, u32[]{:S(2)}) collective-permute-start(bf16[160,128]{1,0:T(8,128)(2,1)S(1)} %get-tuple-element.19), channel_id=1, source_target_pairs={{0,8},{8,0},{16,24},{24,16},{1,9},{9,1},{17,25},{25,17},{2,10},{10... | collective-permute-start | bytes 122888 | tf_op jit(solution)/shard_map/ppermute | solution.py:409
  14.4 2.5 %collective-permute-start.3 = (bf16[160,128]{1,0:T(8,128)(2,1)S(1)}, bf16[160,128]{1,0:T(8,128)(2,1)S(1)}, u32[]{:S(2)}, u32[]{:S(2)}) collective-permute-start(bf16[160,128]{1,0:T(8,128)(2,1)S(1)} %get-tuple-element.20), channel_id=1, source_target_pairs={{0,24},{8,16},{16,8},{24,0},{1,25},{9,17},{17,9},{25,1},{2,26},{10... | collective-permute-start | bytes 122888 | tf_op jit(solution)/shard_map/ppermute | solution.py:409
  16.9 0.0 copy-done.17
  16.9 0.0 copy-done.16
  16.9 0.2 copy.16.first
  17.1 0.0 copy-done.12
  17.1 0.0 copy-done.13
  17.1 0.0 copy-done.14
  17.1 0.0 copy-start.9
  17.1 0.5 %weights.1 = (bf16[4,256,256]{2,1,0:T(8,128)(2,1)S(1)}, bf16[1024,256]{1,0:T(8,128)(2,1)S(1)}, bf16[16,256]{1,0:T(8,128)(2,1)S(1)}, f32[8,256]{1,0:T(8,128)S(1)}, f32[8,256]{1,0:T(8,128)S(1)}) custom-call(bf16[3,3,64,4]{3,2,1,0:T(8,128)(2,1)S(1)} %copy.16.first, bf16[3,3,64,64]{3,2,1,0:T(8,128)(2,1)S(1)} %copy-done.12, bf16[3,3,1,64]{3,2,1,0:T(2,128)(2,1)S(1)} %copy.17.last, ...), custom_call_target="tpu_custom_call" | custom-call | tf_op jit(solution)/shard_map/weights/pallas_call | solution.py:442
  17.6 0.0 collective-permute-done.2.lon_a
  17.6 2.6 %collective-permute-done.3.lon_b = bf16[160,128]{1,0:T(8,128)(2,1)S(1)} collective-permute-done((bf16[160,128]{1,0:T(8,128)(2,1)S(1)}, bf16[160,128]{1,0:T(8,128)(2,1)S(1)}, u32[]{:S(2)}, u32[]{:S(2)}) %collective-permute-start.3) | collective-permute-done | bytes 40992 | tf_op jit(solution)/shard_map/ppermute | solution.py:409
  20.2 0.0 copy-start.15
  20.2 0.0 copy-done.5
  20.2 0.0 copy-done.7
  20.2 0.0 copy-done.11
  20.2 0.0 copy-done.3
  20.2 0.0 copy-done.1
  20.2 0.0 copy-done.9
  20.2 0.6 %copy-done.15 = f32[4]{0:T(128)S(1)} copy-done((f32[4]{0:T(128)S(1)}, f32[4]{0:T(128)}, u32[]{:S(2)}) %copy-start.15) | copy-done | bytes 40
  20.8 20.5 %step.1 = (f32[4,128,128]{2,1,0:T(8,128)}, f32[4,128,128]{2,1,0:T(8,128)}, f32[4,128,128]{2,1,0:T(8,128)}, f32[128,128]{1,0:T(8,128)}) custom-call(f32[4,128,128]{2,1,0:T(8,128)S(1)} %copy-done.1, f32[4,128,128]{2,1,0:T(8,128)S(1)} %copy-done.3, f32[4,128,128]{2,1,0:T(8,128)S(1)} %copy-done.5, s32[128,128]{1,0:T(8,128)S(1)} %copy-done.9, ...), custom_call_target="tpu_custom_call" | custom-call | tf_op jit(solution)/shard_map/step/pallas_call | solution.py:469
  (2 shorter events, 0.0 us)
Async XLA Ops:
  0.6 1.0 %copy-start = (f32[4,128,128]{2,1,0:T(8,128)S(1)}, f32[4,128,128]{2,1,0:T(8,128)}, u32[]{:S(2)}) copy-start(f32[4,128,128]{2,1,0:T(8,128)} %zonal.3) | copy-start | bytes 786436
  1.6 0.9 %copy-start.2 = (f32[4,128,128]{2,1,0:T(8,128)S(1)}, f32[4,128,128]{2,1,0:T(8,128)}, u32[]{:S(2)}) copy-start(f32[4,128,128]{2,1,0:T(8,128)} %merid.3) | copy-start | bytes 786436
  2.5 0.9 %copy-start.4 = (f32[4,128,128]{2,1,0:T(8,128)S(1)}, f32[4,128,128]{2,1,0:T(8,128)}, u32[]{:S(2)}) copy-start(f32[4,128,128]{2,1,0:T(8,128)} %thick.3) | copy-start | bytes 786436
  3.5 0.9 %copy-start.6 = (f32[2,128,128]{2,1,0:T(8,128)S(1)}, f32[2,128,128]{2,1,0:T(8,128)}, u32[]{:S(2)}) copy-start(f32[2,128,128]{2,1,0:T(8,128)} %wind.3) | copy-start | bytes 393220
  4.4 0.8 %copy-start.8 = (s32[128,128]{1,0:T(8,128)S(1)}, s32[128,128]{1,0:T(8,128)}, u32[]{:S(2)}) copy-start(s32[128,128]{1,0:T(8,128)} %land.3) | copy-start | bytes 196612
  5.2 0.8 %copy-start.10 = (f32[128,128]{1,0:T(8,128)S(1)}, f32[128,128]{1,0:T(8,128)}, u32[]{:S(2)}) copy-start(f32[128,128]{1,0:T(8,128)} %visc.3) | copy-start | bytes 196612
  6.1 11.0 %copy-start.12 = (bf16[3,3,64,64]{3,2,1,0:T(8,128)(2,1)S(1)}, bf16[3,3,64,64]{3,2,1,0:T(8,128)(2,1)}, u32[]{:S(2)}) copy-start(bf16[3,3,64,64]{3,2,1,0:T(8,128)(2,1)} %second.1) | copy-start | bytes 221188
  6.1 14.1 %copy-start.5 = (f32[4,128,128]{2,1,0:T(8,128)S(1)}, f32[4,128,128]{2,1,0:T(8,128)}, u32[]{:S(2)}) copy-start(f32[4,128,128]{2,1,0:T(8,128)} %thick.3) | copy-start | bytes 786436
  6.1 14.1 %copy-start.7 = (f32[2,128,128]{2,1,0:T(8,128)S(1)}, f32[2,128,128]{2,1,0:T(8,128)}, u32[]{:S(2)}) copy-start(f32[2,128,128]{2,1,0:T(8,128)} %wind.3) | copy-start | bytes 393220
  6.1 14.1 %copy-start.11 = (f32[128,128]{1,0:T(8,128)S(1)}, f32[128,128]{1,0:T(8,128)}, u32[]{:S(2)}) copy-start(f32[128,128]{1,0:T(8,128)} %visc.3) | copy-start | bytes 196612
  6.4 3.5 %collective-permute-start = (bf16[128,128]{1,0:T(8,128)(2,1)S(1)}, bf16[128,128]{1,0:T(8,128)(2,1)S(1)}, u32[]{:S(2)}, u32[]{:S(2)}) collective-permute-start(bf16[128,128]{1,0:T(8,128)(2,1)S(1)} %get-tuple-element.15), channel_id=1, source_target_pairs={{0,1},{1,0},{2,3},{3,2},{4,5},{5,4},{6,7},{7,6},{8,9},{9,8},{10,11... | collective-permute-start | bytes 98312 | tf_op jit(solution)/shard_map/ppermute | solution.py:409
  6.5 6.1 %collective-permute-start.1 = (bf16[128,128]{1,0:T(8,128)(2,1)S(1)}, bf16[128,128]{1,0:T(8,128)(2,1)S(1)}, u32[]{:S(2)}, u32[]{:S(2)}) collective-permute-start(bf16[128,128]{1,0:T(8,128)(2,1)S(1)} %get-tuple-element.16), channel_id=1, source_target_pairs={{1,2},{2,1},{3,4},{4,3},{5,6},{6,5},{9,10},{10,9},{11,12},{12,11},... | collective-permute-start | bytes 98312 | tf_op jit(solution)/shard_map/ppermute | solution.py:409
  12.6 4.2 %copy-start.17 = (bf16[3,3,1,64]{3,1,2,0:T(4,128)(2,1)S(1)}, bf16[3,3,1,64]{3,1,2,0:T(4,128)(2,1)}, u32[]{:S(2)}) copy-start(bf16[3,3,1,64]{3,1,2,0:T(4,128)(2,1)} %param.23) | copy-start | bytes 3460
  12.6 4.2 %copy-start.16 = (bf16[3,3,64,4]{2,3,1,0:T(4,128)(2,1)S(1)}, bf16[3,3,64,4]{2,3,1,0:T(4,128)(2,1)}, u32[]{:S(2)}) copy-start(bf16[3,3,64,4]{2,3,1,0:T(4,128)(2,1)} %param.19) | copy-start | bytes 13828
  12.6 4.4 %copy-start.13 = (f32[64]{0:T(128)S(1)}, f32[64]{0:T(128)}, u32[]{:S(2)}) copy-start(f32[64]{0:T(128)} %param.20) | copy-start | bytes 772
  12.6 4.4 %copy-start.14 = (f32[64]{0:T(128)S(1)}, f32[64]{0:T(128)}, u32[]{:S(2)}) copy-start(f32[64]{0:T(128)} %param.22) | copy-start | bytes 772
  12.6 7.6 %copy-start.3 = (f32[4,128,128]{2,1,0:T(8,128)S(1)}, f32[4,128,128]{2,1,0:T(8,128)}, u32[]{:S(2)}) copy-start(f32[4,128,128]{2,1,0:T(8,128)} %merid.3) | copy-start | bytes 786436
  12.7 7.5 %copy-start.1 = (f32[4,128,128]{2,1,0:T(8,128)S(1)}, f32[4,128,128]{2,1,0:T(8,128)}, u32[]{:S(2)}) copy-start(f32[4,128,128]{2,1,0:T(8,128)} %zonal.3) | copy-start | bytes 786436
  12.7 4.9 %collective-permute-start.2 = (bf16[160,128]{1,0:T(8,128)(2,1)S(1)}, bf16[160,128]{1,0:T(8,128)(2,1)S(1)}, u32[]{:S(2)}, u32[]{:S(2)}) collective-permute-start(bf16[160,128]{1,0:T(8,128)(2,1)S(1)} %get-tuple-element.19), channel_id=1, source_target_pairs={{0,8},{8,0},{16,24},{24,16},{1,9},{9,1},{17,25},{25,17},{2,10},{10... | collective-permute-start | bytes 122888 | tf_op jit(solution)/shard_map/ppermute | solution.py:409
  14.4 5.8 %collective-permute-start.3 = (bf16[160,128]{1,0:T(8,128)(2,1)S(1)}, bf16[160,128]{1,0:T(8,128)(2,1)S(1)}, u32[]{:S(2)}, u32[]{:S(2)}) collective-permute-start(bf16[160,128]{1,0:T(8,128)(2,1)S(1)} %get-tuple-element.20), channel_id=1, source_target_pairs={{0,24},{8,16},{16,8},{24,0},{1,25},{9,17},{17,9},{25,1},{2,26},{10... | collective-permute-start | bytes 122888 | tf_op jit(solution)/shard_map/ppermute | solution.py:409
  17.1 3.1 %copy-start.9 = (s32[128,128]{1,0:T(8,128)S(1)}, s32[128,128]{1,0:T(8,128)}, u32[]{:S(2)}) copy-start(s32[128,128]{1,0:T(8,128)} %land.3) | copy-start | bytes 196612
  20.2 0.7 %copy-start.15 = (f32[4]{0:T(128)S(1)}, f32[4]{0:T(128)}, u32[]{:S(2)}) copy-start(f32[4]{0:T(128)} %gravity.1) | copy-start | bytes 52

commit v2 on v1

--- a/solution.py
+++ b/solution.py
@@ -28,7 +28,14 @@
     return maps + [sea, visc[rows, :], wind[0, rows, :], wind[1, rows, :]]
 
 
-def pack_kernel(zonal, merid, thick, land, visc, wind, lat_a, lat_b, lon_a, lon_b):
+def pack_kernel(*refs):
+    sources, (lat_a, lat_b, lon_a, lon_b), held, sems = refs[:6], refs[6:10], refs[10:16], refs[16:]
+    copies = [pltpu.make_async_copy(*each) for each in zip(sources, held, sems)]
+    for copy in copies:
+        copy.start()
+    for copy in copies:
+        copy.wait()
+    zonal, merid, thick, land, visc, wind = held
     columns, lat = land.shape
     even_y = lax.rem(lax.axis_index("oy"), 2) == 0
     even_x = lax.rem(lax.axis_index("ox"), 2) == 0
@@ -64,7 +71,7 @@
         out_b[size + 16 * n : size + 16 * n + 16, :] = jnp.where(even_x, low, high)
 
 
-def weight_kernel(first, second, last, bias_first, bias_second, w1, w2, w3, b1, b2):
+def weight_kernel(first, second, last, bias_first, bias_second, gravity, w1, w2, w3, b1, b2, grav):
     hidden = second.shape[2]
     zero = jnp.zeros((hidden, hidden), F32)
     turned = [[second[a, b].astype(F32).T * 0.5 for b in range(3)] for a in range(3)]
@@ -111,10 +118,16 @@
             p, q = 2 * a + ex - dx, 2 * b - dy
             line = jnp.concatenate([piece(p, q), piece(p, q + 1)], axis=1)
             tile = jnp.where(row == k, jnp.broadcast_to(line, (16, 128)), tile)
-        w3[:, 128 * ex : 128 * ex + 128] = tile.astype(BF16)
+        turned_tile = jnp.concatenate([tile] * 8, axis=0).T
+        lane = lax.broadcasted_iota(jnp.int32, (128, 128), 1) // 16
+        for m in range(8):
+            start = 256 * m + 128 * ex
+            w3[start : start + 128, :] = jnp.where(lane == m, turned_tile, 0.0).astype(BF16)
     for bias, out in ((bias_first, b1), (bias_second, b2)):
         half = bias[...] * 0.5
         out[...] = jnp.broadcast_to(jnp.concatenate([half] * 4, axis=1), (8, 256))
+    for l in range(grav.shape[0]):
+        grav[l] = jnp.broadcast_to(gravity[0:1, l : l + 1], grav.shape[1:])
 
 
 def main_kernel(
@@ -125,7 +138,7 @@
     land,
     visc,
     wind,
-    gravity,
+    grav,
     lat_a,
     lat_b,
     lon_a,
@@ -146,6 +159,7 @@
     feat,
     act,
     act_up,
+    second,
     parts,
     sums,
 ):
@@ -228,7 +242,7 @@
             odd[l] = odd[l] + odd[l + 1]
         total = jnp.zeros_like(sea)
         for l in range(layers):
-            total = total + gravity[l] * odd[l]
+            total = total + grav[l] * odd[l]
             prs[l, r : r + 8, :] = total
 
     place = lax.broadcasted_iota(jnp.int32, (EDGE, wide), 1)
@@ -303,9 +317,9 @@
         g = lax.dot_general(
             chooser, got, (((1,), (1,)), ((), ())), preferred_element_type=F32
         ).astype(BF16)
-        feat[t, :, 0:128] = g[:, 0:128]
-        feat[t, :, 128:256] = g[:, 128:256]
-        feat[t + 1, :, 0:128] = g[:, 128:256]
+        feat[t] = g
+        if t + 1 < tiles - 1:
+            feat[t + 1, :, 0:128] = g[:, 128:256]
         if t > 0:
             feat[t - 1, :, 128:256] = g[:, 0:128]
 
@@ -328,65 +342,50 @@
 
     bias1 = b1[0:1, :]
     bias2 = b2[0:1, :]
-    group = 4
-
-    def first_conv(t, count, s):
-        left = feat[pl.ds(t, count)].reshape(count * PITCH, 256)
-        h = jnp.dot(left, w1[s], preferred_element_type=F32)
-        h = activate(h, bias1, count, low_1, high_1)
-        flat = h.reshape(count * PITCH, 256)
-        moved = pltpu.roll(flat, count * PITCH - 1, 0).reshape(count, PITCH, 256)
-        act[pl.ds(t, count), s] = h.astype(BF16)
-        act_up[pl.ds(t, count), s] = moved.astype(BF16)
-
-    whole_groups = (columns // 8) // group
-
-    def first_step(g, carry):
-        for s in range(4):
-            first_conv(g * group, group, s)
+    groups = feat.shape[0]
+
+    def first_step(n, carry):
+        left = feat[...].reshape(groups * PITCH, 256)
+        h = jnp.dot(left, w1[n], preferred_element_type=F32)
+        h = activate(h, bias1, groups, low_1, high_1)
+        moved = pltpu.roll(h.reshape(groups * PITCH, 256), groups * PITCH - 1, 0)
+        act[:, n] = h.astype(BF16)
+        act_up[:, n] = moved.reshape(groups, PITCH, 256).astype(BF16)
         return carry
 
-    lax.fori_loop(0, whole_groups, first_step, 0)
-    for s in range(2):
-        first_conv(columns // 8, 1, s)
-
-    zero_part = jnp.zeros((16, 128), F32)
-
-    def second_step(t, carry):
-        for half in range(2):
-            first_s = 2 * half
-            nxt_t, nxt_s = (t, first_s + 2) if half == 0 else (t + 1, 0)
-            rows = 2 * PITCH
-            top = act[t, first_s : first_s + 2].reshape(rows, 256)
-            top_up = act_up[t, first_s : first_s + 2].reshape(rows, 256)
-            one = act[t, first_s + 1]
-            two = act[nxt_t, nxt_s]
-            one_up = act_up[t, first_s + 1]
-            two_up = act_up[nxt_t, nxt_s]
-            low = jnp.concatenate([one, two], axis=0)
-            low_up = jnp.concatenate([one_up, two_up], axis=0)
-            left = jnp.concatenate([top, top_up, low, low_up], axis=1)
-            h = jnp.dot(left, w2[...], preferred_element_type=F32)
-            h = activate(h, bias2, 2, low_2, high_2).astype(BF16)
-            for k in range(2):
-                parts[t * 4 + first_s + k] = zero_part
-                parts[t * 4 + first_s + k, :, 0:PITCH] = lax.dot_general(
-                    w3[...], h[k], (((1,), (1,)), ((), ())), preferred_element_type=F32
-                )
+    lax.fori_loop(0, 4, first_step, 0)
+
+    block_rows = columns // 2 + 1
+    some = next(n for n in range(16, 0, -1) if block_rows % n == 0)
+    flat = lambda ref: ref.reshape(4 * groups, PITCH, 256)
+    first_act, first_up = flat(act), flat(act_up)
+
+    def second_step(n, carry):
+        at = n * some
+        parts_of = [
+            ref[pl.ds(at + shift, some)].reshape(some * PITCH, 256)
+            for shift in range(2)
+            for ref in (first_act, first_up)
+        ]
+        h = jnp.dot(jnp.concatenate(parts_of, axis=1), w2[...], preferred_element_type=F32)
+        second[pl.ds(at, some)] = activate(h, bias2, some, low_2, high_2).astype(BF16)
         return carry
 
-    lax.fori_loop(0, columns // 8, second_step, 0)
-    t = columns // 8
-    left = jnp.concatenate([act[t, 0], act_up[t, 0], act[t, 1], act_up[t, 1]], axis=1)
-    h = jnp.dot(left, w2[...], preferred_element_type=F32)
-    h = activate(h, bias2, 1, low_2, high_2).astype(BF16)
-    parts[4 * t] = zero_part
-    parts[4 * t, :, 0:PITCH] = lax.dot_general(
-        w3[...], h[0], (((1,), (1,)), ((), ())), preferred_element_type=F32
-    )
+    lax.fori_loop(0, block_rows // some, second_step, 0)
+
+    eights = columns // 16
+    wide_left = [
+        jnp.concatenate([second[8 * g + m] for g in range(eights)], axis=0) for m in range(8)
+    ]
+    last = jnp.dot(jnp.concatenate(wide_left, axis=1), w3[...], preferred_element_type=F32)
+    pad = jnp.zeros((128 - PITCH, 128), F32)
+    for g in range(eights):
+        parts[128 * g : 128 * g + 128, :] = jnp.concatenate([last[PITCH * g : PITCH * (g + 1)], pad], axis=0).T
+    end = jnp.dot(second[8 * eights], w3[0:256], preferred_element_type=F32)
+    parts[128 * eights : 128 * eights + 16, :] = jnp.concatenate([end, pad], axis=0).T[0:16]
 
     for i in range(columns // 2):
-        sums[8 * i : 8 * i + 8, :] = parts[i, 0:8, :] + parts[i + 1, 8:16, :]
+        sums[8 * i : 8 * i + 8, :] = parts[16 * i : 16 * i + 8, :] + parts[16 * i + 24 : 16 * i + 32, :]
     jj = lax.broadcasted_iota(jnp.int32, (128, lat), 0)
     ll = lax.broadcasted_iota(jnp.int32, (128, lat), 1)
     out = jnp.zeros((columns, lat), F32)
@@ -432,27 +431,30 @@
         pack_kernel,
         out_shape=[jax.ShapeDtypeStruct((columns, lat), BF16)] * 2
         + [jax.ShapeDtypeStruct((lon_rows, lat), BF16)] * 2,
-        in_specs=[VMEM] * 6,
+        in_specs=[pl.BlockSpec(memory_space=pltpu.HBM)] * 6,
         out_specs=[VMEM] * 4,
+        scratch_shapes=[pltpu.VMEM(a.shape, a.dtype) for a in (zonal, merid, thick, land, visc, wind)]
+        + [pltpu.SemaphoreType.DMA] * 6,
         compiler_params=big,
         name="pack",
     )(zonal, merid, thick, land, visc, wind)
     lat_a = swap(lat_a, "oy", 0, ny, False)
     lat_b = swap(lat_b, "oy", 1, ny, False)
-    w1, w2, w3, b1, b2 = pl.pallas_call(
+    w1, w2, w3, b1, b2, grav = pl.pallas_call(
         weight_kernel,
         out_shape=[
             jax.ShapeDtypeStruct((4, 256, 256), BF16),
             jax.ShapeDtypeStruct((1024, 256), BF16),
-            jax.ShapeDtypeStruct((16, 256), BF16),
+            jax.ShapeDtypeStruct((2048, 128), BF16),
             jax.ShapeDtypeStruct((8, 256), F32),
             jax.ShapeDtypeStruct((8, 256), F32),
+            jax.ShapeDtypeStruct((layers, 8, 2 * lat), F32),
         ],
-        in_specs=[VMEM] * 5,
-        out_specs=[VMEM] * 5,
+        in_specs=[VMEM] * 6,
+        out_specs=[VMEM] * 6,
         compiler_params=big,
         name="weights",
-    )(conv_first, conv_second, conv_last, bias_first[None], bias_second[None])
+    )(conv_first, conv_second, conv_last, bias_first[None], bias_second[None], gravity[None])
     lon_a, lon_b = pl.pallas_call(
         corner_kernel,
         out_shape=[jax.ShapeDtypeStruct((lon_rows + 32, lat), BF16)] * 2,
@@ -470,22 +472,23 @@
         functools.partial(main_kernel, ny),
         out_shape=[jax.ShapeDtypeStruct((layers, columns, lat), F32)] * 3
         + [jax.ShapeDtypeStruct((columns, lat), F32)],
-        in_specs=[VMEM] * 6 + [pl.BlockSpec(memory_space=pltpu.SMEM)] + [VMEM] * 9,
+        in_specs=[VMEM] * 16,
         out_specs=[VMEM] * 4,
         scratch_shapes=[
             pltpu.VMEM((FIELDS, outer, wide), F32),
             pltpu.VMEM((layers, outer, wide), F32),
             pltpu.VMEM((layers, outer, wide), F32),
             pltpu.VMEM((columns + 2 * EDGE, 16, wide), F32),
-            pltpu.VMEM((tiles, PITCH, 256), BF16),
+            pltpu.VMEM((tiles - 1, PITCH, 256), BF16),
             pltpu.VMEM((tiles - 1, 4, PITCH, 256), BF16),
             pltpu.VMEM((tiles - 1, 4, PITCH, 256), BF16),
-            pltpu.VMEM((columns // 2 + 1, 16, 128), F32),
+            pltpu.VMEM((columns // 2 + 1, PITCH, 256), BF16),
+            pltpu.VMEM((8 * columns + 16, 128), F32),
             pltpu.VMEM((4 * columns, 128), F32),
         ],
         compiler_params=big,
         name="step",
-    )(zonal, merid, thick, land, visc, wind, gravity, lat_a, lat_b, lon_a, lon_b, w1, w2, w3, b1, b2)
+    )(zonal, merid, thick, land, visc, wind, grav, lat_a, lat_b, lon_a, lon_b, w1, w2, w3, b1, b2)
 
 
 def solution(mesh):

time: 41.7 us -> 32.7 us (0.78)
  Pallas kernels: 21.4 us -> 13.1 us
  local copies, waits for them, and re-layouts: 6.26 us -> 5.66 us
    pallas_call x1, Pallas kernels: 20.5 us -> 11.7 us  [local(): pl.pallas_call(functools.partial(main_kernel, ny), out_shape=[jax.ShapeDt...]
    unnamed x38, local copies, waits for them, and re-layouts: 6.26 us -> 5.66 us
    pallas_call x1, Pallas kernels: 0.33 us -> 0.78 us  [local(): pl.pallas_call(pack_kernel, out_shape=[jax.ShapeDtypeStruct((columns, lat...]
  transfers between devices with their start and end apart: 4 -> 4, of which waited for: 2 -> 2; matrix products, arithmetic and copies ran while one was open for 0% -> 1% of each run, Pallas kernels for 1% -> 2%
where the time goes in v2:
time: 32.7 us; the launch traced here: 32.4 us
  Pallas kernels  13.1 us (40%)
  starting transfers between devices  7.68 us (23%)
  local copies, waits for them, and re-layouts  5.66 us (17%)
  waiting for transfers between devices  5.14 us (16%)
  between operations  0.82 us (3%)
    pallas_call x1, Pallas kernels, local(): pl.pallas_call(functools.partial(main_kernel, ny), out_shape=[jax.ShapeDt...  11.7 us
    ppermute x4, starting transfers between devices, swap(): return lax.ppermute(x, axis, pairs)  7.68 us
    unnamed x38, local copies, waits for them, and re-layouts  5.66 us
    ppermute x4, waiting for transfers between devices, swap(): return lax.ppermute(x, axis, pairs)  5.14 us
    pallas_call x1, Pallas kernels, local(): pl.pallas_call(pack_kernel, out_shape=[jax.ShapeDtypeStruct((columns, lat...  0.78 us
  transfers between devices with their start and end apart: 4, of which 2 were waited for; matrix products, arithmetic and copies ran while one was open for 1% of the time, Pallas kernels for 2%

profile of v2, /device:TPU:4, one launch (start us, length us, event | category | flops | bytes accessed | tf_op | source)
XLA Modules:
  0.0 32.4 jit_solution(7311631835141018286)
XLA Ops:
  0.6 0.0 copy-start
  0.6 0.9 %copy-done = f32[4,128,128]{2,1,0:T(8,128)S(1)} copy-done((f32[4,128,128]{2,1,0:T(8,128)S(1)}, f32[4,128,128]{2,1,0:T(8,128)}, u32[]{:S(2)}) %copy-start) | copy-done | bytes 262168
  1.6 0.0 copy-start.2
  1.6 0.9 %copy-done.2 = f32[4,128,128]{2,1,0:T(8,128)S(1)} copy-done((f32[4,128,128]{2,1,0:T(8,128)S(1)}, f32[4,128,128]{2,1,0:T(8,128)}, u32[]{:S(2)}) %copy-start.2) | copy-done | bytes 262168
  2.5 0.0 copy-start.4
  2.5 0.9 %copy-done.4 = f32[4,128,128]{2,1,0:T(8,128)S(1)} copy-done((f32[4,128,128]{2,1,0:T(8,128)S(1)}, f32[4,128,128]{2,1,0:T(8,128)}, u32[]{:S(2)}) %copy-start.4) | copy-done | bytes 262168
  3.5 0.0 copy-start.6
  3.5 0.9 %copy-done.6 = f32[2,128,128]{2,1,0:T(8,128)S(1)} copy-done((f32[2,128,128]{2,1,0:T(8,128)S(1)}, f32[2,128,128]{2,1,0:T(8,128)}, u32[]{:S(2)}) %copy-start.6) | copy-done | bytes 131096
  4.4 0.0 copy-start.8
  4.4 0.8 %copy-done.8 = s32[128,128]{1,0:T(8,128)S(1)} copy-done((s32[128,128]{1,0:T(8,128)S(1)}, s32[128,128]{1,0:T(8,128)}, u32[]{:S(2)}) %copy-start.8) | copy-done | bytes 65560
  5.2 0.0 copy-start.10
  5.2 0.8 %copy-done.10 = f32[128,128]{1,0:T(8,128)S(1)} copy-done((f32[128,128]{1,0:T(8,128)S(1)}, f32[128,128]{1,0:T(8,128)}, u32[]{:S(2)}) %copy-start.10) | copy-done | bytes 65560
  6.1 0.0 copy-start.12
  6.1 0.0 copy-start.5
  6.1 0.0 copy-start.7
  6.1 0.0 copy-start.11
  6.1 0.8 %pack.1 = (bf16[128,128]{1,0:T(8,128)(2,1)S(1)}, bf16[128,128]{1,0:T(8,128)(2,1)S(1)}, bf16[128,128]{1,0:T(8,128)(2,1)S(1)}, bf16[128,128]{1,0:T(8,128)(2,1)S(1)}) custom-call(f32[4,128,128]{2,1,0:T(8,128)S(1)} %copy-done, f32[4,128,128]{2,1,0:T(8,128)S(1)} %copy-done.2, f32[4,128,128]{2,1,0:T(8,128)S(1)} %copy-done.4, s32[128,128]{1,0:T(8,128)S(1)} %copy-done.8, ...), custom_call_target="tpu_custom_call" | custom-call | tf_op jit(solution)/shard_map/pack/pallas_call | solution.py:430
  6.9 0.1 collective-permute-start
  7.0 3.4 %collective-permute-start.1 = (bf16[128,128]{1,0:T(8,128)(2,1)S(1)}, bf16[128,128]{1,0:T(8,128)(2,1)S(1)}, u32[]{:S(2)}, u32[]{:S(2)}) collective-permute-start(bf16[128,128]{1,0:T(8,128)(2,1)S(1)} %get-tuple-element.18), channel_id=1, source_target_pairs={{1,2},{2,1},{3,4},{4,3},{5,6},{6,5},{9,10},{10,9},{11,12},{12,11},... | collective-permute-start | bytes 98312 | tf_op jit(solution)/shard_map/ppermute | solution.py:408
  10.4 0.0 collective-permute-done.got_a.lat_a
  10.4 2.7 %collective-permute-done.1.got_b.lat_b = bf16[128,128]{1,0:T(8,128)(2,1)S(1)} collective-permute-done((bf16[128,128]{1,0:T(8,128)(2,1)S(1)}, bf16[128,128]{1,0:T(8,128)(2,1)S(1)}, u32[]{:S(2)}, u32[]{:S(2)}) %collective-permute-start.1) | collective-permute-done | bytes 32800 | tf_op jit(solution)/shard_map/ppermute | solution.py:408
  13.1 0.0 copy-start.17
  13.1 0.0 copy-start.16
  13.1 0.0 copy-start.13
  13.1 0.0 copy-start.14
  13.1 0.0 copy-start.15
  13.1 0.0 copy-start.3
  13.1 0.0 copy-start.1
  13.2 1.7 %collective-permute-start.2 = (bf16[160,128]{1,0:T(8,128)(2,1)S(1)}, bf16[160,128]{1,0:T(8,128)(2,1)S(1)}, u32[]{:S(2)}, u32[]{:S(2)}) collective-permute-start(bf16[160,128]{1,0:T(8,128)(2,1)S(1)} %get-tuple-element.21), channel_id=1, source_target_pairs={{0,8},{8,0},{16,24},{24,16},{1,9},{9,1},{17,25},{25,17},{2,10},{10... | collective-permute-start | bytes 122888 | tf_op jit(solution)/shard_map/ppermute | solution.py:408
  14.9 2.5 %collective-permute-start.3 = (bf16[160,128]{1,0:T(8,128)(2,1)S(1)}, bf16[160,128]{1,0:T(8,128)(2,1)S(1)}, u32[]{:S(2)}, u32[]{:S(2)}) collective-permute-start(bf16[160,128]{1,0:T(8,128)(2,1)S(1)} %get-tuple-element.22), channel_id=1, source_target_pairs={{0,24},{8,16},{16,8},{24,0},{1,25},{9,17},{17,9},{25,1},{2,26},{10... | collective-permute-start | bytes 122888 | tf_op jit(solution)/shard_map/ppermute | solution.py:408
  17.3 0.0 copy-done.17
  17.3 0.0 copy-done.16
  17.4 0.2 copy.16.first
  17.5 0.0 copy-done.12
  17.5 0.0 copy-done.13
  17.6 0.0 copy-done.14
  17.6 0.0 copy-done.15
  17.6 0.0 copy-start.9
  17.6 0.6 %weights.1 = (bf16[4,256,256]{2,1,0:T(8,128)(2,1)S(1)}, bf16[1024,256]{1,0:T(8,128)(2,1)S(1)}, bf16[2048,128]{1,0:T(8,128)(2,1)S(1)}, f32[8,256]{1,0:T(8,128)S(1...) custom-call(bf16[3,3,64,4]{3,2,1,0:T(8,128)(2,1)S(1)} %copy.16.first, bf16[3,3,64,64]{3,2,1,0:T(8,128)(2,1)S(1)} %copy-done.12, ...), custom_call_target="tpu_custom_call" | custom-call | tf_op jit(solution)/shard_map/weights/pallas_call | solution.py:443
  18.2 0.0 collective-permute-done.2.lon_a
  18.2 2.4 %collective-permute-done.3.lon_b = bf16[160,128]{1,0:T(8,128)(2,1)S(1)} collective-permute-done((bf16[160,128]{1,0:T(8,128)(2,1)S(1)}, bf16[160,128]{1,0:T(8,128)(2,1)S(1)}, u32[]{:S(2)}, u32[]{:S(2)}) %collective-permute-start.3) | collective-permute-done | bytes 40992 | tf_op jit(solution)/shard_map/ppermute | solution.py:408
  20.7 0.0 copy-done.5
  20.7 0.0 copy-done.7
  20.7 0.0 copy-done.11
  20.7 0.0 copy-done.3
  20.7 0.0 copy-done.1
  20.7 0.0 copy-done.9
  20.7 11.7 %step.1 = (f32[4,128,128]{2,1,0:T(8,128)}, f32[4,128,128]{2,1,0:T(8,128)}, f32[4,128,128]{2,1,0:T(8,128)}, f32[128,128]{1,0:T(8,128)}) custom-call(f32[4,128,128]{2,1,0:T(8,128)S(1)} %copy-done.1, f32[4,128,128]{2,1,0:T(8,128)S(1)} %copy-done.3, f32[4,128,128]{2,1,0:T(8,128)S(1)} %copy-done.5, s32[128,128]{1,0:T(8,128)S(1)} %copy-done.9, ...), custom_call_target="tpu_custom_call" | custom-call | tf_op jit(solution)/shard_map/step/pallas_call | solution.py:471
  (2 shorter events, 0.0 us)
Async XLA Ops:
  0.6 1.0 %copy-start = (f32[4,128,128]{2,1,0:T(8,128)S(1)}, f32[4,128,128]{2,1,0:T(8,128)}, u32[]{:S(2)}) copy-start(f32[4,128,128]{2,1,0:T(8,128)} %zonal.1) | copy-start | bytes 786436
  1.6 0.9 %copy-start.2 = (f32[4,128,128]{2,1,0:T(8,128)S(1)}, f32[4,128,128]{2,1,0:T(8,128)}, u32[]{:S(2)}) copy-start(f32[4,128,128]{2,1,0:T(8,128)} %merid.1) | copy-start | bytes 786436
  2.5 0.9 %copy-start.4 = (f32[4,128,128]{2,1,0:T(8,128)S(1)}, f32[4,128,128]{2,1,0:T(8,128)}, u32[]{:S(2)}) copy-start(f32[4,128,128]{2,1,0:T(8,128)} %thick.1) | copy-start | bytes 786436
  3.5 0.9 %copy-start.6 = (f32[2,128,128]{2,1,0:T(8,128)S(1)}, f32[2,128,128]{2,1,0:T(8,128)}, u32[]{:S(2)}) copy-start(f32[2,128,128]{2,1,0:T(8,128)} %wind.1) | copy-start | bytes 393220
  4.4 0.8 %copy-start.8 = (s32[128,128]{1,0:T(8,128)S(1)}, s32[128,128]{1,0:T(8,128)}, u32[]{:S(2)}) copy-start(s32[128,128]{1,0:T(8,128)} %land.1) | copy-start | bytes 196612
  5.2 0.8 %copy-start.10 = (f32[128,128]{1,0:T(8,128)S(1)}, f32[128,128]{1,0:T(8,128)}, u32[]{:S(2)}) copy-start(f32[128,128]{1,0:T(8,128)} %visc.1) | copy-start | bytes 196612
  6.1 11.5 %copy-start.12 = (bf16[3,3,64,64]{3,2,1,0:T(8,128)(2,1)S(1)}, bf16[3,3,64,64]{3,2,1,0:T(8,128)(2,1)}, u32[]{:S(2)}) copy-start(bf16[3,3,64,64]{3,2,1,0:T(8,128)(2,1)} %second.1) | copy-start | bytes 221188
  6.1 14.6 %copy-start.5 = (f32[4,128,128]{2,1,0:T(8,128)S(1)}, f32[4,128,128]{2,1,0:T(8,128)}, u32[]{:S(2)}) copy-start(f32[4,128,128]{2,1,0:T(8,128)} %thick.1) | copy-start | bytes 786436
  6.1 14.6 %copy-start.7 = (f32[2,128,128]{2,1,0:T(8,128)S(1)}, f32[2,128,128]{2,1,0:T(8,128)}, u32[]{:S(2)}) copy-start(f32[2,128,128]{2,1,0:T(8,128)} %wind.1) | copy-start | bytes 393220
  6.1 14.6 %copy-start.11 = (f32[128,128]{1,0:T(8,128)S(1)}, f32[128,128]{1,0:T(8,128)}, u32[]{:S(2)}) copy-start(f32[128,128]{1,0:T(8,128)} %visc.1) | copy-start | bytes 196612
  6.9 3.5 %collective-permute-start = (bf16[128,128]{1,0:T(8,128)(2,1)S(1)}, bf16[128,128]{1,0:T(8,128)(2,1)S(1)}, u32[]{:S(2)}, u32[]{:S(2)}) collective-permute-start(bf16[128,128]{1,0:T(8,128)(2,1)S(1)} %get-tuple-element.17), channel_id=1, source_target_pairs={{0,1},{1,0},{2,3},{3,2},{4,5},{5,4},{6,7},{7,6},{8,9},{9,8},{10,11... | collective-permute-start | bytes 98312 | tf_op jit(solution)/shard_map/ppermute | solution.py:408
  7.0 6.1 %collective-permute-start.1 = (bf16[128,128]{1,0:T(8,128)(2,1)S(1)}, bf16[128,128]{1,0:T(8,128)(2,1)S(1)}, u32[]{:S(2)}, u32[]{:S(2)}) collective-permute-start(bf16[128,128]{1,0:T(8,128)(2,1)S(1)} %get-tuple-element.18), channel_id=1, source_target_pairs={{1,2},{2,1},{3,4},{4,3},{5,6},{6,5},{9,10},{10,9},{11,12},{12,11},... | collective-permute-start | bytes 98312 | tf_op jit(solution)/shard_map/ppermute | solution.py:408
  13.1 4.3 %copy-start.17 = (bf16[3,3,1,64]{3,1,2,0:T(4,128)(2,1)S(1)}, bf16[3,3,1,64]{3,1,2,0:T(4,128)(2,1)}, u32[]{:S(2)}) copy-start(bf16[3,3,1,64]{3,1,2,0:T(4,128)(2,1)} %param.23) | copy-start | bytes 3460
  13.1 4.3 %copy-start.16 = (bf16[3,3,64,4]{2,3,1,0:T(4,128)(2,1)S(1)}, bf16[3,3,64,4]{2,3,1,0:T(4,128)(2,1)}, u32[]{:S(2)}) copy-start(bf16[3,3,64,4]{2,3,1,0:T(4,128)(2,1)} %param.19) | copy-start | bytes 13828
  13.1 4.5 %copy-start.13 = (f32[64]{0:T(128)S(1)}, f32[64]{0:T(128)}, u32[]{:S(2)}) copy-start(f32[64]{0:T(128)} %param.20) | copy-start | bytes 772
  13.1 4.5 %copy-start.14 = (f32[64]{0:T(128)S(1)}, f32[64]{0:T(128)}, u32[]{:S(2)}) copy-start(f32[64]{0:T(128)} %param.22) | copy-start | bytes 772
  13.1 4.5 %copy-start.15 = (f32[4]{0:T(128)S(1)}, f32[4]{0:T(128)}, u32[]{:S(2)}) copy-start(f32[4]{0:T(128)} %param.18) | copy-start | bytes 52
  13.1 7.6 %copy-start.3 = (f32[4,128,128]{2,1,0:T(8,128)S(1)}, f32[4,128,128]{2,1,0:T(8,128)}, u32[]{:S(2)}) copy-start(f32[4,128,128]{2,1,0:T(8,128)} %merid.1) | copy-start | bytes 786436
  13.1 7.5 %copy-start.1 = (f32[4,128,128]{2,1,0:T(8,128)S(1)}, f32[4,128,128]{2,1,0:T(8,128)}, u32[]{:S(2)}) copy-start(f32[4,128,128]{2,1,0:T(8,128)} %zonal.1) | copy-start | bytes 786436
  13.2 5.0 %collective-permute-start.2 = (bf16[160,128]{1,0:T(8,128)(2,1)S(1)}, bf16[160,128]{1,0:T(8,128)(2,1)S(1)}, u32[]{:S(2)}, u32[]{:S(2)}) collective-permute-start(bf16[160,128]{1,0:T(8,128)(2,1)S(1)} %get-tuple-element.21), channel_id=1, source_target_pairs={{0,8},{8,0},{16,24},{24,16},{1,9},{9,1},{17,25},{25,17},{2,10},{10... | collective-permute-start | bytes 122888 | tf_op jit(solution)/shard_map/ppermute | solution.py:408
  14.9 5.8 %collective-permute-start.3 = (bf16[160,128]{1,0:T(8,128)(2,1)S(1)}, bf16[160,128]{1,0:T(8,128)(2,1)S(1)}, u32[]{:S(2)}, u32[]{:S(2)}) collective-permute-start(bf16[160,128]{1,0:T(8,128)(2,1)S(1)} %get-tuple-element.22), channel_id=1, source_target_pairs={{0,24},{8,16},{16,8},{24,0},{1,25},{9,17},{17,9},{25,1},{2,26},{10... | collective-permute-start | bytes 122888 | tf_op jit(solution)/shard_map/ppermute | solution.py:408
  17.6 3.1 %copy-start.9 = (s32[128,128]{1,0:T(8,128)S(1)}, s32[128,128]{1,0:T(8,128)}, u32[]{:S(2)}) copy-start(s32[128,128]{1,0:T(8,128)} %land.1) | copy-start | bytes 196612

commit v3 on v2

v3 whole, which is shorter than its diff:
```python
import functools

import jax
import jax.numpy as jnp
from jax import lax
from jax.experimental import pallas as pl
from jax.experimental.pallas import tpu as pltpu
from jax.sharding import PartitionSpec as P

TIME_STEP = 0.05
REST_DEPTH = 1.4
DRAG_RATE = 0.5

F32 = jnp.float32
BF16 = jnp.bfloat16
EDGE = 8
FIELDS = 16
PITCH = 80
VMEM = pl.BlockSpec(memory_space=pltpu.VMEM)


def own_fields(zonal, merid, thick, land, visc, wind, rows):
    sea = land[rows, :].astype(F32)
    layers = zonal.shape[0]
    maps = [zonal[l, rows, :] * sea for l in range(layers)]
    maps += [merid[l, rows, :] * sea for l in range(layers)]
    maps += [thick[l, rows, :] - REST_DEPTH for l in range(layers)]
    return maps + [sea, visc[rows, :], wind[0, rows, :], wind[1, rows, :]]


def pack_kernel(*refs):
    sources, (lat_a, lat_b), held, sems = refs[:6], refs[6:8], refs[8:14], refs[14:]
    copies = [pltpu.make_async_copy(*each) for each in zip(sources, held, sems)]
    for copy in copies:
        copy.start()
    for copy in copies:
        copy.wait()
    zonal, merid, thick, land, visc, wind = held
    columns, lat = land.shape
    even_y = lax.rem(lax.axis_index("oy"), 2) == 0
    lane = lax.broadcasted_iota(jnp.int32, (16, lat), 1) // EDGE
    for c in range(0, columns, 16):
        low = jnp.zeros((16, lat), F32)
        high = jnp.zeros((16, lat), F32)
        for f, field in enumerate(own_fields(zonal, merid, thick, land, visc, wind, slice(c, c + 16))):
            here = lane == f
            low = jnp.where(here, pltpu.roll(field, EDGE * f % lat, 1), low)
            high = jnp.where(here, pltpu.roll(field, (EDGE * f + EDGE) % lat, 1), high)
        lat_a[c : c + 16, :] = jnp.where(even_y, high, low).astype(BF16)
        lat_b[c : c + 16, :] = jnp.where(even_y, low, high).astype(BF16)


def lon_kernel(zonal, merid, thick, land, visc, wind, got_a, got_b, after, lon_a, lon_b):
    del after
    columns = got_a.shape[0]
    even_x = lax.rem(lax.axis_index("ox"), 2) == 0
    size = EDGE * FIELDS
    maps_low = own_fields(zonal, merid, thick, land, visc, wind, slice(0, EDGE))
    maps_high = own_fields(zonal, merid, thick, land, visc, wind, slice(columns - EDGE, columns))
    for f in range(0, FIELDS, 2):
        low = jnp.concatenate(maps_low[f : f + 2], axis=0)
        high = jnp.concatenate(maps_high[f : f + 2], axis=0)
        lon_a[EDGE * f : EDGE * f + 16, :] = jnp.where(even_x, high, low).astype(BF16)
        lon_b[EDGE * f : EDGE * f + 16, :] = jnp.where(even_x, low, high).astype(BF16)
    for n, got in enumerate((got_a, got_b)):
        low = got[0:16, :]
        high = got[columns - 16 : columns, :]
        lon_a[size + 16 * n : size + 16 * n + 16, :] = jnp.where(even_x, high, low)
        lon_b[size + 16 * n : size + 16 * n + 16, :] = jnp.where(even_x, low, high)


def weight_kernel(first, second, last, bias_first, bias_second, gravity, w1, w2, w3, b1, b2, grav):
    hidden = second.shape[2]
    zero = jnp.zeros((hidden, hidden), F32)
    turned = [[second[a, b].astype(F32).T * 0.5 for b in range(3)] for a in range(3)]
    tap = lambda a, b: turned[a][b] if 0 <= a < 3 and 0 <= b < 3 else zero
    for px in range(4):
        for py in range(4):
            ex, ey, a, b = px % 2, py % 2, px // 2, py // 2
            row = ((2 * a + b) * 4 + 2 * ex + ey) * hidden
            for dx in range(2):
                w2[row : row + hidden, 128 * dx : 128 * dx + 128] = jnp.concatenate(
                    [tap(px - dx, py), tap(px - dx, py - 1)], axis=1
                ).astype(BF16)
    feats = first.shape[3]
    spot = lax.broadcasted_iota(jnp.int32, (256, feats), 0)
    chan = lax.broadcasted_iota(jnp.int32, (256, feats), 1)
    total = jnp.zeros((256, hidden), F32)
    ddx, ddy = spot // 128, (spot // 64) % 2
    for a in range(3):
        for b in range(3):
            want = ((ddx + a) * 4 + ddy + b) * feats + chan
            place = jnp.where(spot % 64 == want, 0.5, 0.0).astype(BF16)
            total = total + lax.dot_general(
                place, first[a, b], (((1,), (1,)), ((), ())), preferred_element_type=F32
            )
    base = jnp.concatenate(
        [
            jnp.concatenate([total[0:64], total[64:128]], axis=1),
            jnp.concatenate([total[128:192], total[192:256]], axis=1),
        ],
        axis=1,
    )
    for s in range(4):
        off = 80 + 32 * s
        w1[s] = jnp.concatenate(
            [jnp.zeros((off, 256), F32), base, jnp.zeros((192 - off, 256), F32)], axis=0
        ).astype(BF16)
    row = lax.broadcasted_iota(jnp.int32, (16, 128), 0)
    blank = jnp.zeros((1, hidden), F32)
    piece = lambda a, b: last[a, b].astype(F32) if 0 <= a < 3 and 0 <= b < 3 else blank
    for ex in range(2):
        tile = jnp.zeros((16, 128), F32)
        for k in range(16):
            a, dx, b, dy = k // 8, (k // 4) % 2, (k // 2) % 2, k % 2
            p, q = 2 * a + ex - dx, 2 * b - dy
            line = jnp.concatenate([piece(p, q), piece(p, q + 1)], axis=1)
            tile = jnp.where(row == k, jnp.broadcast_to(line, (16, 128)), tile)
        turned_tile = jnp.concatenate([tile] * 8, axis=0).T
        lane = lax.broadcasted_iota(jnp.int32, (128, 128), 1) // 16
        for m in range(8):
            start = 256 * m + 128 * ex
            w3[start : start + 128, :] = jnp.where(lane == m, turned_tile, 0.0).astype(BF16)
    for bias, out in ((bias_first, b1), (bias_second, b2)):
        half = bias[...] * 0.5
        out[...] = jnp.broadcast_to(jnp.concatenate([half] * 4, axis=1), (8, 256))
    for l in range(grav.shape[0]):
        grav[l] = jnp.broadcast_to(gravity[0:1, l : l + 1], grav.shape[1:])


def far_tile(n_rows, s_rows, f):
    lat = n_rows.shape[1]
    lane = lax.broadcasted_iota(jnp.int32, n_rows.shape, 1)
    up = pltpu.roll(n_rows, (lat - EDGE * f) % lat, 1)
    down = pltpu.roll(s_rows, (2 * lat - EDGE - EDGE * f) % lat, 1)
    return jnp.where(lane < EDGE, up, jnp.where(lane >= lat - EDGE, down, 0.0))


def dynamics(layers, columns, lat, lat_count, ext, nxt, prs, spread, grav, store):
    oy = lax.axis_index("oy")
    base = 2 * EDGE
    wide = 2 * lat
    chunks = (columns + 2 * EDGE) // EDGE
    sea_id, visc_id, wind_id = 3 * layers, 3 * layers + 1, 3 * layers + 2
    place = lax.broadcasted_iota(jnp.int32, (EDGE, wide), 1)
    place = jnp.where(place < lat + lat // 2, place, place - wide)
    coriolis = 0.3 + 1.4 * ((oy * lat + place).astype(F32) + 0.5) / (lat_count * lat)
    in_lat = (place >= -3) & (place < lat + 3)

    def up(x):
        return pltpu.roll(x, wide - 1, 1)

    def down(x):
        return pltpu.roll(x, 1, 1)

    def rows_of(ch):
        r = EDGE + EDGE * ch
        return slice(r, r + 8), slice(r + 1, r + 9), slice(r - 1, r + 7)

    def thickness(ch):
        here, plus, minus = rows_of(ch)
        sea = ext[sea_id, here, :]
        odd = []
        for l in range(layers):
            h = ext[2 * layers + l, here, :]
            flux_e = ext[l, plus, :] * ext[2 * layers + l, plus, :]
            flux_w = ext[l, minus, :] * ext[2 * layers + l, minus, :]
            flux_y = ext[layers + l, here, :] * h
            diverge = (flux_e - flux_w) * 0.5 + (up(flux_y) - down(flux_y)) * 0.5
            h = h - TIME_STEP * sea * diverge
            nxt[l, here, :] = h
            odd.append(h - REST_DEPTH)
        for l in reversed(range(layers - 1)):
            odd[l] = odd[l] + odd[l + 1]
        total = jnp.zeros_like(sea)
        for l in range(layers):
            total = total + grav[l] * odd[l]
            prs[l, here, :] = total

    def velocity(ch):
        here, plus, minus = rows_of(ch)
        sea = ext[sea_id, here, :]
        v = ext[visc_id, here, :]
        mix = [
            0.5 * (v + ext[visc_id, plus, :]),
            0.5 * (v + ext[visc_id, minus, :]),
            0.5 * (v + up(v)),
            0.5 * (v + down(v)),
        ]

        def lap(f, q):
            near = (ext[f, plus, :], ext[f, minus, :], up(q), down(q))
            total = mix[0] * (near[0] - q)
            for side in range(1, 4):
                total = total + mix[side] * (near[side] - q)
            return total

        heavy = jnp.zeros_like(sea)
        moving = jnp.zeros_like(sea)
        for l in range(layers):
            zm = ext[l, here, :]
            vm = ext[layers + l, here, :]
            p = prs[l, here, :]
            h = nxt[l, here, :]
            grad_x = (prs[l, plus, :] - prs[l, minus, :]) * 0.5
            grad_y = (up(p) - down(p)) * 0.5
            push_x = coriolis * vm - grad_x + lap(l, zm)
            push_y = -coriolis * zm - grad_y + lap(layers + l, vm)
            if l == 0:
                push_x = push_x + ext[wind_id, here, :] / h
                push_y = push_y + ext[wind_id + 1, here, :] / h
            if l == layers - 1:
                push_x = push_x - DRAG_RATE * zm
                push_y = push_y - DRAG_RATE * vm
            zn = sea * (zm + TIME_STEP * push_x)
            vn = sea * (vm + TIME_STEP * push_y)
            store(ch, l, zn[:, 0:lat], vn[:, 0:lat], h[:, 0:lat])
            heavy = heavy + h
            moving = moving + h * (zn * zn + vn * vn)
            if l == 0:
                maps = [zn, vn, sea * (h - REST_DEPTH)]
        maps.append(sea * (0.5 * moving / heavy))
        keep = in_lat
        if ch == 0 or ch == chunks - 1:
            column = lax.broadcasted_iota(jnp.int32, (EDGE, wide), 0) + (EDGE + EDGE * ch - base)
            keep = keep & (column >= -3) & (column < columns + 3)
        for f, m in enumerate(maps):
            m = jnp.where(keep, m, 0.0)
            for dy in range(4):
                spread[EDGE * ch : EDGE * ch + 8, 4 * dy + f, :] = pltpu.roll(m, (wide - dy) % wide, 1) if dy else m

    return thickness, velocity


def block_features(spread, lat):
    wide = 2 * lat
    block = lax.broadcasted_iota(jnp.int32, (PITCH, wide), 0)
    source = lax.broadcasted_iota(jnp.int32, (PITCH, wide), 1)
    chooser = jnp.where(
        (block < lat // 2 + 2) & (source == lax.rem(wide - 3 + 2 * block, wide)), 1.0, 0.0
    ).astype(BF16)

    def take(t):
        got = spread[8 * t : 8 * t + 16].reshape(256, wide).astype(BF16)
        return lax.dot_general(
            chooser, got, (((1,), (1,)), ((), ())), preferred_element_type=F32
        ).astype(BF16)

    return take


def inner_kernel(
    lat_count,
    zonal,
    merid,
    thick,
    land,
    visc,
    wind,
    grav,
    lat_a,
    lat_b,
    zonal_out,
    merid_out,
    thick_out,
    feat,
    edge_ext,
    edge_prs,
    ext,
    nxt,
    prs,
    spread,
):
    layers, columns, lat = zonal.shape
    even_y = lax.rem(lax.axis_index("oy"), 2) == 0
    base = 2 * EDGE
    wide = 2 * lat
    for c in range(0, columns, 16):
        got_a = lat_a[c : c + 16, :].astype(F32)
        got_b = lat_b[c : c + 16, :].astype(F32)
        n_both = jnp.where(even_y, got_a, got_b)
        s_both = jnp.where(even_y, got_b, got_a)
        for h in range(0, 16, EDGE):
            rows = slice(c + h, c + h + EDGE)
            sea = land[rows, :].astype(F32)
            maps = [zonal[l, rows, :] * sea for l in range(layers)]
            maps += [merid[l, rows, :] * sea for l in range(layers)]
            maps += [thick[l, rows, :] for l in range(layers)]
            maps += [sea, visc[rows, :], wind[0, rows, :], wind[1, rows, :]]
            for f in range(FIELDS):
                far = far_tile(n_both[h : h + EDGE], s_both[h : h + EDGE], f)
                if 2 * layers <= f < 3 * layers:
                    far = far + REST_DEPTH
                row = base + c + h
                ext[f, row : row + EDGE, 0:lat] = maps[f]
                ext[f, row : row + EDGE, lat:wide] = far
                edge = {0: 0, EDGE: EDGE, columns - 16: 16, columns - EDGE: 24}.get(c + h)
                if edge is not None:
                    edge_ext[f, edge : edge + EDGE, 0:lat] = maps[f]
                    edge_ext[f, edge : edge + EDGE, lat:wide] = far

    def store(ch, l, zn, vn, h):
        row = EDGE * ch - EDGE
        zonal_out[l, row : row + 8, :] = zn
        merid_out[l, row : row + 8, :] = vn
        thick_out[l, row : row + 8, :] = h

    thickness, velocity = dynamics(layers, columns, lat, lat_count, ext, nxt, prs, spread, grav, store)
    own = columns // EDGE
    for ch in range(1, own + 1):
        thickness(ch)
    for l in range(layers):
        edge_prs[l, 0:8, :] = prs[l, base + EDGE : base + 2 * EDGE, :]
        edge_prs[l, 8:16, :] = prs[l, base + columns - 2 * EDGE : base + columns - EDGE, :]
    for ch in range(2, own):
        velocity(ch)
    take = block_features(spread, lat)
    for t in range(2, own, 2):
        g = take(t)
        feat[t] = g
        feat[t + 1, :, 0:128] = g[:, 128:256]
        feat[t - 1, :, 128:256] = g[:, 0:128]


def main_kernel(
    lat_count,
    zonal_in,
    merid_in,
    thick_in,
    grav,
    lon_a,
    lon_b,
    inner_feat,
    edge_ext,
    edge_prs,
    w1,
    w2,
    w3,
    b1,
    b2,
    zonal_out,
    merid_out,
    thick_out,
    visc_out,
    ext,
    nxt,
    prs,
    spread,
    feat,
    act,
    act_up,
    second,
    parts,
    sums,
    edge_out,
    sems,
):
    columns, lat = visc_out.shape
    layers = grav.shape[0]
    oy = lax.axis_index("oy")
    even_y = lax.rem(oy, 2) == 0
    even_x = lax.rem(lax.axis_index("ox"), 2) == 0
    base = 2 * EDGE
    wide = 2 * lat
    own = columns // EDGE

    west = jnp.where(even_x, lon_b[...], lon_a[...])
    east = jnp.where(even_x, lon_a[...], lon_b[...])
    size = EDGE * FIELDS
    for side, slot, row in ((west, slice(8, 16), base - EDGE), (east, slice(0, 8), base + columns)):
        from_a = side[size : size + 16].astype(F32)[slot]
        from_b = side[size + 16 : size + 32].astype(F32)[slot]
        north = jnp.where(even_y, from_a, from_b)
        south = jnp.where(even_y, from_b, from_a)
        near = side[:size].astype(F32)
        for f in range(FIELDS):
            lift = REST_DEPTH if 2 * layers <= f < 3 * layers else 0.0
            ext[f, row : row + EDGE, 0:lat] = near[EDGE * f : EDGE * f + EDGE] + lift
            ext[f, row : row + EDGE, lat:wide] = far_tile(north, south, f) + lift
    for f in range(FIELDS):
        ext[f, base : base + 16, :] = edge_ext[f, 0:16, :]
        ext[f, base + columns - 16 : base + columns, :] = edge_ext[f, 16:32, :]
    for l in range(layers):
        prs[l, base + EDGE : base + 2 * EDGE, :] = edge_prs[l, 0:8, :]
        prs[l, base + columns - 2 * EDGE : base + columns - EDGE, :] = edge_prs[l, 8:16, :]

    def store(ch, l, zn, vn, h):
        if ch in (1, own):
            side = 0 if ch == 1 else 1
            for k, tile in enumerate((zn, vn, h)):
                edge_out[k, side, l] = tile

    thickness, velocity = dynamics(layers, columns, lat, lat_count, ext, nxt, prs, spread, grav, store)
    edges = (0, 1, own, own + 1)
    for ch in edges:
        thickness(ch)

    for ch in edges:
        velocity(ch)
    copies = [
        pltpu.make_async_copy(
            edge_out.at[k, side],
            out.at[:, pl.ds(side * (columns - EDGE), EDGE), :],
            sems.at[k, side],
        )
        for k, out in enumerate((zonal_out, merid_out, thick_out))
        for side in range(2)
    ]
    for copy in copies:
        copy.start()

    take = block_features(spread, lat)
    blocks = lat // 2 + 2
    first, last = take(0), take(own)
    feat[0] = first
    feat[1, :, 0:128] = first[:, 128:256]
    feat[1, :, 128:256] = inner_feat[1, :, 128:256]
    feat[2, :, 0:128] = inner_feat[own - 1, :, 0:128]
    feat[2, :, 128:256] = last[:, 0:128]
    feat[3] = last

    south_end = jnp.where(oy == 0, 0.0, 1.0)
    north_end = jnp.where(oy == lat_count - 1, 0.0, 1.0)
    brow = lax.broadcasted_iota(jnp.int32, (8, 256), 0)
    quad = lax.broadcasted_iota(jnp.int32, (8, 256), 1) // 64 % 2
    low_1 = jnp.where(brow == 0, south_end, 1.0)
    high_1 = jnp.where(brow == blocks - 1 - 64, north_end, 1.0)
    low_2 = jnp.where((brow == 0) & (quad == 0), south_end, 1.0)
    high_2 = jnp.where((brow == blocks - 2 - 64) & (quad == 1), north_end, 1.0)

    def activate(total, bias, count, low, high):
        total = total + bias
        total = total * jnp.tanh(total) + total
        total = total.reshape(count, PITCH, 256)
        return jnp.concatenate(
            [total[:, 0:8] * low, total[:, 8:64], total[:, 64:72] * high, total[:, 72:]], axis=1
        )

    bias1 = b1[0:1, :]
    bias2 = b2[0:1, :]
    groups = inner_feat.shape[0]

    def first_step(n, carry):
        left = jnp.concatenate([feat[0:2], inner_feat[2 : own - 1], feat[2:4]], axis=0).reshape(groups * PITCH, 256)
        h = jnp.dot(left, w1[n], preferred_element_type=F32)
        h = activate(h, bias1, groups, low_1, high_1)
        moved = pltpu.roll(h.reshape(groups * PITCH, 256), groups * PITCH - 1, 0)
        act[:, n] = h.astype(BF16)
        act_up[:, n] = moved.reshape(groups, PITCH, 256).astype(BF16)
        return carry

    lax.fori_loop(0, 4, first_step, 0)

    block_rows = columns // 2 + 1
    some = next(n for n in range(16, 0, -1) if block_rows % n == 0)
    flat = lambda ref: ref.reshape(4 * groups, PITCH, 256)
    first_act, first_up = flat(act), flat(act_up)

    def second_step(n, carry):
        at = n * some
        parts_of = [
            ref[pl.ds(at + shift, some)].reshape(some * PITCH, 256)
            for shift in range(2)
            for ref in (first_act, first_up)
        ]
        h = jnp.dot(jnp.concatenate(parts_of, axis=1), w2[...], preferred_element_type=F32)
        second[pl.ds(at, some)] = activate(h, bias2, some, low_2, high_2).astype(BF16)
        return carry

    lax.fori_loop(0, block_rows // some, second_step, 0)

    eights = columns // 16
    wide_left = [
        jnp.concatenate([second[8 * g + m] for g in range(eights)], axis=0) for m in range(8)
    ]
    total = jnp.dot(jnp.concatenate(wide_left, axis=1), w3[...], preferred_element_type=F32)
    pad = jnp.zeros((128 - PITCH, 128), F32)
    for g in range(eights):
        parts[128 * g : 128 * g + 128, :] = jnp.concatenate([total[PITCH * g : PITCH * (g + 1)], pad], axis=0).T
    end = jnp.dot(second[8 * eights], w3[0:256], preferred_element_type=F32)
    parts[128 * eights : 128 * eights + 16, :] = jnp.concatenate([end, pad], axis=0).T[0:16]

    for i in range(columns // 2):
        sums[8 * i : 8 * i + 8, :] = parts[16 * i : 16 * i + 8, :] + parts[16 * i + 24 : 16 * i + 32, :]
    jj = lax.broadcasted_iota(jnp.int32, (128, lat), 0)
    ll = lax.broadcasted_iota(jnp.int32, (128, lat), 1)
    out = jnp.zeros((columns, lat), F32)
    for k in range(4):
        x = sums[pl.ds(k, columns, stride=4), :]
        high = x.astype(BF16)
        rest = (x - high.astype(F32)).astype(BF16)
        put_at = jnp.where(ll == 2 * (jj - k // 2) + k % 2, 1.0, 0.0).astype(BF16)
        out = out + jnp.dot(high, put_at, preferred_element_type=F32)
        out = out + jnp.dot(rest, put_at, preferred_element_type=F32)
    visc_out[...] = jnp.exp(out)
    for copy in copies:
        copy.wait()


def swap(x, axis, parity, count, periodic):
    pairs = []
    for i in range(count):
        j = i + 1 if i % 2 == parity else i - 1
        if periodic or 0 <= j < count:
            pairs.append((i, j % count))
    return lax.ppermute(x, axis, pairs)


def local(
    nx,
    ny,
    zonal,
    merid,
    thick,
    land,
    visc,
    wind,
    gravity,
    conv_first,
    bias_first,
    conv_second,
    bias_second,
    conv_last,
):
    layers, columns, lat = zonal.shape
    big = pltpu.CompilerParams(vmem_limit_bytes=48 * 1024 * 1024)
    lon_rows = EDGE * FIELDS
    lat_a, lat_b = pl.pallas_call(
        pack_kernel,
        out_shape=[jax.ShapeDtypeStruct((columns, lat), BF16)] * 2,
        in_specs=[pl.BlockSpec(memory_space=pltpu.HBM)] * 6,
        out_specs=[VMEM] * 2,
        scratch_shapes=[pltpu.VMEM(a.shape, a.dtype) for a in (zonal, merid, thick, land, visc, wind)]
        + [pltpu.SemaphoreType.DMA] * 6,
        compiler_params=pltpu.CompilerParams(vmem_limit_bytes=62 * 1024 * 1024),
        name="pack",
    )(zonal, merid, thick, land, visc, wind)
    lat_a = swap(lat_a, "oy", 0, ny, False)
    lat_b = swap(lat_b, "oy", 1, ny, False)
    w1, w2, w3, b1, b2, grav = pl.pallas_call(
        weight_kernel,
        out_shape=[
            jax.ShapeDtypeStruct((4, 256, 256), BF16),
            jax.ShapeDtypeStruct((1024, 256), BF16),
            jax.ShapeDtypeStruct((2048, 128), BF16),
            jax.ShapeDtypeStruct((8, 256), F32),
            jax.ShapeDtypeStruct((8, 256), F32),
            jax.ShapeDtypeStruct((layers, 8, 2 * lat), F32),
        ],
        in_specs=[VMEM] * 6,
        out_specs=[VMEM] * 6,
        compiler_params=big,
        name="weights",
    )(conv_first, conv_second, conv_last, bias_first[None], bias_second[None], gravity[None])
    lon_a, lon_b = pl.pallas_call(
        lon_kernel,
        out_shape=[jax.ShapeDtypeStruct((lon_rows + 32, lat), BF16)] * 2,
        in_specs=[VMEM] * 8 + [pl.BlockSpec(memory_space=pl.ANY)],
        out_specs=[VMEM] * 2,
        compiler_params=big,
        name="lon",
    )(zonal, merid, thick, land, visc, wind, lat_a, lat_b, grav)
    lon_a = swap(lon_a, "ox", 0, nx, True)
    lon_b = swap(lon_b, "ox", 1, nx, True)
    wide = 2 * lat
    outer = columns + 4 * EDGE
    groups = columns // 8 + 1
    flow = jax.ShapeDtypeStruct((layers, columns, lat), F32)
    work = [
        pltpu.VMEM((FIELDS, outer, wide), F32),
        pltpu.VMEM((layers, outer, wide), F32),
        pltpu.VMEM((layers, outer, wide), F32),
        pltpu.VMEM((columns + 2 * EDGE, 16, wide), F32),
    ]
    zonal_mid, merid_mid, thick_mid, feat, edge_ext, edge_prs = pl.pallas_call(
        functools.partial(inner_kernel, ny),
        out_shape=[
            flow,
            flow,
            flow,
            jax.ShapeDtypeStruct((groups, PITCH, 256), BF16),
            jax.ShapeDtypeStruct((FIELDS, 32, wide), F32),
            jax.ShapeDtypeStruct((layers, 16, wide), F32),
        ],
        in_specs=[VMEM] * 9,
        out_specs=[VMEM] * 6,
        scratch_shapes=work,
        compiler_params=big,
        cost_estimate=pl.CostEstimate(flops=40_000_000, bytes_accessed=8_000_000, transcendentals=0),
        name="inner",
    )(zonal, merid, thick, land, visc, wind, grav, lat_a, lat_b)
    hbm = pl.BlockSpec(memory_space=pltpu.HBM)
    return pl.pallas_call(
        functools.partial(main_kernel, ny),
        out_shape=[flow] * 3 + [jax.ShapeDtypeStruct((columns, lat), F32)],
        in_specs=[hbm] * 3 + [VMEM] * 11,
        out_specs=[hbm] * 3 + [VMEM],
        input_output_aliases={0: 0, 1: 1, 2: 2},
        scratch_shapes=work
        + [
            pltpu.VMEM((4, PITCH, 256), BF16),
            pltpu.VMEM((groups, 4, PITCH, 256), BF16),
            pltpu.VMEM((groups, 4, PITCH, 256), BF16),
            pltpu.VMEM((columns // 2 + 1, PITCH, 256), BF16),
            pltpu.VMEM((8 * columns + 16, 128), F32),
            pltpu.VMEM((4 * columns, 128), F32),
            pltpu.VMEM((3, 2, layers, EDGE, lat), F32),
            pltpu.SemaphoreType.DMA((3, 2)),
        ],
        compiler_params=big,
        name="step",
    )(
        zonal_mid,
        merid_mid,
        thick_mid,
        grav,
        lon_a,
        lon_b,
        feat,
        edge_ext,
        edge_prs,
        w1,
        w2,
        w3,
        b1,
        b2,
    )


def solution(mesh):
    in_specs = (
        P(None, "ox", "oy"),
        P(None, "ox", "oy"),
        P(None, "ox", "oy"),
        P("ox", "oy"),
        P("ox", "oy"),
        P(None, "ox", "oy"),
        P(),
        P(),
        P(),
        P(),
        P(),
        P(),
    )
    out_specs = (P(None, "ox", "oy"), P(None, "ox", "oy"), P(None, "ox", "oy"), P("ox", "oy"))
    body = functools.partial(local, mesh.shape["ox"], mesh.shape["oy"])
    return jax.shard_map(body, mesh=mesh, in_specs=in_specs, out_specs=out_specs, check_vma=False)
```

time: 32.7 us -> 26.6 us (0.81)
  local copies, waits for them, and re-layouts: 5.66 us -> 0.23 us
  waiting for transfers between devices: 5.14 us -> 2.01 us
  Pallas kernels: 13.1 us -> 15.5 us
    unnamed x38 -> x26, local copies, waits for them, and re-layouts: 5.66 us -> 0.23 us
    ppermute x4, waiting for transfers between devices: 5.14 us -> 2.01 us  [swap(): return lax.ppermute(x, axis, pairs)]
    pallas_call x1, Pallas kernels: 0.78 us -> 2.29 us  [local(): pl.pallas_call(pack_kernel, out_shape=[jax.ShapeDtypeStruct((columns, lat...]
    pallas_call x2 -> x3, Pallas kernels: 11.7 us -> 12.6 us  [the longest x1 8.75 us: local(): pl.pallas_call(functools.partial(main_kernel, ny), out_shape=[flow] * 3 +...]
  transfers between devices with their start and end apart: 4 -> 4, of which waited for: 2 -> 1; matrix products, arithmetic and copies ran while one was open for 1% -> 1% of each run, Pallas kernels for 2% -> 17%
where the time goes in v3:
time: 26.6 us; the launch traced here: 26.3 us
  Pallas kernels  15.5 us (58%)
  starting transfers between devices  7.68 us (29%)
  waiting for transfers between devices  2.01 us (8%)
  between operations  0.86 us (3%)
    pallas_call x1, Pallas kernels, local(): pl.pallas_call(functools.partial(main_kernel, ny), out_shape=[flow] * 3 +...  8.75 us
    ppermute x4, starting transfers between devices, swap(): return lax.ppermute(x, axis, pairs)  7.68 us
    pallas_call x1, Pallas kernels, local(): pl.pallas_call(functools.partial(inner_kernel, ny), out_shape=[flow, flow...  3.87 us
    pallas_call x1, Pallas kernels, local(): pl.pallas_call(pack_kernel, out_shape=[jax.ShapeDtypeStruct((columns, lat...  2.29 us
    ppermute x4, waiting for transfers between devices, swap(): return lax.ppermute(x, axis, pairs)  2.01 us
    pallas_call x1, Pallas kernels, local(): pl.pallas_call(weight_kernel, out_shape=[jax.ShapeDtypeStruct((4, 256, 25...  0.61 us
  transfers between devices with their start and end apart: 4, of which 1 were waited for; matrix products, arithmetic and copies ran while one was open for 1% of the time, Pallas kernels for 17%

profile of v3, /device:TPU:4, one launch (start us, length us, event | category | flops | bytes accessed | tf_op | source)
XLA Modules:
  0.0 26.3 jit_solution(11777223017538067147)
XLA Ops:
  0.6 0.0 copy-start.11
  0.6 0.0 copy-start.10
  0.7 0.0 copy-start.6
  0.7 0.0 copy-start.7
  0.7 0.0 copy-start.8
  0.7 0.0 copy-start.9
  0.7 0.0 copy-start.1
  0.7 0.0 copy-start.2
  0.7 0.0 copy-start.5
  0.7 2.3 %pack.1 = (bf16[128,128]{1,0:T(8,128)(2,1)}, bf16[128,128]{1,0:T(8,128)(2,1)}) custom-call(f32[4,128,128]{2,1,0:T(8,128)} %zonal.3, f32[4,128,128]{2,1,0:T(8,128)} %merid.3, f32[4,128,128]{2,1,0:T(8,128)} %thick.3, s32[128,128]{1,0:T(8,128)} %land.3, f32[128,128]{1,0:T(8,128)} %visc.3, f32[2,128,128]{2,1,0:T(8,128)} %wind.3), custom_call_target="tpu_custom_call" | custom-call | tf_op jit(solution)/shard_map/pack/pallas_call | solution.py:528
  3.0 0.0 copy-start
  3.0 0.1 collective-permute-start
  3.1 3.4 %collective-permute-start.1 = (bf16[128,128]{1,0:T(8,128)(2,1)}, bf16[128,128]{1,0:T(8,128)(2,1)S(1)}, u32[]{:S(2)}, u32[]{:S(2)}) collective-permute-start(bf16[128,128]{1,0:T(8,128)(2,1)} %get-tuple-element.22), channel_id=1, source_target_pairs={{1,2},{2,1},{3,4},{4,3},{5,6},{6,5},{9,10},{10,9},{11,12},{12,11},... | collective-permute-start | bytes 98312 | tf_op jit(solution)/shard_map/ppermute | solution.py:506
  6.6 0.0 copy-done.11
  6.6 0.0 copy-done.10
  6.6 0.2 copy.19.first
  6.8 0.0 copy-done.6
  6.8 0.0 copy-done.7
  6.8 0.0 copy-done.8
  6.8 0.0 copy-done.9
  6.8 0.0 copy-start.3
  6.8 0.0 copy-start.4
  6.8 0.6 %weights.1 = (bf16[4,256,256]{2,1,0:T(8,128)(2,1)S(1)}, bf16[1024,256]{1,0:T(8,128)(2,1)S(1)}, bf16[2048,128]{1,0:T(8,128)(2,1)S(1)}, f32[8,256]{1,0:T(8,128)S(1...) custom-call(bf16[3,3,64,4]{3,2,1,0:T(8,128)(2,1)S(1)} %copy.19.first, bf16[3,3,64,64]{3,2,1,0:T(8,128)(2,1)S(1)} %copy-done.6, ...), custom_call_target="tpu_custom_call" | custom-call | tf_op jit(solution)/shard_map/weights/pallas_call | solution.py:540
  7.4 0.0 collective-permute-done.lat_a.got_a
  7.5 2.0 %collective-permute-done.1.lat_b.got_b = bf16[128,128]{1,0:T(8,128)(2,1)S(1)} collective-permute-done((bf16[128,128]{1,0:T(8,128)(2,1)}, bf16[128,128]{1,0:T(8,128)(2,1)S(1)}, u32[]{:S(2)}, u32[]{:S(2)}) %collective-permute-start.1) | collective-permute-done | bytes 32800 | tf_op jit(solution)/shard_map/ppermute | solution.py:506
  9.5 0.0 copy-done.1
  9.5 0.0 copy-done.2
  9.5 0.0 copy-done.5
  9.5 0.0 copy-done
  9.5 0.0 copy-done.3
  9.5 0.0 copy-done.4
  9.5 1.7 %collective-permute-start.2 = (bf16[160,128]{1,0:T(8,128)(2,1)S(1)}, bf16[160,128]{1,0:T(8,128)(2,1)S(1)}, u32[]{:S(2)}, u32[]{:S(2)}) collective-permute-start(bf16[160,128]{1,0:T(8,128)(2,1)S(1)} %get-tuple-element.26), channel_id=1, source_target_pairs={{0,8},{8,0},{16,24},{24,16},{1,9},{9,1},{17,25},{25,17},{2,10},{10... | collective-permute-start | bytes 122888 | tf_op jit(solution)/shard_map/ppermute | solution.py:506
  11.2 2.5 %collective-permute-start.3 = (bf16[160,128]{1,0:T(8,128)(2,1)S(1)}, bf16[160,128]{1,0:T(8,128)(2,1)S(1)}, u32[]{:S(2)}, u32[]{:S(2)}) collective-permute-start(bf16[160,128]{1,0:T(8,128)(2,1)S(1)} %get-tuple-element.27), channel_id=1, source_target_pairs={{0,24},{8,16},{16,8},{24,0},{1,25},{9,17},{17,9},{25,1},{2,26},{10... | collective-permute-start | bytes 122888 | tf_op jit(solution)/shard_map/ppermute | solution.py:506
  13.7 3.9 %inner.1 = (f32[4,128,128]{2,1,0:T(8,128)}, f32[4,128,128]{2,1,0:T(8,128)}, f32[4,128,128]{2,1,0:T(8,128)}, bf16[17,80,256]{2,1,0:T(8,128)(2,1)S(1)}, f32[16,32,...) custom-call(f32[4,128,128]{2,1,0:T(8,128)S(1)} %copy-done, f32[4,128,128]{2,1,0:T(8,128)S(1)} %copy-done.1, ...), custom_call_target="tpu_custom_call" | custom-call | flops 40000000 | bytes 8000000 | tf_op jit(solution)/shard_map/inner/pallas_call | solution.py:575
  17.6 0.0 collective-permute-done.2.lon_a
  17.6 0.0 collective-permute-done.3.lon_b
  17.6 8.7 %step.1 = (f32[4,128,128]{2,1,0:T(8,128)}, f32[4,128,128]{2,1,0:T(8,128)}, f32[4,128,128]{2,1,0:T(8,128)}, f32[128,128]{1,0:T(8,128)}) custom-call(f32[4,128,128]{2,1,0:T(8,128)} %get-tuple-element.23.zonal_in, f32[4,128,128]{2,1,0:T(8,128)} %get-tuple-element.24.merid_in, ...), custom_call_target="tpu_custom_call", output_to_operand_aliasing={{0}: (0, {}), {1}: (1, {}), {2}: (2, {})} | custom-call | tf_op jit(solution)/shard_map/step/pallas_call | solution.py:593
  (2 shorter events, 0.0 us)
Async XLA Ops:
  0.6 5.9 %copy-start.11 = (bf16[3,3,1,64]{3,1,2,0:T(4,128)(2,1)S(1)}, bf16[3,3,1,64]{3,1,2,0:T(4,128)(2,1)}, u32[]{:S(2)}) copy-start(bf16[3,3,1,64]{3,1,2,0:T(4,128)(2,1)} %param.23) | copy-start | bytes 3460
  0.6 5.9 %copy-start.10 = (bf16[3,3,64,4]{2,3,1,0:T(4,128)(2,1)S(1)}, bf16[3,3,64,4]{2,3,1,0:T(4,128)(2,1)}, u32[]{:S(2)}) copy-start(bf16[3,3,64,4]{2,3,1,0:T(4,128)(2,1)} %param.19) | copy-start | bytes 13828
  0.7 6.1 %copy-start.6 = (bf16[3,3,64,64]{3,2,1,0:T(8,128)(2,1)S(1)}, bf16[3,3,64,64]{3,2,1,0:T(8,128)(2,1)}, u32[]{:S(2)}) copy-start(bf16[3,3,64,64]{3,2,1,0:T(8,128)(2,1)} %second.1) | copy-start | bytes 221188
  0.7 6.1 %copy-start.7 = (f32[64]{0:T(128)S(1)}, f32[64]{0:T(128)}, u32[]{:S(2)}) copy-start(f32[64]{0:T(128)} %param.20) | copy-start | bytes 772
  0.7 6.1 %copy-start.8 = (f32[64]{0:T(128)S(1)}, f32[64]{0:T(128)}, u32[]{:S(2)}) copy-start(f32[64]{0:T(128)} %param.22) | copy-start | bytes 772
  0.7 6.1 %copy-start.9 = (f32[4]{0:T(128)S(1)}, f32[4]{0:T(128)}, u32[]{:S(2)}) copy-start(f32[4]{0:T(128)} %param.18) | copy-start | bytes 52
  0.7 8.8 %copy-start.1 = (f32[4,128,128]{2,1,0:T(8,128)S(1)}, f32[4,128,128]{2,1,0:T(8,128)}, u32[]{:S(2)}) copy-start(f32[4,128,128]{2,1,0:T(8,128)} %merid.3) | copy-start | bytes 786436
  0.7 8.8 %copy-start.2 = (f32[4,128,128]{2,1,0:T(8,128)S(1)}, f32[4,128,128]{2,1,0:T(8,128)}, u32[]{:S(2)}) copy-start(f32[4,128,128]{2,1,0:T(8,128)} %thick.3) | copy-start | bytes 786436
  0.7 8.8 %copy-start.5 = (f32[128,128]{1,0:T(8,128)S(1)}, f32[128,128]{1,0:T(8,128)}, u32[]{:S(2)}) copy-start(f32[128,128]{1,0:T(8,128)} %visc.3) | copy-start | bytes 196612
  3.0 6.4 %copy-start = (f32[4,128,128]{2,1,0:T(8,128)S(1)}, f32[4,128,128]{2,1,0:T(8,128)}, u32[]{:S(2)}) copy-start(f32[4,128,128]{2,1,0:T(8,128)} %zonal.3) | copy-start | bytes 786436
  3.0 4.4 %collective-permute-start = (bf16[128,128]{1,0:T(8,128)(2,1)}, bf16[128,128]{1,0:T(8,128)(2,1)S(1)}, u32[]{:S(2)}, u32[]{:S(2)}) collective-permute-start(bf16[128,128]{1,0:T(8,128)(2,1)} %get-tuple-element.21), channel_id=1, source_target_pairs={{0,1},{1,0},{2,3},{3,2},{4,5},{5,4},{6,7},{7,6},{8,9},{9,8},{10,11... | collective-permute-start | bytes 98312 | tf_op jit(solution)/shard_map/ppermute | solution.py:506
  3.1 6.3 %collective-permute-start.1 = (bf16[128,128]{1,0:T(8,128)(2,1)}, bf16[128,128]{1,0:T(8,128)(2,1)S(1)}, u32[]{:S(2)}, u32[]{:S(2)}) collective-permute-start(bf16[128,128]{1,0:T(8,128)(2,1)} %get-tuple-element.22), channel_id=1, source_target_pairs={{1,2},{2,1},{3,4},{4,3},{5,6},{6,5},{9,10},{10,9},{11,12},{12,11},... | collective-permute-start | bytes 98312 | tf_op jit(solution)/shard_map/ppermute | solution.py:506
  6.8 2.7 %copy-start.3 = (f32[2,128,128]{2,1,0:T(8,128)S(1)}, f32[2,128,128]{2,1,0:T(8,128)}, u32[]{:S(2)}) copy-start(f32[2,128,128]{2,1,0:T(8,128)} %wind.3) | copy-start | bytes 393220
  6.8 2.7 %copy-start.4 = (s32[128,128]{1,0:T(8,128)S(1)}, s32[128,128]{1,0:T(8,128)}, u32[]{:S(2)}) copy-start(s32[128,128]{1,0:T(8,128)} %land.3) | copy-start | bytes 196612
  9.5 8.0 %collective-permute-start.2 = (bf16[160,128]{1,0:T(8,128)(2,1)S(1)}, bf16[160,128]{1,0:T(8,128)(2,1)S(1)}, u32[]{:S(2)}, u32[]{:S(2)}) collective-permute-start(bf16[160,128]{1,0:T(8,128)(2,1)S(1)} %get-tuple-element.26), channel_id=1, source_target_pairs={{0,8},{8,0},{16,24},{24,16},{1,9},{9,1},{17,25},{25,17},{2,10},{10... | collective-permute-start | bytes 122888 | tf_op jit(solution)/shard_map/ppermute | solution.py:506
  11.2 6.3 %collective-permute-start.3 = (bf16[160,128]{1,0:T(8,128)(2,1)S(1)}, bf16[160,128]{1,0:T(8,128)(2,1)S(1)}, u32[]{:S(2)}, u32[]{:S(2)}) collective-permute-start(bf16[160,128]{1,0:T(8,128)(2,1)S(1)} %get-tuple-element.27), channel_id=1, source_target_pairs={{0,24},{8,16},{16,8},{24,0},{1,25},{9,17},{17,9},{25,1},{2,26},{10... | collective-permute-start | bytes 122888 | tf_op jit(solution)/shard_map/ppermute | solution.py:506

commit v4 on v3

--- a/solution.py
+++ b/solution.py
@@ -17,6 +17,10 @@
 FIELDS = 16
 PITCH = 80
 VMEM = pl.BlockSpec(memory_space=pltpu.VMEM)
+
+
+def slot(f):
+    return 4 * (f % 4) + f // 4
 
 
 def own_fields(zonal, merid, thick, land, visc, wind, rows):
@@ -43,9 +47,9 @@
         low = jnp.zeros((16, lat), F32)
         high = jnp.zeros((16, lat), F32)
         for f, field in enumerate(own_fields(zonal, merid, thick, land, visc, wind, slice(c, c + 16))):
-            here = lane == f
-            low = jnp.where(here, pltpu.roll(field, EDGE * f % lat, 1), low)
-            high = jnp.where(here, pltpu.roll(field, (EDGE * f + EDGE) % lat, 1), high)
+            here = lane == slot(f)
+            low = jnp.where(here, pltpu.roll(field, EDGE * slot(f) % lat, 1), low)
+            high = jnp.where(here, pltpu.roll(field, (EDGE * slot(f) + EDGE) % lat, 1), high)
         lat_a[c : c + 16, :] = jnp.where(even_y, high, low).astype(BF16)
         lat_b[c : c + 16, :] = jnp.where(even_y, low, high).astype(BF16)
 
@@ -131,21 +135,18 @@
 def far_tile(n_rows, s_rows, f):
     lat = n_rows.shape[1]
     lane = lax.broadcasted_iota(jnp.int32, n_rows.shape, 1)
-    up = pltpu.roll(n_rows, (lat - EDGE * f) % lat, 1)
-    down = pltpu.roll(s_rows, (2 * lat - EDGE - EDGE * f) % lat, 1)
+    up = pltpu.roll(n_rows, (lat - EDGE * slot(f)) % lat, 1)
+    down = pltpu.roll(s_rows, (2 * lat - EDGE - EDGE * slot(f)) % lat, 1)
     return jnp.where(lane < EDGE, up, jnp.where(lane >= lat - EDGE, down, 0.0))
 
 
-def dynamics(layers, columns, lat, lat_count, ext, nxt, prs, spread, grav, store):
+def dynamics(layers, wide, lat, lat_count, ext, nxt, prs, grav, store, emit):
     oy = lax.axis_index("oy")
-    base = 2 * EDGE
-    wide = 2 * lat
-    chunks = (columns + 2 * EDGE) // EDGE
     sea_id, visc_id, wind_id = 3 * layers, 3 * layers + 1, 3 * layers + 2
     place = lax.broadcasted_iota(jnp.int32, (EDGE, wide), 1)
-    place = jnp.where(place < lat + lat // 2, place, place - wide)
+    if wide > lat:
+        place = jnp.where(place < lat + lat // 2, place, place - wide)
     coriolis = 0.3 + 1.4 * ((oy * lat + place).astype(F32) + 0.5) / (lat_count * lat)
-    in_lat = (place >= -3) & (place < lat + 3)
 
     def up(x):
         return pltpu.roll(x, wide - 1, 1)
@@ -174,7 +175,7 @@
             odd[l] = odd[l] + odd[l + 1]
         total = jnp.zeros_like(sea)
         for l in range(layers):
-            total = total + grav[l] * odd[l]
+            total = total + grav[l, :, 0:wide] * odd[l]
             prs[l, here, :] = total
 
     def velocity(ch):
@@ -220,14 +221,7 @@
             if l == 0:
                 maps = [zn, vn, sea * (h - REST_DEPTH)]
         maps.append(sea * (0.5 * moving / heavy))
-        keep = in_lat
-        if ch == 0 or ch == chunks - 1:
-            column = lax.broadcasted_iota(jnp.int32, (EDGE, wide), 0) + (EDGE + EDGE * ch - base)
-            keep = keep & (column >= -3) & (column < columns + 3)
-        for f, m in enumerate(maps):
-            m = jnp.where(keep, m, 0.0)
-            for dy in range(4):
-                spread[EDGE * ch : EDGE * ch + 8, 4 * dy + f, :] = pltpu.roll(m, (wide - dy) % wide, 1) if dy else m
+        emit(ch, maps)
 
     return thickness, velocity
 
@@ -247,6 +241,66 @@
         ).astype(BF16)
 
     return take
+
+
+def scatter(spread, row, maps, wide):
+    for f, m in enumerate(maps):
+        for dy in range(4):
+            spread[row : row + m.shape[0], 4 * dy + f, :] = pltpu.roll(m, (wide - dy) % wide, 1) if dy else m
+
+
+def own_kernel(
+    lat_count,
+    zonal,
+    merid,
+    thick,
+    land,
+    visc,
+    wind,
+    grav,
+    zonal_own,
+    merid_own,
+    thick_own,
+    energy_own,
+    low_out,
+    high_out,
+    ext,
+    nxt,
+    prs,
+):
+    layers, columns, lat = zonal.shape
+    base = 2 * EDGE
+    group = lax.broadcasted_iota(jnp.int32, (EDGE, lat), 1) // EDGE
+    for c in range(0, columns, EDGE):
+        rows = slice(c, c + EDGE)
+        low = jnp.zeros((EDGE, lat), F32)
+        high = jnp.zeros((EDGE, lat), F32)
+        for f, field in enumerate(own_fields(zonal, merid, thick, land, visc, wind, rows)):
+            here = group == slot(f)
+            low = jnp.where(here, pltpu.roll(field, EDGE * slot(f) % lat, 1), low)
+            high = jnp.where(here, pltpu.roll(field, (EDGE * slot(f) + EDGE) % lat, 1), high)
+            if 2 * layers <= f < 3 * layers:
+                field = thick[f - 2 * layers, rows, :]
+            ext[f, base + c : base + c + EDGE, :] = field
+        low_out[rows, :] = low
+        high_out[rows, :] = high
+
+    def store(ch, l, zn, vn, h):
+        row = EDGE * ch - EDGE
+        zonal_own[l, row : row + 8, :] = zn
+        merid_own[l, row : row + 8, :] = vn
+        thick_own[l, row : row + 8, :] = h
+
+    def emit(ch, maps):
+        row = EDGE * ch - EDGE
+        energy_own[row : row + 8, :] = maps[3]
+
+    thickness, velocity = dynamics(layers, lat, lat, lat_count, ext, nxt, prs, grav, store, emit)
+    own = columns // EDGE
+    for ch in range(1, own + 1):
+        thickness(ch)
+    for ch in range(2, own):
+        velocity(ch)
 
 
 def inner_kernel(
@@ -260,21 +314,37 @@
     grav,
     lat_a,
     lat_b,
+    zonal_own,
+    merid_own,
+    thick_own,
+    energy_own,
+    low_own,
+    high_own,
     zonal_out,
     merid_out,
     thick_out,
     feat,
     edge_ext,
-    edge_prs,
-    ext,
+    strip,
     nxt,
     prs,
     spread,
 ):
     layers, columns, lat = zonal.shape
-    even_y = lax.rem(lax.axis_index("oy"), 2) == 0
+    oy = lax.axis_index("oy")
+    even_y = lax.rem(oy, 2) == 0
     base = 2 * EDGE
     wide = 2 * lat
+    own = columns // EDGE
+    part = lat // layers
+    lane = lax.broadcasted_iota(jnp.int32, (EDGE, lat), 1)
+    layer = lane // part
+    spot = lane % part
+
+    def turn(x, shift):
+        return pltpu.roll(x, shift % lat, 1) if shift % lat else x
+
+    edge_rows = {0: 0, 8: 8, 16: 16, columns - 24: 24, columns - 16: 32, columns - 8: 40}
     for c in range(0, columns, 16):
         got_a = lat_a[c : c + 16, :].astype(F32)
         got_b = lat_b[c : c + 16, :].astype(F32)
@@ -282,38 +352,120 @@
         s_both = jnp.where(even_y, got_b, got_a)
         for h in range(0, 16, EDGE):
             rows = slice(c + h, c + h + EDGE)
-            sea = land[rows, :].astype(F32)
-            maps = [zonal[l, rows, :] * sea for l in range(layers)]
-            maps += [merid[l, rows, :] * sea for l in range(layers)]
-            maps += [thick[l, rows, :] for l in range(layers)]
-            maps += [sea, visc[rows, :], wind[0, rows, :], wind[1, rows, :]]
-            for f in range(FIELDS):
-                far = far_tile(n_both[h : h + EDGE], s_both[h : h + EDGE], f)
-                if 2 * layers <= f < 3 * layers:
-                    far = far + REST_DEPTH
-                row = base + c + h
-                ext[f, row : row + EDGE, 0:lat] = maps[f]
-                ext[f, row : row + EDGE, lat:wide] = far
-                edge = {0: 0, EDGE: EDGE, columns - 16: 16, columns - EDGE: 24}.get(c + h)
-                if edge is not None:
-                    edge_ext[f, edge : edge + EDGE, 0:lat] = maps[f]
-                    edge_ext[f, edge : edge + EDGE, lat:wide] = far
-
-    def store(ch, l, zn, vn, h):
-        row = EDGE * ch - EDGE
-        zonal_out[l, row : row + 8, :] = zn
-        merid_out[l, row : row + 8, :] = vn
-        thick_out[l, row : row + 8, :] = h
-
-    thickness, velocity = dynamics(layers, columns, lat, lat_count, ext, nxt, prs, spread, grav, store)
-    own = columns // EDGE
-    for ch in range(1, own + 1):
-        thickness(ch)
-    for l in range(layers):
-        edge_prs[l, 0:8, :] = prs[l, base + EDGE : base + 2 * EDGE, :]
-        edge_prs[l, 8:16, :] = prs[l, base + columns - 2 * EDGE : base + columns - EDGE, :]
-    for ch in range(2, own):
-        velocity(ch)
+            north, south = n_both[h : h + EDGE], s_both[h : h + EDGE]
+            low, high = low_own[rows, :], high_own[rows, :]
+            four = []
+            for g in range(4):
+                tile = jnp.where(spot < 24, turn(high, 16 - 8 * g), turn(north, 24 - 8 * g))
+                tile = jnp.where(spot < 16, turn(low, 8 - 8 * g), tile)
+                four.append(jnp.where(spot < 8, turn(south, -8 * g), tile))
+            four[2] = four[2] + REST_DEPTH
+            other = four.pop()
+            sea, v = other, turn(other, -part)
+            for l in range(1, layers):
+                sea = jnp.where(layer == l, turn(other, part * l), sea)
+                v = jnp.where(layer == l, turn(other, part * (l - 1)), v)
+            four += [sea, v, turn(other, -2 * part), turn(other, -3 * part)]
+            row = base + c + h
+            for n, tile in enumerate(four):
+                strip[n, row : row + EDGE, :] = tile
+            edge = edge_rows.get(c + h)
+            if edge is not None:
+                maps = own_fields(zonal, merid, thick, land, visc, wind, rows)
+                for f in range(FIELDS):
+                    lift = REST_DEPTH if 2 * layers <= f < 3 * layers else 0.0
+                    first = thick[f - 2 * layers, rows, :] if lift else maps[f]
+                    edge_ext[f, edge : edge + EDGE, 0:lat] = first
+                    edge_ext[f, edge : edge + EDGE, lat:wide] = far_tile(north, south, f) + lift
+
+    def lanes(rows):
+        at = lax.broadcasted_iota(jnp.int32, (rows, lat), 1)
+        return at, at // part, at % part
+
+    up = lambda x: turn(x, -1)
+    down = lambda x: turn(x, 1)
+
+    some = columns // 1
+    lane, layer, spot = lanes(some)
+    pull = jnp.broadcast_to(grav[0, 0:1, 0:lat], (some, lat))
+    for l in range(1, layers):
+        pull = jnp.where(layer == l, jnp.broadcast_to(grav[l, 0:1, 0:lat], (some, lat)), pull)
+    for r in range(base, base + columns, some):
+        here, plus, minus = slice(r, r + some), slice(r + 1, r + some + 1), slice(r - 1, r + some - 1)
+        h = strip[2, here, :]
+        flux_y = strip[1, here, :] * h
+        flux_e = strip[0, plus, :] * strip[2, plus, :]
+        flux_w = strip[0, minus, :] * strip[2, minus, :]
+        diverge = (flux_e - flux_w) * 0.5 + (up(flux_y) - down(flux_y)) * 0.5
+        h = h - TIME_STEP * strip[3, here, :] * diverge
+        nxt[here, :] = h
+        total = h - REST_DEPTH
+        total = total + jnp.where(layer < 3, turn(total, -part), 0.0)
+        total = total + jnp.where(layer < 2, turn(total, -2 * part), 0.0)
+        total = total * pull
+        total = total + jnp.where(layer >= 1, turn(total, part), 0.0)
+        prs[here, :] = total + jnp.where(layer >= 2, turn(total, 2 * part), 0.0)
+
+    def over_layers(x):
+        x = x + turn(x, part)
+        return x + turn(x, 2 * part)
+
+    def patch(tile, result, l):
+        tile = jnp.where(lane < 2, turn(result, -EDGE - part * l), tile)
+        return jnp.where(lane >= lat - 2, turn(result, lat - 24 - part * l), tile)
+
+    some = (columns - 2 * EDGE) // 1
+    lane, layer, spot = lanes(some)
+    place = jnp.where(spot < 16, spot - EDGE, lat - EDGE + spot - 16)
+    coriolis = 0.3 + 1.4 * ((oy * lat + place).astype(F32) + 0.5) / (lat_count * lat)
+    drag = jnp.where(layer == layers - 1, DRAG_RATE, 0.0)
+    for r in range(base + EDGE, base + columns - EDGE, some):
+        here, plus, minus = slice(r, r + some), slice(r + 1, r + some + 1), slice(r - 1, r + some - 1)
+        row = slice(r - base, r - base + some)
+        v = strip[4, here, :]
+        mix = [
+            0.5 * (v + strip[4, plus, :]),
+            0.5 * (v + strip[4, minus, :]),
+            0.5 * (v + up(v)),
+            0.5 * (v + down(v)),
+        ]
+
+        def lap(n, q):
+            near = (strip[n, plus, :], strip[n, minus, :], up(q), down(q))
+            total = mix[0] * (near[0] - q)
+            for side in range(1, 4):
+                total = total + mix[side] * (near[side] - q)
+            return total
+
+        sea = strip[3, here, :]
+        zm, vm = strip[0, here, :], strip[1, here, :]
+        h, p = nxt[here, :], prs[here, :]
+        grad_x = (prs[plus, :] - prs[minus, :]) * 0.5
+        grad_y = (up(p) - down(p)) * 0.5
+        wind_x = jnp.where(layer == 0, strip[5, here, :] / h, 0.0)
+        wind_y = jnp.where(layer == 0, strip[6, here, :] / h, 0.0)
+        zn = sea * (zm + TIME_STEP * (coriolis * vm - grad_x + lap(0, zm) + wind_x - drag * zm))
+        vn = sea * (vm + TIME_STEP * (-coriolis * zm - grad_y + lap(1, vm) + wind_y - drag * vm))
+        energy = sea * (0.5 * over_layers(h * (zn * zn + vn * vn)) / over_layers(h))
+        for l in range(layers):
+            for source, result, out in (
+                (zonal_own, zn, zonal_out),
+                (merid_own, vn, merid_out),
+                (thick_own, h, thick_out),
+            ):
+                out[l, row, :] = patch(source[l, row, :], result, l)
+        own_sea = land[row, :].astype(F32)
+        maps = []
+        for tile, result in (
+            (zonal_own[0, row, :], zn),
+            (merid_own[0, row, :], vn),
+            (own_sea * (thick_own[0, row, :] - REST_DEPTH), sea * (h - REST_DEPTH)),
+            (energy_own[row, :], energy),
+        ):
+            far = jnp.where(lane < 3, turn(result, -24), jnp.where(lane >= lat - 3, turn(result, -8), 0.0))
+            maps.append(jnp.concatenate([patch(tile, result, 0), far], axis=1))
+        scatter(spread, r - EDGE, maps, wide)
+
     take = block_features(spread, lat)
     for t in range(2, own, 2):
         g = take(t)
@@ -332,7 +484,6 @@
     lon_b,
     inner_feat,
     edge_ext,
-    edge_prs,
     w1,
     w2,
     w3,
@@ -364,6 +515,14 @@
     wide = 2 * lat
     own = columns // EDGE
 
+    inside = pl.ds(EDGE, columns - 2 * EDGE)
+    copies = [
+        pltpu.make_async_copy(mid.at[:, inside, :], out.at[:, inside, :], sems.at[k, 2])
+        for k, (mid, out) in enumerate(((zonal_in, zonal_out), (merid_in, merid_out), (thick_in, thick_out)))
+    ]
+    for copy in copies:
+        copy.start()
+
     west = jnp.where(even_x, lon_b[...], lon_a[...])
     east = jnp.where(even_x, lon_a[...], lon_b[...])
     size = EDGE * FIELDS
@@ -378,11 +537,8 @@
             ext[f, row : row + EDGE, 0:lat] = near[EDGE * f : EDGE * f + EDGE] + lift
             ext[f, row : row + EDGE, lat:wide] = far_tile(north, south, f) + lift
     for f in range(FIELDS):
-        ext[f, base : base + 16, :] = edge_ext[f, 0:16, :]
-        ext[f, base + columns - 16 : base + columns, :] = edge_ext[f, 16:32, :]
-    for l in range(layers):
-        prs[l, base + EDGE : base + 2 * EDGE, :] = edge_prs[l, 0:8, :]
-        prs[l, base + columns - 2 * EDGE : base + columns - EDGE, :] = edge_prs[l, 8:16, :]
+        ext[f, base : base + 24, :] = edge_ext[f, 0:24, :]
+        ext[f, base + columns - 24 : base + columns, :] = edge_ext[f, 24:48, :]
 
     def store(ch, l, zn, vn, h):
         if ch in (1, own):
@@ -390,14 +546,22 @@
             for k, tile in enumerate((zn, vn, h)):
                 edge_out[k, side, l] = tile
 
-    thickness, velocity = dynamics(layers, columns, lat, lat_count, ext, nxt, prs, spread, grav, store)
+    place = lax.broadcasted_iota(jnp.int32, (EDGE, wide), 1)
+    in_lat = (place < lat + 3) | (place >= wide - 3)
+
+    def emit(ch, maps):
+        column = lax.broadcasted_iota(jnp.int32, (EDGE, wide), 0) + (EDGE + EDGE * ch - base)
+        keep = in_lat & (column >= -3) & (column < columns + 3)
+        scatter(spread, EDGE * ch, [jnp.where(keep, m, 0.0) for m in maps], wide)
+
+    thickness, velocity = dynamics(layers, wide, lat, lat_count, ext, nxt, prs, grav, store, emit)
     edges = (0, 1, own, own + 1)
-    for ch in edges:
+    for ch in (0, 1, 2, own - 1, own, own + 1):
         thickness(ch)
 
     for ch in edges:
         velocity(ch)
-    copies = [
+    copies += [
         pltpu.make_async_copy(
             edge_out.at[k, side],
             out.at[:, pl.ds(side * (columns - EDGE), EDGE), :],
@@ -406,7 +570,7 @@
         for k, out in enumerate((zonal_out, merid_out, thick_out))
         for side in range(2)
     ]
-    for copy in copies:
+    for copy in copies[3:]:
         copy.start()
 
     take = block_features(spread, lat)
@@ -552,6 +716,24 @@
         compiler_params=big,
         name="weights",
     )(conv_first, conv_second, conv_last, bias_first[None], bias_second[None], gravity[None])
+    flow = jax.ShapeDtypeStruct((layers, columns, lat), F32)
+    flat = jax.ShapeDtypeStruct((columns, lat), F32)
+    outer = columns + 4 * EDGE
+    inputs = (zonal, merid, thick, land, visc, wind)
+    own = pl.pallas_call(
+        functools.partial(own_kernel, ny),
+        out_shape=[flow] * 3 + [flat] * 3,
+        in_specs=[VMEM] * 7,
+        out_specs=[VMEM] * 6,
+        scratch_shapes=[
+            pltpu.VMEM((FIELDS, outer, lat), F32),
+            pltpu.VMEM((layers, outer, lat), F32),
+            pltpu.VMEM((layers, outer, lat), F32),
+        ],
+        compiler_params=big,
+        cost_estimate=pl.CostEstimate(flops=20_000_000, bytes_accessed=4_000_000, transcendentals=0),
+        name="own",
+    )(*inputs, grav)
     lon_a, lon_b = pl.pallas_call(
         lon_kernel,
         out_shape=[jax.ShapeDtypeStruct((lon_rows + 32, lat), BF16)] * 2,
@@ -559,43 +741,44 @@
         out_specs=[VMEM] * 2,
         compiler_params=big,
         name="lon",
-    )(zonal, merid, thick, land, visc, wind, lat_a, lat_b, grav)
+    )(*inputs, lat_a, lat_b, own[3])
     lon_a = swap(lon_a, "ox", 0, nx, True)
     lon_b = swap(lon_b, "ox", 1, nx, True)
     wide = 2 * lat
-    outer = columns + 4 * EDGE
     groups = columns // 8 + 1
-    flow = jax.ShapeDtypeStruct((layers, columns, lat), F32)
     work = [
         pltpu.VMEM((FIELDS, outer, wide), F32),
         pltpu.VMEM((layers, outer, wide), F32),
         pltpu.VMEM((layers, outer, wide), F32),
         pltpu.VMEM((columns + 2 * EDGE, 16, wide), F32),
     ]
-    zonal_mid, merid_mid, thick_mid, feat, edge_ext, edge_prs = pl.pallas_call(
+    zonal_mid, merid_mid, thick_mid, feat, edge_ext = pl.pallas_call(
         functools.partial(inner_kernel, ny),
         out_shape=[
             flow,
             flow,
             flow,
             jax.ShapeDtypeStruct((groups, PITCH, 256), BF16),
-            jax.ShapeDtypeStruct((FIELDS, 32, wide), F32),
-            jax.ShapeDtypeStruct((layers, 16, wide), F32),
+            jax.ShapeDtypeStruct((FIELDS, 48, wide), F32),
         ],
-        in_specs=[VMEM] * 9,
-        out_specs=[VMEM] * 6,
-        scratch_shapes=work,
+        in_specs=[VMEM] * 15,
+        out_specs=[VMEM] * 5,
+        scratch_shapes=[
+            pltpu.VMEM((7, outer, lat), F32),
+            pltpu.VMEM((outer, lat), F32),
+            pltpu.VMEM((outer, lat), F32),
+            pltpu.VMEM((columns + 2 * EDGE, 16, wide), F32),
+        ],
         compiler_params=big,
         cost_estimate=pl.CostEstimate(flops=40_000_000, bytes_accessed=8_000_000, transcendentals=0),
         name="inner",
-    )(zonal, merid, thick, land, visc, wind, grav, lat_a, lat_b)
+    )(*inputs, grav, lat_a, lat_b, *own)
     hbm = pl.BlockSpec(memory_space=pltpu.HBM)
     return pl.pallas_call(
         functools.partial(main_kernel, ny),
         out_shape=[flow] * 3 + [jax.ShapeDtypeStruct((columns, lat), F32)],
-        in_specs=[hbm] * 3 + [VMEM] * 11,
+        in_specs=[VMEM] * 13,
         out_specs=[hbm] * 3 + [VMEM],
-        input_output_aliases={0: 0, 1: 1, 2: 2},
         scratch_shapes=work
         + [
             pltpu.VMEM((4, PITCH, 256), BF16),
@@ -605,7 +788,7 @@
             pltpu.VMEM((8 * columns + 16, 128), F32),
             pltpu.VMEM((4 * columns, 128), F32),
             pltpu.VMEM((3, 2, layers, EDGE, lat), F32),
-            pltpu.SemaphoreType.DMA((3, 2)),
+            pltpu.SemaphoreType.DMA((3, 3)),
         ],
         compiler_params=big,
         name="step",
@@ -618,7 +801,6 @@
         lon_b,
         feat,
         edge_ext,
-        edge_prs,
         w1,
         w2,
         w3,

time: 26.6 us -> 26 us (0.977)
  waiting for transfers between devices: 2.01 us -> 0.82 us
  Pallas kernels: 15.5 us -> 16 us
    ppermute x4, waiting for transfers between devices: 2.01 us -> 0.82 us  [swap(): return lax.ppermute(x, axis, pairs)]
    pallas_call x0 -> x1, Pallas kernels: none -> 1.12 us  [local(): pl.pallas_call(functools.partial(own_kernel, ny), out_shape=[flow] * 3 +...]
    pallas_call x1, Pallas kernels: 3.87 us -> 3.1 us  [local(): pl.pallas_call(functools.partial(inner_kernel, ny), out_shape=[flow, flow...]
  transfers between devices with their start and end apart: 4 -> 4, of which waited for: 1 -> 2; matrix products, arithmetic and copies ran while one was open for 1% -> 1% of each run, Pallas kernels for 17% -> 19%
where the time goes in v4:
time: 26 us; the launch traced here: 25.8 us
  Pallas kernels  16 us (62%)
  starting transfers between devices  7.68 us (30%)
  between operations  0.89 us (3%)
  waiting for transfers between devices  0.82 us (3%)
  local copies, waits for them, and re-layouts  0.45 us (2%)
    pallas_call x1, Pallas kernels, local(): pl.pallas_call(functools.partial(main_kernel, ny), out_shape=[flow] * 3 +...  8.84 us
    ppermute x4, starting transfers between devices, swap(): return lax.ppermute(x, axis, pairs)  7.68 us
    pallas_call x1, Pallas kernels, local(): pl.pallas_call(functools.partial(inner_kernel, ny), out_shape=[flow, flow...  3.1 us
    pallas_call x1, Pallas kernels, local(): pl.pallas_call(pack_kernel, out_shape=[jax.ShapeDtypeStruct((columns, lat...  2.29 us
    pallas_call x1, Pallas kernels, local(): pl.pallas_call(functools.partial(own_kernel, ny), out_shape=[flow] * 3 +...  1.12 us
    ppermute x4, waiting for transfers between devices, swap(): return lax.ppermute(x, axis, pairs)  0.82 us
    pallas_call x1, Pallas kernels, local(): pl.pallas_call(weight_kernel, out_shape=[jax.ShapeDtypeStruct((4, 256, 25...  0.61 us
  transfers between devices with their start and end apart: 4, of which 2 were waited for; matrix products, arithmetic and copies ran while one was open for 1% of the time, Pallas kernels for 19%

profile of v4, /device:TPU:4, one launch (start us, length us, event | category | flops | bytes accessed | tf_op | source)
XLA Modules:
  0.0 25.8 jit_solution(16069684400970360859)
XLA Ops:
  0.6 0.0 copy-start.10
  0.6 0.0 copy-start.11
  0.7 0.0 copy-start.6
  0.7 0.0 copy-start.7
  0.7 0.0 copy-start.8
  0.7 0.0 copy-start.9
  0.7 0.0 copy-start.1
  0.7 0.0 copy-start.2
  0.7 0.0 copy-start.5
  0.7 2.3 %pack.1 = (bf16[128,128]{1,0:T(8,128)(2,1)}, bf16[128,128]{1,0:T(8,128)(2,1)}) custom-call(f32[4,128,128]{2,1,0:T(8,128)} %zonal.5, f32[4,128,128]{2,1,0:T(8,128)} %merid.5, f32[4,128,128]{2,1,0:T(8,128)} %thick.5, s32[128,128]{1,0:T(8,128)} %land.5, f32[128,128]{1,0:T(8,128)} %visc.5, f32[2,128,128]{2,1,0:T(8,128)} %wind.5), custom_call_target="tpu_custom_call" | custom-call | tf_op jit(solution)/shard_map/pack/pallas_call | solution.py:692
  3.0 0.0 copy-start
  3.0 0.1 collective-permute-start
  3.1 3.4 %collective-permute-start.1 = (bf16[128,128]{1,0:T(8,128)(2,1)}, bf16[128,128]{1,0:T(8,128)(2,1)S(1)}, u32[]{:S(2)}, u32[]{:S(2)}) collective-permute-start(bf16[128,128]{1,0:T(8,128)(2,1)} %get-tuple-element.27), channel_id=1, source_target_pairs={{1,2},{2,1},{3,4},{4,3},{5,6},{6,5},{9,10},{10,9},{11,12},{12,11},... | collective-permute-start | bytes 98312 | tf_op jit(solution)/shard_map/ppermute | solution.py:670
  6.6 0.0 copy-done.10
  6.6 0.2 copy.16.first
  6.7 0.0 copy-done.11
  6.8 0.0 copy-done.6
  6.8 0.0 copy-done.7
  6.8 0.0 copy-done.8
  6.8 0.0 copy-done.9
  6.8 0.0 copy-start.3
  6.8 0.0 copy-start.4
  6.8 0.6 %weights.1 = (bf16[4,256,256]{2,1,0:T(8,128)(2,1)S(1)}, bf16[1024,256]{1,0:T(8,128)(2,1)S(1)}, bf16[2048,128]{1,0:T(8,128)(2,1)S(1)}, f32[8,256]{1,0:T(8,128)S(1...) custom-call(bf16[3,3,64,4]{3,2,1,0:T(8,128)(2,1)S(1)} %copy.16.first, bf16[3,3,64,64]{3,2,1,0:T(8,128)(2,1)S(1)} %copy-done.6, ...), custom_call_target="tpu_custom_call" | custom-call | tf_op jit(solution)/shard_map/weights/pallas_call | solution.py:704
  7.4 0.0 copy-done.1
  7.5 0.0 copy-done.2
  7.5 0.0 copy-done.5
  7.5 0.0 copy-done
  7.5 0.2 copy-done.3
  7.7 0.0 copy-done.4
  7.7 1.1 %own.1 = (f32[4,128,128]{2,1,0:T(8,128)S(1)}, f32[4,128,128]{2,1,0:T(8,128)S(1)}, f32[4,128,128]{2,1,0:T(8,128)S(1)}, f32[128,128]{1,0:T(8,128)S(1)}, f32[128,128]{1,0:T(8,128)S(1)}, /*index=5*/f32[128,128]{1,0:T(8,128)S(1)}) custom-call(f32[4,128,128]{2,1,0:T(8,128)S(1)} %copy-done, f32[4,128,128]{2,1,0:T(8,128)S(1)} %copy-done.1, ...), custom_call_target="tpu_custom_call" | custom-call | flops 20000000 | bytes 4000000 | tf_op jit(solution)/shard_map/own/pallas_call | solution.py:723
  8.8 0.0 collective-permute-done.lat_a.got_a
  8.8 0.6 %collective-permute-done.1.lat_b.got_b = bf16[128,128]{1,0:T(8,128)(2,1)S(1)} collective-permute-done((bf16[128,128]{1,0:T(8,128)(2,1)}, bf16[128,128]{1,0:T(8,128)(2,1)S(1)}, u32[]{:S(2)}, u32[]{:S(2)}) %collective-permute-start.1) | collective-permute-done | bytes 32800 | tf_op jit(solution)/shard_map/ppermute | solution.py:670
  9.5 1.7 %collective-permute-start.2 = (bf16[160,128]{1,0:T(8,128)(2,1)S(1)}, bf16[160,128]{1,0:T(8,128)(2,1)S(1)}, u32[]{:S(2)}, u32[]{:S(2)}) collective-permute-start(bf16[160,128]{1,0:T(8,128)(2,1)S(1)} %get-tuple-element.37), channel_id=1, source_target_pairs={{0,8},{8,0},{16,24},{24,16},{1,9},{9,1},{17,25},{25,17},{2,10},{10... | collective-permute-start | bytes 122888 | tf_op jit(solution)/shard_map/ppermute | solution.py:670
  11.2 2.5 %collective-permute-start.3 = (bf16[160,128]{1,0:T(8,128)(2,1)S(1)}, bf16[160,128]{1,0:T(8,128)(2,1)S(1)}, u32[]{:S(2)}, u32[]{:S(2)}) collective-permute-start(bf16[160,128]{1,0:T(8,128)(2,1)S(1)} %get-tuple-element.38), channel_id=1, source_target_pairs={{0,24},{8,16},{16,8},{24,0},{1,25},{9,17},{17,9},{25,1},{2,26},{10... | collective-permute-start | bytes 122888 | tf_op jit(solution)/shard_map/ppermute | solution.py:670
  13.7 3.1 %inner.1 = (f32[4,128,128]{2,1,0:T(8,128)S(1)}, f32[4,128,128]{2,1,0:T(8,128)S(1)}, f32[4,128,128]{2,1,0:T(8,128)S(1)}, bf16[17,80,256]{2,1,0:T(8,128)(2,1)S(1)}, f32[16,48,256]{2,1,0:T(8,128)S(1)}) custom-call(f32[4,128,128]{2,1,0:T(8,128)S(1)} %copy-done, f32[4,128,128]{2,1,0:T(8,128)S(1)} %copy-done.1, f32[4,128,128]{2,1,0:T(8,128)S(1)} %copy-done.2, ...), custom_call_target="tpu_custom_call" | custom-call | flops 40000000 | bytes 8000000 | tf_op jit(solution)/shard_map/inner/pallas_call | solution.py:755
  16.8 0.0 collective-permute-done.2.lon_a
  16.8 0.2 collective-permute-done.3.lon_b
  17.0 8.8 %step.1 = (f32[4,128,128]{2,1,0:T(8,128)}, f32[4,128,128]{2,1,0:T(8,128)}, f32[4,128,128]{2,1,0:T(8,128)}, f32[128,128]{1,0:T(8,128)}) custom-call(f32[4,128,128]{2,1,0:T(8,128)S(1)} %get-tuple-element.34.zonal_in, f32[4,128,128]{2,1,0:T(8,128)S(1)} %get-tuple-element.35.merid_in, f32[4,128,128]{2,1,0:T(8,128)S(1)} %get-tuple-element.36.thick_in, ...), custom_call_target="tpu_custom_call" | custom-call | tf_op jit(solution)/shard_map/step/pallas_call | solution.py:777
  (2 shorter events, 0.0 us)
Async XLA Ops:
  0.6 5.9 %copy-start.10 = (bf16[3,3,64,4]{2,3,1,0:T(4,128)(2,1)S(1)}, bf16[3,3,64,4]{2,3,1,0:T(4,128)(2,1)}, u32[]{:S(2)}) copy-start(bf16[3,3,64,4]{2,3,1,0:T(4,128)(2,1)} %param.19) | copy-start | bytes 13828
  0.6 6.1 %copy-start.11 = (bf16[3,3,1,64]{3,1,2,0:T(4,128)(2,1)S(1)}, bf16[3,3,1,64]{3,1,2,0:T(4,128)(2,1)}, u32[]{:S(2)}) copy-start(bf16[3,3,1,64]{3,1,2,0:T(4,128)(2,1)} %param.23) | copy-start | bytes 3460
  0.7 6.1 %copy-start.6 = (bf16[3,3,64,64]{3,2,1,0:T(8,128)(2,1)S(1)}, bf16[3,3,64,64]{3,2,1,0:T(8,128)(2,1)}, u32[]{:S(2)}) copy-start(bf16[3,3,64,64]{3,2,1,0:T(8,128)(2,1)} %second.1) | copy-start | bytes 221188
  0.7 6.1 %copy-start.7 = (f32[64]{0:T(128)S(1)}, f32[64]{0:T(128)}, u32[]{:S(2)}) copy-start(f32[64]{0:T(128)} %param.20) | copy-start | bytes 772
  0.7 6.1 %copy-start.8 = (f32[64]{0:T(128)S(1)}, f32[64]{0:T(128)}, u32[]{:S(2)}) copy-start(f32[64]{0:T(128)} %param.22) | copy-start | bytes 772
  0.7 6.1 %copy-start.9 = (f32[4]{0:T(128)S(1)}, f32[4]{0:T(128)}, u32[]{:S(2)}) copy-start(f32[4]{0:T(128)} %param.18) | copy-start | bytes 52
  0.7 6.8 %copy-start.1 = (f32[4,128,128]{2,1,0:T(8,128)S(1)}, f32[4,128,128]{2,1,0:T(8,128)}, u32[]{:S(2)}) copy-start(f32[4,128,128]{2,1,0:T(8,128)} %merid.5) | copy-start | bytes 786436
  0.7 6.8 %copy-start.2 = (f32[4,128,128]{2,1,0:T(8,128)S(1)}, f32[4,128,128]{2,1,0:T(8,128)}, u32[]{:S(2)}) copy-start(f32[4,128,128]{2,1,0:T(8,128)} %thick.5) | copy-start | bytes 786436
  0.7 6.8 %copy-start.5 = (f32[128,128]{1,0:T(8,128)S(1)}, f32[128,128]{1,0:T(8,128)}, u32[]{:S(2)}) copy-start(f32[128,128]{1,0:T(8,128)} %visc.5) | copy-start | bytes 196612
  3.0 4.5 %copy-start = (f32[4,128,128]{2,1,0:T(8,128)S(1)}, f32[4,128,128]{2,1,0:T(8,128)}, u32[]{:S(2)}) copy-start(f32[4,128,128]{2,1,0:T(8,128)} %zonal.5) | copy-start | bytes 786436
  3.0 5.8 %collective-permute-start = (bf16[128,128]{1,0:T(8,128)(2,1)}, bf16[128,128]{1,0:T(8,128)(2,1)S(1)}, u32[]{:S(2)}, u32[]{:S(2)}) collective-permute-start(bf16[128,128]{1,0:T(8,128)(2,1)} %get-tuple-element.26), channel_id=1, source_target_pairs={{0,1},{1,0},{2,3},{3,2},{4,5},{5,4},{6,7},{7,6},{8,9},{9,8},{10,11... | collective-permute-start | bytes 98312 | tf_op jit(solution)/shard_map/ppermute | solution.py:670
  3.1 6.3 %collective-permute-start.1 = (bf16[128,128]{1,0:T(8,128)(2,1)}, bf16[128,128]{1,0:T(8,128)(2,1)S(1)}, u32[]{:S(2)}, u32[]{:S(2)}) collective-permute-start(bf16[128,128]{1,0:T(8,128)(2,1)} %get-tuple-element.27), channel_id=1, source_target_pairs={{1,2},{2,1},{3,4},{4,3},{5,6},{6,5},{9,10},{10,9},{11,12},{12,11},... | collective-permute-start | bytes 98312 | tf_op jit(solution)/shard_map/ppermute | solution.py:670
  6.8 0.9 %copy-start.3 = (f32[2,128,128]{2,1,0:T(8,128)S(1)}, f32[2,128,128]{2,1,0:T(8,128)}, u32[]{:S(2)}) copy-start(f32[2,128,128]{2,1,0:T(8,128)} %wind.5) | copy-start | bytes 393220
  6.8 0.9 %copy-start.4 = (s32[128,128]{1,0:T(8,128)S(1)}, s32[128,128]{1,0:T(8,128)}, u32[]{:S(2)}) copy-start(s32[128,128]{1,0:T(8,128)} %land.5) | copy-start | bytes 196612
  9.5 7.3 %collective-permute-start.2 = (bf16[160,128]{1,0:T(8,128)(2,1)S(1)}, bf16[160,128]{1,0:T(8,128)(2,1)S(1)}, u32[]{:S(2)}, u32[]{:S(2)}) collective-permute-start(bf16[160,128]{1,0:T(8,128)(2,1)S(1)} %get-tuple-element.37), channel_id=1, source_target_pairs={{0,8},{8,0},{16,24},{24,16},{1,9},{9,1},{17,25},{25,17},{2,10},{10... | collective-permute-start | bytes 122888 | tf_op jit(solution)/shard_map/ppermute | solution.py:670
  11.2 5.8 %collective-permute-start.3 = (bf16[160,128]{1,0:T(8,128)(2,1)S(1)}, bf16[160,128]{1,0:T(8,128)(2,1)S(1)}, u32[]{:S(2)}, u32[]{:S(2)}) collective-permute-start(bf16[160,128]{1,0:T(8,128)(2,1)S(1)} %get-tuple-element.38), channel_id=1, source_target_pairs={{0,24},{8,16},{16,8},{24,0},{1,25},{9,17},{17,9},{25,1},{2,26},{10... | collective-permute-start | bytes 122888 | tf_op jit(solution)/shard_map/ppermute | solution.py:670

commit v5 on v4

--- a/solution.py
+++ b/solution.py
@@ -604,19 +604,22 @@
     bias2 = b2[0:1, :]
     groups = inner_feat.shape[0]
 
-    def first_step(n, carry):
-        left = jnp.concatenate([feat[0:2], inner_feat[2 : own - 1], feat[2:4]], axis=0).reshape(groups * PITCH, 256)
+    all_feat = jnp.concatenate([feat[0:2], inner_feat[2 : own - 1], feat[2:4]], axis=0)
+
+    def first_step(t, count, n):
+        left = all_feat[t : t + count].reshape(count * PITCH, 256)
         h = jnp.dot(left, w1[n], preferred_element_type=F32)
-        h = activate(h, bias1, groups, low_1, high_1)
-        moved = pltpu.roll(h.reshape(groups * PITCH, 256), groups * PITCH - 1, 0)
-        act[:, n] = h.astype(BF16)
-        act_up[:, n] = moved.reshape(groups, PITCH, 256).astype(BF16)
-        return carry
-
-    lax.fori_loop(0, 4, first_step, 0)
+        h = activate(h, bias1, count, low_1, high_1)
+        moved = pltpu.roll(h.reshape(count * PITCH, 256), count * PITCH - 1, 0)
+        act[t : t + count, n] = h.astype(BF16)
+        act_up[t : t + count, n] = moved.reshape(count, PITCH, 256).astype(BF16)
+
+    for n in range(4):
+        for t in range(0, groups, 6):
+            first_step(t, min(6, groups - t), n)
 
     block_rows = columns // 2 + 1
-    some = next(n for n in range(16, 0, -1) if block_rows % n == 0)
+    some = next(n for n in range(6, 0, -1) if block_rows % n == 0)
     flat = lambda ref: ref.reshape(4 * groups, PITCH, 256)
     first_act, first_up = flat(act), flat(act_up)
 
@@ -631,7 +634,8 @@
         second[pl.ds(at, some)] = activate(h, bias2, some, low_2, high_2).astype(BF16)
         return carry
 
-    lax.fori_loop(0, block_rows // some, second_step, 0)
+    for n in range(block_rows // some):
+        second_step(n, 0)
 
     eights = columns // 16
     wide_left = [

time: 26 us -> 24 us (0.923)
  Pallas kernels: 16 us -> 14 us
    pallas_call x1, Pallas kernels: 8.84 us -> 6.81 us  [local(): pl.pallas_call(functools.partial(main_kernel, ny), out_shape=[flow] * 3 +...]
  transfers between devices with their start and end apart: 4 -> 4, of which waited for: 2 -> 2; matrix products, arithmetic and copies ran while one was open for 1% -> 1% of each run, Pallas kernels for 19% -> 20%
where the time goes in v5:
time: 24 us; the launch traced here: 23.8 us
  Pallas kernels  14 us (58%)
  starting transfers between devices  7.68 us (32%)
  between operations  0.89 us (4%)
  waiting for transfers between devices  0.82 us (3%)
  local copies, waits for them, and re-layouts  0.45 us (2%)
    ppermute x4, starting transfers between devices, swap(): return lax.ppermute(x, axis, pairs)  7.68 us
    pallas_call x1, Pallas kernels, local(): pl.pallas_call(functools.partial(main_kernel, ny), out_shape=[flow] * 3 +...  6.81 us
    pallas_call x1, Pallas kernels, local(): pl.pallas_call(functools.partial(inner_kernel, ny), out_shape=[flow, flow...  3.1 us
    pallas_call x1, Pallas kernels, local(): pl.pallas_call(pack_kernel, out_shape=[jax.ShapeDtypeStruct((columns, lat...  2.29 us
    pallas_call x1, Pallas kernels, local(): pl.pallas_call(functools.partial(own_kernel, ny), out_shape=[flow] * 3 +...  1.12 us
    ppermute x4, waiting for transfers between devices, swap(): return lax.ppermute(x, axis, pairs)  0.82 us
    pallas_call x1, Pallas kernels, local(): pl.pallas_call(weight_kernel, out_shape=[jax.ShapeDtypeStruct((4, 256, 25...  0.61 us
  transfers between devices with their start and end apart: 4, of which 2 were waited for; matrix products, arithmetic and copies ran while one was open for 1% of the time, Pallas kernels for 20%

profile of v5, /device:TPU:4, one launch (start us, length us, event | category | flops | bytes accessed | tf_op | source)
XLA Modules:
  0.0 23.8 jit_solution(8425228118478093946)
XLA Ops:
  0.6 0.0 copy-start.10
  0.6 0.0 copy-start.11
  0.7 0.0 copy-start.6
  0.7 0.0 copy-start.7
  0.7 0.0 copy-start.8
  0.7 0.0 copy-start.9
  0.7 0.0 copy-start.1
  0.7 0.0 copy-start.2
  0.7 0.0 copy-start.5
  0.7 2.3 %pack.1 = (bf16[128,128]{1,0:T(8,128)(2,1)}, bf16[128,128]{1,0:T(8,128)(2,1)}) custom-call(f32[4,128,128]{2,1,0:T(8,128)} %zonal.5, f32[4,128,128]{2,1,0:T(8,128)} %merid.5, f32[4,128,128]{2,1,0:T(8,128)} %thick.5, s32[128,128]{1,0:T(8,128)} %land.5, f32[128,128]{1,0:T(8,128)} %visc.5, f32[2,128,128]{2,1,0:T(8,128)} %wind.5), custom_call_target="tpu_custom_call" | custom-call | tf_op jit(solution)/shard_map/pack/pallas_call | solution.py:696
  3.0 0.0 copy-start
  3.0 0.1 collective-permute-start
  3.1 3.4 %collective-permute-start.1 = (bf16[128,128]{1,0:T(8,128)(2,1)}, bf16[128,128]{1,0:T(8,128)(2,1)S(1)}, u32[]{:S(2)}, u32[]{:S(2)}) collective-permute-start(bf16[128,128]{1,0:T(8,128)(2,1)} %get-tuple-element.27), channel_id=1, source_target_pairs={{1,2},{2,1},{3,4},{4,3},{5,6},{6,5},{9,10},{10,9},{11,12},{12,11},... | collective-permute-start | bytes 98312 | tf_op jit(solution)/shard_map/ppermute | solution.py:674
  6.6 0.0 copy-done.10
  6.6 0.2 copy.16.first
  6.7 0.0 copy-done.11
  6.8 0.0 copy-done.6
  6.8 0.0 copy-done.7
  6.8 0.0 copy-done.8
  6.8 0.0 copy-done.9
  6.8 0.0 copy-start.3
  6.8 0.0 copy-start.4
  6.8 0.6 %weights.1 = (bf16[4,256,256]{2,1,0:T(8,128)(2,1)S(1)}, bf16[1024,256]{1,0:T(8,128)(2,1)S(1)}, bf16[2048,128]{1,0:T(8,128)(2,1)S(1)}, f32[8,256]{1,0:T(8,128)S(1...) custom-call(bf16[3,3,64,4]{3,2,1,0:T(8,128)(2,1)S(1)} %copy.16.first, bf16[3,3,64,64]{3,2,1,0:T(8,128)(2,1)S(1)} %copy-done.6, ...), custom_call_target="tpu_custom_call" | custom-call | tf_op jit(solution)/shard_map/weights/pallas_call | solution.py:708
  7.4 0.0 copy-done.1
  7.5 0.0 copy-done.2
  7.5 0.0 copy-done.5
  7.5 0.0 copy-done
  7.5 0.2 copy-done.3
  7.7 0.0 copy-done.4
  7.7 1.1 %own.1 = (f32[4,128,128]{2,1,0:T(8,128)S(1)}, f32[4,128,128]{2,1,0:T(8,128)S(1)}, f32[4,128,128]{2,1,0:T(8,128)S(1)}, f32[128,128]{1,0:T(8,128)S(1)}, f32[128,128]{1,0:T(8,128)S(1)}, /*index=5*/f32[128,128]{1,0:T(8,128)S(1)}) custom-call(f32[4,128,128]{2,1,0:T(8,128)S(1)} %copy-done, f32[4,128,128]{2,1,0:T(8,128)S(1)} %copy-done.1, ...), custom_call_target="tpu_custom_call" | custom-call | flops 20000000 | bytes 4000000 | tf_op jit(solution)/shard_map/own/pallas_call | solution.py:727
  8.8 0.0 collective-permute-done.lat_a.got_a
  8.8 0.6 %collective-permute-done.1.lat_b.got_b = bf16[128,128]{1,0:T(8,128)(2,1)S(1)} collective-permute-done((bf16[128,128]{1,0:T(8,128)(2,1)}, bf16[128,128]{1,0:T(8,128)(2,1)S(1)}, u32[]{:S(2)}, u32[]{:S(2)}) %collective-permute-start.1) | collective-permute-done | bytes 32800 | tf_op jit(solution)/shard_map/ppermute | solution.py:674
  9.5 1.7 %collective-permute-start.2 = (bf16[160,128]{1,0:T(8,128)(2,1)S(1)}, bf16[160,128]{1,0:T(8,128)(2,1)S(1)}, u32[]{:S(2)}, u32[]{:S(2)}) collective-permute-start(bf16[160,128]{1,0:T(8,128)(2,1)S(1)} %get-tuple-element.37), channel_id=1, source_target_pairs={{0,8},{8,0},{16,24},{24,16},{1,9},{9,1},{17,25},{25,17},{2,10},{10... | collective-permute-start | bytes 122888 | tf_op jit(solution)/shard_map/ppermute | solution.py:674
  11.2 2.5 %collective-permute-start.3 = (bf16[160,128]{1,0:T(8,128)(2,1)S(1)}, bf16[160,128]{1,0:T(8,128)(2,1)S(1)}, u32[]{:S(2)}, u32[]{:S(2)}) collective-permute-start(bf16[160,128]{1,0:T(8,128)(2,1)S(1)} %get-tuple-element.38), channel_id=1, source_target_pairs={{0,24},{8,16},{16,8},{24,0},{1,25},{9,17},{17,9},{25,1},{2,26},{10... | collective-permute-start | bytes 122888 | tf_op jit(solution)/shard_map/ppermute | solution.py:674
  13.7 3.1 %inner.1 = (f32[4,128,128]{2,1,0:T(8,128)S(1)}, f32[4,128,128]{2,1,0:T(8,128)S(1)}, f32[4,128,128]{2,1,0:T(8,128)S(1)}, bf16[17,80,256]{2,1,0:T(8,128)(2,1)S(1)}, f32[16,48,256]{2,1,0:T(8,128)S(1)}) custom-call(f32[4,128,128]{2,1,0:T(8,128)S(1)} %copy-done, f32[4,128,128]{2,1,0:T(8,128)S(1)} %copy-done.1, f32[4,128,128]{2,1,0:T(8,128)S(1)} %copy-done.2, ...), custom_call_target="tpu_custom_call" | custom-call | flops 40000000 | bytes 8000000 | tf_op jit(solution)/shard_map/inner/pallas_call | solution.py:759
  16.8 0.0 collective-permute-done.2.lon_a
  16.8 0.2 collective-permute-done.3.lon_b
  17.0 6.8 %step.1 = (f32[4,128,128]{2,1,0:T(8,128)}, f32[4,128,128]{2,1,0:T(8,128)}, f32[4,128,128]{2,1,0:T(8,128)}, f32[128,128]{1,0:T(8,128)}) custom-call(f32[4,128,128]{2,1,0:T(8,128)S(1)} %get-tuple-element.34.zonal_in, f32[4,128,128]{2,1,0:T(8,128)S(1)} %get-tuple-element.35.merid_in, f32[4,128,128]{2,1,0:T(8,128)S(1)} %get-tuple-element.36.thick_in, ...), custom_call_target="tpu_custom_call" | custom-call | tf_op jit(solution)/shard_map/step/pallas_call | solution.py:781
  (2 shorter events, 0.0 us)
Async XLA Ops:
  0.6 5.9 %copy-start.10 = (bf16[3,3,64,4]{2,3,1,0:T(4,128)(2,1)S(1)}, bf16[3,3,64,4]{2,3,1,0:T(4,128)(2,1)}, u32[]{:S(2)}) copy-start(bf16[3,3,64,4]{2,3,1,0:T(4,128)(2,1)} %param.19) | copy-start | bytes 13828
  0.6 6.1 %copy-start.11 = (bf16[3,3,1,64]{3,1,2,0:T(4,128)(2,1)S(1)}, bf16[3,3,1,64]{3,1,2,0:T(4,128)(2,1)}, u32[]{:S(2)}) copy-start(bf16[3,3,1,64]{3,1,2,0:T(4,128)(2,1)} %param.23) | copy-start | bytes 3460
  0.7 6.1 %copy-start.6 = (bf16[3,3,64,64]{3,2,1,0:T(8,128)(2,1)S(1)}, bf16[3,3,64,64]{3,2,1,0:T(8,128)(2,1)}, u32[]{:S(2)}) copy-start(bf16[3,3,64,64]{3,2,1,0:T(8,128)(2,1)} %second.1) | copy-start | bytes 221188
  0.7 6.1 %copy-start.7 = (f32[64]{0:T(128)S(1)}, f32[64]{0:T(128)}, u32[]{:S(2)}) copy-start(f32[64]{0:T(128)} %param.20) | copy-start | bytes 772
  0.7 6.1 %copy-start.8 = (f32[64]{0:T(128)S(1)}, f32[64]{0:T(128)}, u32[]{:S(2)}) copy-start(f32[64]{0:T(128)} %param.22) | copy-start | bytes 772
  0.7 6.1 %copy-start.9 = (f32[4]{0:T(128)S(1)}, f32[4]{0:T(128)}, u32[]{:S(2)}) copy-start(f32[4]{0:T(128)} %param.18) | copy-start | bytes 52
  0.7 6.8 %copy-start.1 = (f32[4,128,128]{2,1,0:T(8,128)S(1)}, f32[4,128,128]{2,1,0:T(8,128)}, u32[]{:S(2)}) copy-start(f32[4,128,128]{2,1,0:T(8,128)} %merid.5) | copy-start | bytes 786436
  0.7 6.8 %copy-start.2 = (f32[4,128,128]{2,1,0:T(8,128)S(1)}, f32[4,128,128]{2,1,0:T(8,128)}, u32[]{:S(2)}) copy-start(f32[4,128,128]{2,1,0:T(8,128)} %thick.5) | copy-start | bytes 786436
  0.7 6.8 %copy-start.5 = (f32[128,128]{1,0:T(8,128)S(1)}, f32[128,128]{1,0:T(8,128)}, u32[]{:S(2)}) copy-start(f32[128,128]{1,0:T(8,128)} %visc.5) | copy-start | bytes 196612
  3.0 4.5 %copy-start = (f32[4,128,128]{2,1,0:T(8,128)S(1)}, f32[4,128,128]{2,1,0:T(8,128)}, u32[]{:S(2)}) copy-start(f32[4,128,128]{2,1,0:T(8,128)} %zonal.5) | copy-start | bytes 786436
  3.0 5.8 %collective-permute-start = (bf16[128,128]{1,0:T(8,128)(2,1)}, bf16[128,128]{1,0:T(8,128)(2,1)S(1)}, u32[]{:S(2)}, u32[]{:S(2)}) collective-permute-start(bf16[128,128]{1,0:T(8,128)(2,1)} %get-tuple-element.26), channel_id=1, source_target_pairs={{0,1},{1,0},{2,3},{3,2},{4,5},{5,4},{6,7},{7,6},{8,9},{9,8},{10,11... | collective-permute-start | bytes 98312 | tf_op jit(solution)/shard_map/ppermute | solution.py:674
  3.1 6.3 %collective-permute-start.1 = (bf16[128,128]{1,0:T(8,128)(2,1)}, bf16[128,128]{1,0:T(8,128)(2,1)S(1)}, u32[]{:S(2)}, u32[]{:S(2)}) collective-permute-start(bf16[128,128]{1,0:T(8,128)(2,1)} %get-tuple-element.27), channel_id=1, source_target_pairs={{1,2},{2,1},{3,4},{4,3},{5,6},{6,5},{9,10},{10,9},{11,12},{12,11},... | collective-permute-start | bytes 98312 | tf_op jit(solution)/shard_map/ppermute | solution.py:674
  6.8 0.9 %copy-start.3 = (f32[2,128,128]{2,1,0:T(8,128)S(1)}, f32[2,128,128]{2,1,0:T(8,128)}, u32[]{:S(2)}) copy-start(f32[2,128,128]{2,1,0:T(8,128)} %wind.5) | copy-start | bytes 393220
  6.8 0.9 %copy-start.4 = (s32[128,128]{1,0:T(8,128)S(1)}, s32[128,128]{1,0:T(8,128)}, u32[]{:S(2)}) copy-start(s32[128,128]{1,0:T(8,128)} %land.5) | copy-start | bytes 196612
  9.5 7.3 %collective-permute-start.2 = (bf16[160,128]{1,0:T(8,128)(2,1)S(1)}, bf16[160,128]{1,0:T(8,128)(2,1)S(1)}, u32[]{:S(2)}, u32[]{:S(2)}) collective-permute-start(bf16[160,128]{1,0:T(8,128)(2,1)S(1)} %get-tuple-element.37), channel_id=1, source_target_pairs={{0,8},{8,0},{16,24},{24,16},{1,9},{9,1},{17,25},{25,17},{2,10},{10... | collective-permute-start | bytes 122888 | tf_op jit(solution)/shard_map/ppermute | solution.py:674
  11.2 5.8 %collective-permute-start.3 = (bf16[160,128]{1,0:T(8,128)(2,1)S(1)}, bf16[160,128]{1,0:T(8,128)(2,1)S(1)}, u32[]{:S(2)}, u32[]{:S(2)}) collective-permute-start(bf16[160,128]{1,0:T(8,128)(2,1)S(1)} %get-tuple-element.38), channel_id=1, source_target_pairs={{0,24},{8,16},{16,8},{24,0},{1,25},{9,17},{17,9},{25,1},{2,26},{10... | collective-permute-start | bytes 122888 | tf_op jit(solution)/shard_map/ppermute | solution.py:674

commit v6 on v5

--- a/solution.py
+++ b/solution.py
@@ -695,7 +695,7 @@
     lon_rows = EDGE * FIELDS
     lat_a, lat_b = pl.pallas_call(
         pack_kernel,
-        out_shape=[jax.ShapeDtypeStruct((columns, lat), BF16)] * 2,
+        out_shape=[pltpu.VMEM((columns, lat), BF16)] * 2,
         in_specs=[pl.BlockSpec(memory_space=pltpu.HBM)] * 6,
         out_specs=[VMEM] * 2,
         scratch_shapes=[pltpu.VMEM(a.shape, a.dtype) for a in (zonal, merid, thick, land, visc, wind)]

time: 24 us -> 23.1 us (0.963)
  Pallas kernels: 14 us -> 13.3 us
    pallas_call x1, Pallas kernels: 2.29 us -> 1.67 us  [local(): pl.pallas_call(pack_kernel, out_shape=[pltpu.VMEM((columns, lat), BF16)]...]
  transfers between devices with their start and end apart: 4 -> 4, of which waited for: 2 -> 2; matrix products, arithmetic and copies ran while one was open for 1% -> 1% of each run, Pallas kernels for 20% -> 21%
where the time goes in v6:
time: 23.1 us; the launch traced here: 23 us
  Pallas kernels  13.3 us (58%)
  starting transfers between devices  7.68 us (33%)
  between operations  0.89 us (4%)
  waiting for transfers between devices  0.61 us (3%)
  local copies, waits for them, and re-layouts  0.45 us (2%)
    ppermute x4, starting transfers between devices, swap(): return lax.ppermute(x, axis, pairs)  7.68 us
    pallas_call x1, Pallas kernels, local(): pl.pallas_call(functools.partial(main_kernel, ny), out_shape=[flow] * 3 +...  6.81 us
    pallas_call x1, Pallas kernels, local(): pl.pallas_call(functools.partial(inner_kernel, ny), out_shape=[flow, flow...  3.1 us
    pallas_call x1, Pallas kernels, local(): pl.pallas_call(pack_kernel, out_shape=[pltpu.VMEM((columns, lat), BF16)]...  1.67 us
    pallas_call x1, Pallas kernels, local(): pl.pallas_call(functools.partial(own_kernel, ny), out_shape=[flow] * 3 +...  1.12 us
    ppermute x4, waiting for transfers between devices, swap(): return lax.ppermute(x, axis, pairs)  0.61 us
    pallas_call x1, Pallas kernels, local(): pl.pallas_call(weight_kernel, out_shape=[jax.ShapeDtypeStruct((4, 256, 25...  0.61 us
  transfers between devices with their start and end apart: 4, of which 2 were waited for; matrix products, arithmetic and copies ran while one was open for 1% of the time, Pallas kernels for 21%

profile of v6, /device:TPU:4, one launch (start us, length us, event | category | flops | bytes accessed | tf_op | source)
XLA Modules:
  0.0 23.0 jit_solution(18190029298245073464)
XLA Ops:
  0.6 0.0 copy-start.10
  0.6 0.0 copy-start.11
  0.7 0.0 copy-start.6
  0.7 0.0 copy-start.7
  0.7 0.0 copy-start.8
  0.7 0.0 copy-start.9
  0.7 0.0 copy-start.1
  0.7 0.0 copy-start.2
  0.7 0.0 copy-start.5
  0.7 1.7 %pack.1 = (bf16[128,128]{1,0:T(8,128)(2,1)S(1)}, bf16[128,128]{1,0:T(8,128)(2,1)S(1)}) custom-call(f32[4,128,128]{2,1,0:T(8,128)} %zonal.5, f32[4,128,128]{2,1,0:T(8,128)} %merid.5, f32[4,128,128]{2,1,0:T(8,128)} %thick.5, s32[128,128]{1,0:T(8,128)} %land.5, f32[128,128]{1,0:T(8,128)} %visc.5, f32[2,128,128]{2,1,0:T(8,128)} %wind.5), custom_call_target="tpu_custom_call" | custom-call | tf_op jit(solution)/shard_map/pack/pallas_call | solution.py:696
  2.4 0.0 copy-start
  2.4 0.1 collective-permute-start
  2.5 3.4 %collective-permute-start.1 = (bf16[128,128]{1,0:T(8,128)(2,1)S(1)}, bf16[128,128]{1,0:T(8,128)(2,1)S(1)}, u32[]{:S(2)}, u32[]{:S(2)}) collective-permute-start(bf16[128,128]{1,0:T(8,128)(2,1)S(1)} %get-tuple-element.27), channel_id=1, source_target_pairs={{1,2},{2,1},{3,4},{4,3},{5,6},{6,5},{9,10},{10,9},{11,12},{12,11},... | collective-permute-start | bytes 98312 | tf_op jit(solution)/shard_map/ppermute | solution.py:674
  5.9 0.0 copy-done.10
  5.9 0.2 copy.16.first
  6.1 0.0 copy-done.11
  6.1 0.0 copy-done.6
  6.1 0.0 copy-done.7
  6.2 0.0 copy-done.8
  6.2 0.0 copy-done.9
  6.2 0.0 copy-start.3
  6.2 0.0 copy-start.4
  6.2 0.6 %weights.1 = (bf16[4,256,256]{2,1,0:T(8,128)(2,1)S(1)}, bf16[1024,256]{1,0:T(8,128)(2,1)S(1)}, bf16[2048,128]{1,0:T(8,128)(2,1)S(1)}, f32[8,256]{1,0:T(8,128)S(1...) custom-call(bf16[3,3,64,4]{3,2,1,0:T(8,128)(2,1)S(1)} %copy.16.first, bf16[3,3,64,64]{3,2,1,0:T(8,128)(2,1)S(1)} %copy-done.6, ...), custom_call_target="tpu_custom_call" | custom-call | tf_op jit(solution)/shard_map/weights/pallas_call | solution.py:708
  6.8 0.0 copy-done.1
  6.8 0.0 copy-done.2
  6.8 0.0 copy-done.5
  6.9 0.0 copy-done
  6.9 0.2 copy-done.3
  7.1 0.0 copy-done.4
  7.1 1.1 %own.1 = (f32[4,128,128]{2,1,0:T(8,128)S(1)}, f32[4,128,128]{2,1,0:T(8,128)S(1)}, f32[4,128,128]{2,1,0:T(8,128)S(1)}, f32[128,128]{1,0:T(8,128)S(1)}, f32[128,128]{1,0:T(8,128)S(1)}, /*index=5*/f32[128,128]{1,0:T(8,128)S(1)}) custom-call(f32[4,128,128]{2,1,0:T(8,128)S(1)} %copy-done, f32[4,128,128]{2,1,0:T(8,128)S(1)} %copy-done.1, ...), custom_call_target="tpu_custom_call" | custom-call | flops 20000000 | bytes 4000000 | tf_op jit(solution)/shard_map/own/pallas_call | solution.py:727
  8.2 0.0 collective-permute-done.lat_a.got_a
  8.2 0.4 %collective-permute-done.1.lat_b.got_b = bf16[128,128]{1,0:T(8,128)(2,1)S(1)} collective-permute-done((bf16[128,128]{1,0:T(8,128)(2,1)S(1)}, bf16[128,128]{1,0:T(8,128)(2,1)S(1)}, u32[]{:S(2)}, u32[]{:S(2)}) %collective-permute-start.1) | collective-permute-done | bytes 32800 | tf_op jit(solution)/shard_map/ppermute | solution.py:674
  8.7 1.7 %collective-permute-start.2 = (bf16[160,128]{1,0:T(8,128)(2,1)S(1)}, bf16[160,128]{1,0:T(8,128)(2,1)S(1)}, u32[]{:S(2)}, u32[]{:S(2)}) collective-permute-start(bf16[160,128]{1,0:T(8,128)(2,1)S(1)} %get-tuple-element.37), channel_id=1, source_target_pairs={{0,8},{8,0},{16,24},{24,16},{1,9},{9,1},{17,25},{25,17},{2,10},{10... | collective-permute-start | bytes 122888 | tf_op jit(solution)/shard_map/ppermute | solution.py:674
  10.4 2.5 %collective-permute-start.3 = (bf16[160,128]{1,0:T(8,128)(2,1)S(1)}, bf16[160,128]{1,0:T(8,128)(2,1)S(1)}, u32[]{:S(2)}, u32[]{:S(2)}) collective-permute-start(bf16[160,128]{1,0:T(8,128)(2,1)S(1)} %get-tuple-element.38), channel_id=1, source_target_pairs={{0,24},{8,16},{16,8},{24,0},{1,25},{9,17},{17,9},{25,1},{2,26},{10... | collective-permute-start | bytes 122888 | tf_op jit(solution)/shard_map/ppermute | solution.py:674
  12.8 3.1 %inner.1 = (f32[4,128,128]{2,1,0:T(8,128)S(1)}, f32[4,128,128]{2,1,0:T(8,128)S(1)}, f32[4,128,128]{2,1,0:T(8,128)S(1)}, bf16[17,80,256]{2,1,0:T(8,128)(2,1)S(1)}, f32[16,48,256]{2,1,0:T(8,128)S(1)}) custom-call(f32[4,128,128]{2,1,0:T(8,128)S(1)} %copy-done, f32[4,128,128]{2,1,0:T(8,128)S(1)} %copy-done.1, f32[4,128,128]{2,1,0:T(8,128)S(1)} %copy-done.2, ...), custom_call_target="tpu_custom_call" | custom-call | flops 40000000 | bytes 8000000 | tf_op jit(solution)/shard_map/inner/pallas_call | solution.py:759
  15.9 0.0 collective-permute-done.2.lon_a
  15.9 0.2 collective-permute-done.3.lon_b
  16.2 6.8 %step.1 = (f32[4,128,128]{2,1,0:T(8,128)}, f32[4,128,128]{2,1,0:T(8,128)}, f32[4,128,128]{2,1,0:T(8,128)}, f32[128,128]{1,0:T(8,128)}) custom-call(f32[4,128,128]{2,1,0:T(8,128)S(1)} %get-tuple-element.34.zonal_in, f32[4,128,128]{2,1,0:T(8,128)S(1)} %get-tuple-element.35.merid_in, f32[4,128,128]{2,1,0:T(8,128)S(1)} %get-tuple-element.36.thick_in, ...), custom_call_target="tpu_custom_call" | custom-call | tf_op jit(solution)/shard_map/step/pallas_call | solution.py:781
  (2 shorter events, 0.0 us)
Async XLA Ops:
  0.6 5.3 %copy-start.10 = (bf16[3,3,64,4]{2,3,1,0:T(4,128)(2,1)S(1)}, bf16[3,3,64,4]{2,3,1,0:T(4,128)(2,1)}, u32[]{:S(2)}) copy-start(bf16[3,3,64,4]{2,3,1,0:T(4,128)(2,1)} %param.19) | copy-start | bytes 13828
  0.6 5.5 %copy-start.11 = (bf16[3,3,1,64]{3,1,2,0:T(4,128)(2,1)S(1)}, bf16[3,3,1,64]{3,1,2,0:T(4,128)(2,1)}, u32[]{:S(2)}) copy-start(bf16[3,3,1,64]{3,1,2,0:T(4,128)(2,1)} %param.23) | copy-start | bytes 3460
  0.7 5.5 %copy-start.6 = (bf16[3,3,64,64]{3,2,1,0:T(8,128)(2,1)S(1)}, bf16[3,3,64,64]{3,2,1,0:T(8,128)(2,1)}, u32[]{:S(2)}) copy-start(bf16[3,3,64,64]{3,2,1,0:T(8,128)(2,1)} %second.1) | copy-start | bytes 221188
  0.7 5.5 %copy-start.7 = (f32[64]{0:T(128)S(1)}, f32[64]{0:T(128)}, u32[]{:S(2)}) copy-start(f32[64]{0:T(128)} %param.20) | copy-start | bytes 772
  0.7 5.5 %copy-start.8 = (f32[64]{0:T(128)S(1)}, f32[64]{0:T(128)}, u32[]{:S(2)}) copy-start(f32[64]{0:T(128)} %param.22) | copy-start | bytes 772
  0.7 5.5 %copy-start.9 = (f32[4]{0:T(128)S(1)}, f32[4]{0:T(128)}, u32[]{:S(2)}) copy-start(f32[4]{0:T(128)} %param.18) | copy-start | bytes 52
  0.7 6.1 %copy-start.1 = (f32[4,128,128]{2,1,0:T(8,128)S(1)}, f32[4,128,128]{2,1,0:T(8,128)}, u32[]{:S(2)}) copy-start(f32[4,128,128]{2,1,0:T(8,128)} %merid.5) | copy-start | bytes 786436
  0.7 6.1 %copy-start.2 = (f32[4,128,128]{2,1,0:T(8,128)S(1)}, f32[4,128,128]{2,1,0:T(8,128)}, u32[]{:S(2)}) copy-start(f32[4,128,128]{2,1,0:T(8,128)} %thick.5) | copy-start | bytes 786436
  0.7 6.1 %copy-start.5 = (f32[128,128]{1,0:T(8,128)S(1)}, f32[128,128]{1,0:T(8,128)}, u32[]{:S(2)}) copy-start(f32[128,128]{1,0:T(8,128)} %visc.5) | copy-start | bytes 196612
  2.4 4.5 %copy-start = (f32[4,128,128]{2,1,0:T(8,128)S(1)}, f32[4,128,128]{2,1,0:T(8,128)}, u32[]{:S(2)}) copy-start(f32[4,128,128]{2,1,0:T(8,128)} %zonal.5) | copy-start | bytes 786436
  2.4 5.8 %collective-permute-start = (bf16[128,128]{1,0:T(8,128)(2,1)S(1)}, bf16[128,128]{1,0:T(8,128)(2,1)S(1)}, u32[]{:S(2)}, u32[]{:S(2)}) collective-permute-start(bf16[128,128]{1,0:T(8,128)(2,1)S(1)} %get-tuple-element.26), channel_id=1, source_target_pairs={{0,1},{1,0},{2,3},{3,2},{4,5},{5,4},{6,7},{7,6},{8,9},{9,8},{10,11... | collective-permute-start | bytes 98312 | tf_op jit(solution)/shard_map/ppermute | solution.py:674
  2.5 6.1 %collective-permute-start.1 = (bf16[128,128]{1,0:T(8,128)(2,1)S(1)}, bf16[128,128]{1,0:T(8,128)(2,1)S(1)}, u32[]{:S(2)}, u32[]{:S(2)}) collective-permute-start(bf16[128,128]{1,0:T(8,128)(2,1)S(1)} %get-tuple-element.27), channel_id=1, source_target_pairs={{1,2},{2,1},{3,4},{4,3},{5,6},{6,5},{9,10},{10,9},{11,12},{12,11},... | collective-permute-start | bytes 98312 | tf_op jit(solution)/shard_map/ppermute | solution.py:674
  6.2 0.9 %copy-start.3 = (f32[2,128,128]{2,1,0:T(8,128)S(1)}, f32[2,128,128]{2,1,0:T(8,128)}, u32[]{:S(2)}) copy-start(f32[2,128,128]{2,1,0:T(8,128)} %wind.5) | copy-start | bytes 393220
  6.2 0.9 %copy-start.4 = (s32[128,128]{1,0:T(8,128)S(1)}, s32[128,128]{1,0:T(8,128)}, u32[]{:S(2)}) copy-start(s32[128,128]{1,0:T(8,128)} %land.5) | copy-start | bytes 196612
  8.7 7.3 %collective-permute-start.2 = (bf16[160,128]{1,0:T(8,128)(2,1)S(1)}, bf16[160,128]{1,0:T(8,128)(2,1)S(1)}, u32[]{:S(2)}, u32[]{:S(2)}) collective-permute-start(bf16[160,128]{1,0:T(8,128)(2,1)S(1)} %get-tuple-element.37), channel_id=1, source_target_pairs={{0,8},{8,0},{16,24},{24,16},{1,9},{9,1},{17,25},{25,17},{2,10},{10... | collective-permute-start | bytes 122888 | tf_op jit(solution)/shard_map/ppermute | solution.py:674
  10.4 5.8 %collective-permute-start.3 = (bf16[160,128]{1,0:T(8,128)(2,1)S(1)}, bf16[160,128]{1,0:T(8,128)(2,1)S(1)}, u32[]{:S(2)}, u32[]{:S(2)}) collective-permute-start(bf16[160,128]{1,0:T(8,128)(2,1)S(1)} %get-tuple-element.38), channel_id=1, source_target_pairs={{0,24},{8,16},{16,8},{24,0},{1,25},{9,17},{17,9},{25,1},{2,26},{10... | collective-permute-start | bytes 122888 | tf_op jit(solution)/shard_map/ppermute | solution.py:674
